TPU v7x, 32 devices: a whole 2x2x4 slice. The times are simulated.
32 devices in a mesh: dp: 8 (over z, x), tensor: 4 (over y, core).
Axes of the slice: x: 2, y: 2, z: 4, core: 2. Of those that a mesh axis runs over, the one named last changes fastest.
Arguments:
- activations: bfloat16 [8192, 2048], P(('dp', 'tensor')), may hold values from -6 to 6
- cotangent: bfloat16 [8192, 2048], P(('dp', 'tensor')), may hold values from -6 to 6
- segments: int32 [8192], P('dp'), may hold values from 0 to 2, as said below
- norm_one_gain: bfloat16 [2048], P(('dp', 'tensor')), may hold values from 0.099609375 to 1.8984375
- norm_one_bias: bfloat16 [2048], P(('dp', 'tensor')), may hold values from -3 to 3
- w_query: bfloat16 [2048, 2048], P('dp', 'tensor'), may hold values from -0.1875 to 0.1875
- w_key: bfloat16 [2048, 2048], P('dp', 'tensor'), may hold values from -0.1875 to 0.1875
- w_value: bfloat16 [2048, 2048], P('dp', 'tensor'), may hold values from -0.125 to 0.125
- qkv_bias: bfloat16 [3, 32, 64], P(None, 'tensor', 'dp'), may hold values from -3 to 3
- w_out: bfloat16 [2048, 2048], P('tensor', 'dp'), may hold values from -0.75 to 0.75
- norm_two_gain: bfloat16 [2048], P(('dp', 'tensor')), may hold values from 0.099609375 to 1.8984375
- norm_two_bias: bfloat16 [2048], P(('dp', 'tensor')), may hold values from -3 to 3
- w_gate: bfloat16 [2048, 5632], P('dp', 'tensor'), may hold values from -0.125 to 0.125
- w_up: bfloat16 [2048, 5632], P('dp', 'tensor'), may hold values from -0.125 to 0.125
- w_down: bfloat16 [5632, 2048], P('tensor', 'dp'), may hold values from -0.109375 to 0.109375
Outputs:
- result: bfloat16 [8192, 2048], P(('dp', 'tensor'))
- input_grad: bfloat16 [8192, 2048], P(('dp', 'tensor'))
- grad_norm_one_gain: float32 [2048], P(('dp', 'tensor'))
- grad_norm_one_bias: float32 [2048], P(('dp', 'tensor'))
- grad_w_query: float32 [2048, 2048], P('dp', 'tensor')
- grad_w_key: float32 [2048, 2048], P('dp', 'tensor')
- grad_w_value: float32 [2048, 2048], P('dp', 'tensor')
- grad_qkv_bias: float32 [3, 32, 64], P(None, 'tensor', 'dp')
- grad_w_out: float32 [2048, 2048], P('tensor', 'dp')
- grad_norm_two_gain: float32 [2048], P(('dp', 'tensor'))
- grad_norm_two_bias: float32 [2048], P(('dp', 'tensor'))
- grad_w_gate: float32 [2048, 5632], P('dp', 'tensor')
- grad_w_up: float32 [2048, 5632], P('dp', 'tensor')
- grad_w_down: float32 [5632, 2048], P('tensor', 'dp')
Inputs may be any that keep to these rules, and one draw needn't show every extreme that they name: `segments`: within each sequence the segment numbers never fall, start at 0 and end at 2; each tells the document of its token.
All inputs are finite; a program needn't handle non-finite values.
Results may differ from a plain program's by a relative error of at most 0.023.
Values may be sent and summed in bfloat16 or wider, within the bound.
No kernel may reach another device: no remote copies, remote signals or barrier semaphores. Data moves between devices by JAX's collectives and lax.ppermute only.
A program may use at most 192 MiB of HBM per device.

v0:
```python
import jax
import jax.numpy as jnp
from jax import lax
from jax.sharding import PartitionSpec as P

HD = 64
ROT = 16


EPSILON = 1e-05
NEGATIVE = -1e30


def rotary_tables(segment_ids):
    length = segment_ids.shape[0]
    places = jnp.arange(length, dtype=jnp.int32)
    starts = jnp.concatenate([jnp.ones((1,), dtype=jnp.bool_), segment_ids[1:] != segment_ids[:-1]])
    begins = lax.cummax(jnp.where(starts, places, 0), axis=0)
    within = (places - begins).astype(jnp.float32)
    frequency = 10000.0 ** (-2.0 * jnp.arange(ROT // 2, dtype=jnp.float32) / ROT)
    angles = within[:, None] * frequency[None, :]
    return (jnp.cos(angles), jnp.sin(angles))


def rotate(heads, cos_table, sin_table):
    halves = ROT // 2
    first_half = heads[..., :halves]
    second_half = heads[..., halves:ROT]
    cos_part = cos_table[:, None, :]
    sin_part = sin_table[:, None, :]
    return jnp.concatenate(
        [
            first_half * cos_part - second_half * sin_part,
            second_half * cos_part + first_half * sin_part,
            heads[..., ROT:],
        ],
        axis=-1,
    )


def norm_forward(inputs, gain_vec, shift_vec):
    average = jnp.mean(inputs, axis=-1, keepdims=True)
    centred = inputs - average
    variance = jnp.mean(centred * centred, axis=-1, keepdims=True)
    inverse = lax.rsqrt(variance + EPSILON)
    standard = centred * inverse
    return (standard, inverse, standard * gain_vec + shift_vec)


def norm_backward(upstream, standard, inverse, gain_vec):
    gain_grad = jnp.sum(upstream * standard, axis=0)
    shift_grad = jnp.sum(upstream, axis=0)
    scaled = upstream * gain_vec
    inner = (
        scaled
        - jnp.mean(scaled, axis=-1, keepdims=True)
        - standard * jnp.mean(scaled * standard, axis=-1, keepdims=True)
    )
    return (inverse * inner, gain_grad, shift_grad)


def split_blocks(values, block_rows):
    return values.reshape((values.shape[0] // block_rows, block_rows) + values.shape[1:])


def block_mask(segment_block, offset, segment_ids, key_places):
    row_places = offset + jnp.arange(segment_block.shape[0], dtype=jnp.int32)
    return (segment_block[:, None] == segment_ids[None, :]) & (
        row_places[:, None] >= key_places[None, :]
    )


def attend_forward(query_heads, key_heads, value_heads, segment_ids):
    length = query_heads.shape[0]
    block_rows = min(512, length)
    scaling = HD ** (-0.5)
    key_places = jnp.arange(length, dtype=jnp.int32)

    def one_block(carried, inputs_block):
        query_block, segment_block, offset = inputs_block
        allowed = block_mask(segment_block, offset, segment_ids, key_places)
        scores = (
            jnp.einsum("qhd,khd->hqk", query_block, key_heads, preferred_element_type=jnp.float32)
            * scaling
        )
        scores = jnp.where(allowed[None], scores, NEGATIVE)
        row_max = jnp.max(scores, axis=-1, keepdims=True)
        exponent = jnp.exp(scores - row_max)
        totals = jnp.sum(exponent, axis=-1, keepdims=True)
        weights = (exponent / totals).astype(jnp.bfloat16)
        attended = jnp.einsum(
            "hqk,khd->qhd", weights, value_heads, preferred_element_type=jnp.float32
        )
        return (carried, (attended, row_max[..., 0] + jnp.log(totals[..., 0])))

    offsets = jnp.arange(length // block_rows, dtype=jnp.int32) * block_rows
    _, (attended, log_totals) = lax.scan(
        one_block,
        0,
        (split_blocks(query_heads, block_rows), split_blocks(segment_ids, block_rows), offsets),
    )
    return (attended.reshape(length, -1), log_totals)


def attend_backward(query_heads, key_heads, value_heads, segment_ids, log_totals, mixed_grad):
    length = query_heads.shape[0]
    block_rows = min(512, length)
    scaling = HD ** (-0.5)
    key_places = jnp.arange(length, dtype=jnp.int32)

    def one_block(carried, inputs_block):
        key_grad, value_grad = carried
        query_block, segment_block, offset, log_block, grad_block = inputs_block
        allowed = block_mask(segment_block, offset, segment_ids, key_places)
        scores = (
            jnp.einsum("qhd,khd->hqk", query_block, key_heads, preferred_element_type=jnp.float32)
            * scaling
        )
        scores = jnp.where(allowed[None], scores, NEGATIVE)
        weights = jnp.exp(scores - log_block[..., None])
        weight_grad = jnp.einsum(
            "qhd,khd->hqk", grad_block, value_heads, preferred_element_type=jnp.float32
        )
        centre_term = jnp.sum(weight_grad * weights, axis=-1, keepdims=True)
        score_grad = (weights * (weight_grad - centre_term)).astype(jnp.bfloat16)
        query_grad = (
            jnp.einsum("hqk,khd->qhd", score_grad, key_heads, preferred_element_type=jnp.float32)
            * scaling
        )
        key_grad = (
            key_grad
            + jnp.einsum(
                "hqk,qhd->khd", score_grad, query_block, preferred_element_type=jnp.float32
            )
            * scaling
        )
        value_grad = value_grad + jnp.einsum(
            "hqk,qhd->khd",
            weights.astype(jnp.bfloat16),
            grad_block,
            preferred_element_type=jnp.float32,
        )
        return ((key_grad, value_grad), query_grad)

    offsets = jnp.arange(length // block_rows, dtype=jnp.int32) * block_rows
    zero_grad = jnp.zeros(key_heads.shape, jnp.float32)
    (key_grad, value_grad), query_grad = lax.scan(
        one_block,
        (zero_grad, zero_grad),
        (
            split_blocks(query_heads, block_rows),
            split_blocks(segment_ids, block_rows),
            offsets,
            log_totals,
            split_blocks(mixed_grad, block_rows),
        ),
    )
    return (query_grad.reshape(key_heads.shape), key_grad, value_grad)


def on_device(
    activations,
    cotangent,
    segments,
    norm_one_gain,
    norm_one_bias,
    w_query,
    w_key,
    w_value,
    qkv_bias,
    w_out,
    norm_two_gain,
    norm_two_bias,
    w_gate,
    w_up,
    w_down,
):
    norm_values = (
        lax.all_gather(norm_one_gain, ("dp", "tensor"), axis=0, tiled=True),
        lax.all_gather(norm_one_bias, ("dp", "tensor"), axis=0, tiled=True),
        lax.all_gather(norm_two_gain, ("dp", "tensor"), axis=0, tiled=True),
        lax.all_gather(norm_two_bias, ("dp", "tensor"), axis=0, tiled=True),
    )
    gain_one = norm_values[0].astype(jnp.float32)
    shift_one = norm_values[1].astype(jnp.float32)
    gain_two = norm_values[2].astype(jnp.float32)
    shift_two = norm_values[3].astype(jnp.float32)
    gathered = (
        lax.all_gather(w_query, "dp", axis=0, tiled=True),
        lax.all_gather(w_key, "dp", axis=0, tiled=True),
        lax.all_gather(w_value, "dp", axis=0, tiled=True),
        lax.all_gather(qkv_bias, "dp", axis=2, tiled=True),
        lax.all_gather(w_out, "dp", axis=1, tiled=True),
        lax.all_gather(w_gate, "dp", axis=0, tiled=True),
        lax.all_gather(w_up, "dp", axis=0, tiled=True),
        lax.all_gather(w_down, "dp", axis=1, tiled=True),
    )
    full_query, full_key, full_value, full_bias, full_out, full_gate, full_up, full_down = gathered
    length = segments.shape[0]
    local_heads = full_query.shape[1] // HD
    bias_rows = full_bias.astype(jnp.float32).reshape(3, local_heads * HD)
    cos_table, sin_table = rotary_tables(segments)
    own_inputs = activations.astype(jnp.float32)
    standard_one, inverse_one, normed_own = norm_forward(own_inputs, gain_one, shift_one)
    normed = lax.all_gather(normed_own.astype(jnp.bfloat16), "tensor", axis=0, tiled=True)
    query_pre = jnp.dot(normed, full_query, preferred_element_type=jnp.float32) + bias_rows[0]
    key_pre = jnp.dot(normed, full_key, preferred_element_type=jnp.float32) + bias_rows[1]
    value_pre = jnp.dot(normed, full_value, preferred_element_type=jnp.float32) + bias_rows[2]
    query_heads = rotate(query_pre.reshape(length, local_heads, HD), cos_table, sin_table).astype(
        jnp.bfloat16
    )
    key_heads = rotate(key_pre.reshape(length, local_heads, HD), cos_table, sin_table).astype(
        jnp.bfloat16
    )
    value_heads = value_pre.astype(jnp.bfloat16).reshape(length, local_heads, HD)
    attended, log_totals = attend_forward(query_heads, key_heads, value_heads, segments)
    mixed_heads = attended.astype(jnp.bfloat16)
    middle = own_inputs + lax.psum_scatter(
        jnp.dot(mixed_heads, full_out, preferred_element_type=jnp.float32).astype(jnp.bfloat16),
        "tensor",
        scatter_dimension=0,
        tiled=True,
    ).astype(jnp.float32)
    standard_two, inverse_two, normed_two_own = norm_forward(middle, gain_two, shift_two)
    normed_two = lax.all_gather(normed_two_own.astype(jnp.bfloat16), "tensor", axis=0, tiled=True)
    gate_values = jnp.dot(normed_two, full_gate, preferred_element_type=jnp.float32)
    up_values = jnp.dot(normed_two, full_up, preferred_element_type=jnp.float32)
    sigmoid_gate = jax.nn.sigmoid(gate_values)
    silu_gate = gate_values * sigmoid_gate
    hidden = (silu_gate * up_values).astype(jnp.bfloat16)
    result = (
        middle
        + lax.psum_scatter(
            jnp.dot(hidden, full_down, preferred_element_type=jnp.float32).astype(jnp.bfloat16),
            "tensor",
            scatter_dimension=0,
            tiled=True,
        ).astype(jnp.float32)
    ).astype(jnp.bfloat16)
    again = (
        lax.all_gather(w_query, "dp", axis=0, tiled=True),
        lax.all_gather(w_key, "dp", axis=0, tiled=True),
        lax.all_gather(w_value, "dp", axis=0, tiled=True),
        lax.all_gather(qkv_bias, "dp", axis=2, tiled=True),
        lax.all_gather(w_out, "dp", axis=1, tiled=True),
        lax.all_gather(w_gate, "dp", axis=0, tiled=True),
        lax.all_gather(w_up, "dp", axis=0, tiled=True),
        lax.all_gather(w_down, "dp", axis=1, tiled=True),
    )
    full_query, full_key, full_value, full_bias, full_out, full_gate, full_up, full_down = again
    grad_full = lax.all_gather(cotangent, "tensor", axis=0, tiled=True)
    down_weight_grad = jnp.einsum(
        "sf,sd->fd", hidden, grad_full, preferred_element_type=jnp.float32
    )
    hidden_grad = jnp.einsum("sd,fd->sf", grad_full, full_down, preferred_element_type=jnp.float32)
    gate_grad = (
        hidden_grad * up_values * (sigmoid_gate + silu_gate * (1.0 - sigmoid_gate))
    ).astype(jnp.bfloat16)
    up_grad = (hidden_grad * silu_gate).astype(jnp.bfloat16)
    gate_weight_grad = jnp.einsum(
        "sd,sf->df", normed_two, gate_grad, preferred_element_type=jnp.float32
    )
    up_weight_grad = jnp.einsum(
        "sd,sf->df", normed_two, up_grad, preferred_element_type=jnp.float32
    )
    normed_two_grad = lax.psum_scatter(
        (
            jnp.einsum("sf,df->sd", gate_grad, full_gate, preferred_element_type=jnp.float32)
            + jnp.einsum("sf,df->sd", up_grad, full_up, preferred_element_type=jnp.float32)
        ).astype(jnp.bfloat16),
        "tensor",
        scatter_dimension=0,
        tiled=True,
    ).astype(jnp.float32)
    middle_part, gain_two_grad, shift_two_grad = norm_backward(
        normed_two_grad, standard_two, inverse_two, gain_two
    )
    middle_grad = cotangent.astype(jnp.float32) + middle_part
    branch_grad = lax.all_gather(middle_grad.astype(jnp.bfloat16), "tensor", axis=0, tiled=True)
    out_weight_grad = jnp.einsum(
        "sc,sd->cd", mixed_heads, branch_grad, preferred_element_type=jnp.float32
    )
    mixed_grad = (
        jnp.einsum("sd,cd->sc", branch_grad, full_out, preferred_element_type=jnp.float32)
        .astype(jnp.bfloat16)
        .reshape(length, local_heads, HD)
    )
    rot_query_grad, rot_key_grad, value_heads_grad = attend_backward(
        query_heads, key_heads, value_heads, segments, log_totals, mixed_grad
    )
    query_grad = (
        rotate(rot_query_grad, cos_table, -sin_table).astype(jnp.bfloat16).reshape(length, -1)
    )
    key_grad = rotate(rot_key_grad, cos_table, -sin_table).astype(jnp.bfloat16).reshape(length, -1)
    value_grad = value_heads_grad.astype(jnp.bfloat16).reshape(length, -1)
    bias_grad = jnp.stack(
        [
            jnp.sum(query_grad.astype(jnp.float32), axis=0),
            jnp.sum(key_grad.astype(jnp.float32), axis=0),
            jnp.sum(value_grad.astype(jnp.float32), axis=0),
        ]
    ).reshape(3, local_heads, HD)
    query_weight_grad = jnp.einsum(
        "sd,sc->dc", normed, query_grad, preferred_element_type=jnp.float32
    )
    key_weight_grad = jnp.einsum("sd,sc->dc", normed, key_grad, preferred_element_type=jnp.float32)
    value_weight_grad = jnp.einsum(
        "sd,sc->dc", normed, value_grad, preferred_element_type=jnp.float32
    )
    total_rows = jnp.einsum("sc,dc->sd", query_grad, full_query, preferred_element_type=jnp.float32)
    total_rows = total_rows + jnp.einsum(
        "sc,dc->sd", key_grad, full_key, preferred_element_type=jnp.float32
    )
    normed_grad = lax.psum_scatter(
        (
            total_rows
            + jnp.einsum("sc,dc->sd", value_grad, full_value, preferred_element_type=jnp.float32)
        ).astype(jnp.bfloat16),
        "tensor",
        scatter_dimension=0,
        tiled=True,
    ).astype(jnp.float32)
    input_part, gain_one_grad, shift_one_grad = norm_backward(
        normed_grad, standard_one, inverse_one, gain_one
    )
    input_grad = (middle_grad + input_part).astype(jnp.bfloat16)
    weight_sums = (
        lax.psum_scatter(
            query_weight_grad.astype(jnp.bfloat16), "dp", scatter_dimension=0, tiled=True
        ).astype(jnp.float32),
        lax.psum_scatter(
            key_weight_grad.astype(jnp.bfloat16), "dp", scatter_dimension=0, tiled=True
        ).astype(jnp.float32),
        lax.psum_scatter(
            value_weight_grad.astype(jnp.bfloat16), "dp", scatter_dimension=0, tiled=True
        ).astype(jnp.float32),
        lax.psum_scatter(
            bias_grad.astype(jnp.bfloat16), "dp", scatter_dimension=2, tiled=True
        ).astype(jnp.float32),
        lax.psum_scatter(
            out_weight_grad.astype(jnp.bfloat16), "dp", scatter_dimension=1, tiled=True
        ).astype(jnp.float32),
        lax.psum_scatter(
            gate_weight_grad.astype(jnp.bfloat16), "dp", scatter_dimension=0, tiled=True
        ).astype(jnp.float32),
        lax.psum_scatter(
            up_weight_grad.astype(jnp.bfloat16), "dp", scatter_dimension=0, tiled=True
        ).astype(jnp.float32),
        lax.psum_scatter(
            down_weight_grad.astype(jnp.bfloat16), "dp", scatter_dimension=1, tiled=True
        ).astype(jnp.float32),
    )
    norm_sums = (
        lax.psum_scatter(gain_one_grad, ("dp", "tensor"), scatter_dimension=0, tiled=True),
        lax.psum_scatter(shift_one_grad, ("dp", "tensor"), scatter_dimension=0, tiled=True),
        lax.psum_scatter(gain_two_grad, ("dp", "tensor"), scatter_dimension=0, tiled=True),
        lax.psum_scatter(shift_two_grad, ("dp", "tensor"), scatter_dimension=0, tiled=True),
    )
    return (
        result,
        input_grad,
        norm_sums[0],
        norm_sums[1],
        weight_sums[0],
        weight_sums[1],
        weight_sums[2],
        weight_sums[3],
        weight_sums[4],
        norm_sums[2],
        norm_sums[3],
        weight_sums[5],
        weight_sums[6],
        weight_sums[7],
    )


def solution(mesh):
    placed = (
        P(("dp", "tensor"), None),
        P(("dp", "tensor"), None),
        P("dp"),
        P(("dp", "tensor")),
        P(("dp", "tensor")),
        P("dp", "tensor"),
        P("dp", "tensor"),
        P("dp", "tensor"),
        P(None, "tensor", "dp"),
        P("tensor", "dp"),
        P(("dp", "tensor")),
        P(("dp", "tensor")),
        P("dp", "tensor"),
        P("dp", "tensor"),
        P("tensor", "dp"),
    )
    return jax.shard_map(
        on_device,
        mesh=mesh,
        in_specs=placed,
        out_specs=(
            P(("dp", "tensor"), None),
            P(("dp", "tensor"), None),
            P(("dp", "tensor")),
            P(("dp", "tensor")),
            P("dp", "tensor"),
            P("dp", "tensor"),
            P("dp", "tensor"),
            P(None, "tensor", "dp"),
            P("tensor", "dp"),
            P(("dp", "tensor")),
            P(("dp", "tensor")),
            P("dp", "tensor"),
            P("dp", "tensor"),
            P("tensor", "dp"),
        ),
        check_vma=False,
    )
```

profile of v0, /device:TPU:0, one launch (start us, length us, event | category | flops | bytes accessed | tf_op | source)
XLA Modules:
  0.0 1503.7 jit_solution(1783604090195298278)
XLA Ops:
  11.4 43.1 %all-reduce.10 = (bf16[2048]{0:T(1024)(128)(2,1)}, bf16[2048]{0:T(1024)(128)(2,1)}, bf16[2048]{0:T(1024)(128)(2,1)S(1)}, bf16[2048]{0:T(1024)(128)(2,1)S(1)}) all-reduce(bf16[2048]{0:T(1024)(128)(2,1)S(1)} %dynamic-update-slice.3, bf16[2048]{0:T(1024)(128)(2,1)S(1)} %dynamic-update-slice.2, ...), channel_id=1, replica_groups=mesh['dp'=8,'tensor'=4] {'dp','tensor'}, use_global_device_ids=true, to_apply=%add.3 | all-reduce | flops 8192 | bytes 32768
  60.8 30.5 %all_gather.59 = bf16[3,8,64]{1,0,2:T(4,128)(2,1)S(1)} all-gather(bf16[3,8,8]{1,0,2:T(4,128)(2,1)S(1)} %copy.48), channel_id=1, replica_groups=mesh['dp'=8,'tensor'=4] {'dp'}, dimensions={2}, use_global_device_ids=true | all-gather | bytes 3456 | tf_op jit(solution)/shard_map/all_gather | solution.py:192
  105.2 44.7 %all-gather.14.cloned.1.call-done = bf16[2048,512]{1,0:T(8,128)(2,1)} async-done(((bf16[256,512]{1,0:T(8,128)(2,1)}), bf16[2048,512]{1,0:T(8,128)(2,1)}) %all-gather.14.cloned.1.call-update) | async-done | bytes 2097168 | tf_op jit(solution)/shard_map/all_gather | solution.py:189
  156.7 43.0 %all-gather.18.cloned.1.call-done = bf16[2048,512]{1,0:T(8,128)(2,1)} async-done(((bf16[256,512]{1,0:T(8,128)(2,1)}), bf16[2048,512]{1,0:T(8,128)(2,1)}) %all-gather.18.cloned.1.call-update) | async-done | bytes 2097168 | tf_op jit(solution)/shard_map/all_gather | solution.py:191
  205.0 31.3 %while.28 = (s32[]{:T(128)}, bf16[2,512,8,64]{1,3,2,0:T(8,128)(2,1)}, f32[2,8,512]{2,1,0:T(8,128)S(1)}, s32[2,512]{1,0:T(2,128)S(1)}, s32[1024]{0:T(1024)S(1)}, ...) while((s32[]{:T(128)}, ...), condition=%wide.region_7.8_spmd.clone, body=%wide.region_4.7_spmd.clone.sunk | while | flops 1125642752 | bytes 64633028 | solution.py:97
  240.6 10.7 all-gather.20.cloned.1.call-done
  258.4 42.0 %reduce-scatter.13.cloned.1.call-done = bf16[256,2048]{1,0:T(8,128)(2,1)} async-done(((bf16[1024,2048]{1,0:T(8,128)(2,1)}), bf16[256,2048]{1,0:T(8,128)(2,1)}) %reduce-scatter.13.cloned.1.call-update) | async-done | bytes 1048592 | tf_op jit(solution)/shard_map/reduce_scatter | solution.py:218
  306.2 89.2 %all-gather.26.cloned.1.call-done = bf16[2048,1408]{1,0:T(8,128)(2,1)} async-done(((bf16[256,1408]{1,0:T(8,128)(2,1)}), bf16[2048,1408]{1,0:T(8,128)(2,1)}) %all-gather.26.cloned.1.call-update) | async-done | bytes 5767184 | tf_op jit(solution)/shard_map/all_gather | solution.py:195
  395.5 34.9 %all-gather.22.cloned.1.call-done = bf16[1024,2048]{1,0:T(8,128)(2,1)} async-done(((bf16[256,2048]{1,0:T(8,128)(2,1)}), bf16[1024,2048]{1,0:T(8,128)(2,1)}) %all-gather.22.cloned.1.call-update) | async-done | bytes 4194320 | tf_op jit(solution)/shard_map/all_gather | solution.py:225
  430.4 11.9 fusion.69
  442.2 83.2 %all-gather.24.cloned.1.call-done = bf16[2048,1408]{1,0:T(8,128)(2,1)} async-done(((bf16[256,1408]{1,0:T(8,128)(2,1)}), bf16[2048,1408]{1,0:T(8,128)(2,1)}) %all-gather.24.cloned.1.call-update) | async-done | bytes 5767184 | tf_op jit(solution)/shard_map/all_gather | solution.py:194
  525.5 11.7 fusion.68
  537.1 22.5 %all-gather.30.cloned.1.call-done = bf16[1024,2048]{1,0:T(8,128)(2,1)} async-done(((bf16[256,2048]{1,0:T(8,128)(2,1)}), bf16[1024,2048]{1,0:T(8,128)(2,1)}) %all-gather.30.cloned.1.call-update) | async-done | bytes 4194320 | tf_op jit(solution)/shard_map/all_gather | solution.py:251
  559.7 95.9 %all-gather.28.cloned.1.call-done = bf16[1408,2048]{1,0:T(8,128)(2,1)} async-done(((bf16[1408,256]{1,0:T(8,128)(2,1)}), bf16[1408,2048]{1,0:T(8,128)(2,1)}) %all-gather.28.cloned.1.call-update) | async-done | bytes 5767184 | tf_op jit(solution)/shard_map/all_gather | solution.py:196
  655.5 16.4 %multiply_convert_fusion.1 = (bf16[1024,1408]{1,0:T(8,128)(2,1)}, bf16[1024,1408]{1,0:T(8,128)(2,1)}, bf16[1024,1408]{1,0:T(8,128)(2,1)}) fusion(f32[1024,1408]{1,0:T(8,128)} %fusion.68, f32[1024,1408]{1,0:T(8,128)} %fusion.69, bf16[1024,2048]{1,0:T(8,128)(2,1)} %all-gather.30.cloned.1.call-done, bf16[1408,2048]{1,0:T(8,128)(2,1)} %all-gather.28.cloned.1.call-done), kind=kOutput, calls=%fused_computation.53 | convolution fusion | flops 5925765120 | bytes 30146560 | tf_op jit(solution)/shard_map/sd,fd->sf/dot_general | solution.py:255
  680.6 11.4 add_convert_fusion.1
  692.1 42.8 %reduce-scatter.17.cloned.1.call-done = bf16[256,2048]{1,0:T(8,128)(2,1)} async-done(((bf16[1024,2048]{1,0:T(8,128)(2,1)}), bf16[256,2048]{1,0:T(8,128)(2,1)}) %reduce-scatter.17.cloned.1.call-update) | async-done | bytes 1048592 | tf_op jit(solution)/shard_map/reduce_scatter | solution.py:266
  750.9 11.0 convolution_convert_fusion.1
  761.9 11.2 convolution_convert_fusion.2
  791.8 126.1 %while.29 = (s32[]{:T(128)}, f32[1024,8,64]{0,2,1:T(8,128)}, f32[1024,8,64]{0,2,1:T(8,128)}, f32[2,512,8,64]{1,0,3,2:T(2,128)}, bf16[2,512,8,64]{1,3,2,0:T(8,128...) while((s32[]{:T(128)}, f32[1024,8,64]{0,2,1:T(8,128)}, ...), condition=%wide.region_17.18_spmd.clone, body=%wide.region_15.17_spmd.clone.sunk | while | flops 2726556160 | bytes 200636768 | solution.py:147
  834.5 19.6 %dynamic_update_slice.21 = f32[2,512,8,64]{1,0,3,2:T(2,128)} dynamic-update-slice(f32[2,512,8,64]{1,0,3,2:T(2,128)} %get-tuple-element.526, f32[1,512,8,64]{1,0,3,2:T(1,128)} %copy.83, s32[]{:T(128)S(6)} %copy.106, s32[]{:T(128)} %constant.66.clone.1..sunk, s32[]{:T(128)} %constant.66.clone.1..sunk, s32[]{:T(128)} %constant.66.clone.1..sunk) | dynamic-update-slice | bytes 2097156 | tf_op jit(solution)/shard_map/while/body/jit(dynamic_update_index_in_dim)/dynamic_update_slice | solution.py:97
  897.8 19.6 %dynamic_update_slice.21 = f32[2,512,8,64]{1,0,3,2:T(2,128)} dynamic-update-slice(f32[2,512,8,64]{1,0,3,2:T(2,128)} %get-tuple-element.526, f32[1,512,8,64]{1,0,3,2:T(1,128)} %copy.83, s32[]{:T(128)S(6)} %copy.106, s32[]{:T(128)} %constant.66.clone.1..sunk, s32[]{:T(128)} %constant.66.clone.1..sunk, s32[]{:T(128)} %constant.66.clone.1..sunk) | dynamic-update-slice | bytes 2097156 | tf_op jit(solution)/shard_map/while/body/jit(dynamic_update_index_in_dim)/dynamic_update_slice | solution.py:97
  960.7 10.9 convolution_convert_fusion.3
  975.8 26.0 %reduce-scatter.31.cloned.1.call-done = bf16[256,1408]{1,0:T(8,128)(2,1)} async-done(((bf16[2048,1408]{1,0:T(8,128)(2,1)}), bf16[256,1408]{1,0:T(8,128)(2,1)}) %reduce-scatter.31.cloned.1.call-update) | async-done | bytes 720912 | tf_op jit(solution)/shard_map/reduce_scatter | solution.py:346
  1004.1 111.0 %reduce-scatter.29.cloned.1.call-done = bf16[256,1408]{1,0:T(8,128)(2,1)} async-done(((bf16[2048,1408]{1,0:T(8,128)(2,1)}), bf16[256,1408]{1,0:T(8,128)(2,1)}) %reduce-scatter.29.cloned.1.call-update) | async-done | bytes 720912 | tf_op jit(solution)/shard_map/reduce_scatter | solution.py:343
  1117.5 21.1 %all-reduce.6 = bf16[3,8,64]{2,1,0:T(8,128)(2,1)S(1)} all-reduce(bf16[3,8,64]{2,1,0:T(8,128)(2,1)S(1)} %pad_maximum_fusion.1), channel_id=11, replica_groups=mesh['dp'=8,'tensor'=4] {'dp'}, use_global_device_ids=true, to_apply=%region_31.32.clone | all-reduce | flops 1536 | bytes 6144
  1139.2 47.8 %reduce-scatter.27.cloned.1.call-done = bf16[512,256]{1,0:T(8,128)(2,1)} async-done(((bf16[512,2048]{1,0:T(8,128)(2,1)}), bf16[512,256]{1,0:T(8,128)(2,1)}) %reduce-scatter.27.cloned.1.call-update) | async-done | bytes 262160 | tf_op jit(solution)/shard_map/reduce_scatter | solution.py:340
  1188.9 68.3 %reduce-scatter.25.cloned.1.call-done = bf16[256,512]{1,0:T(8,128)(2,1)} async-done(((bf16[2048,512]{1,0:T(8,128)(2,1)}), bf16[256,512]{1,0:T(8,128)(2,1)}) %reduce-scatter.25.cloned.1.call-update) | async-done | bytes 262160 | tf_op jit(solution)/shard_map/reduce_scatter | solution.py:334
  1259.0 68.7 %reduce-scatter.21.cloned.1.call-done = bf16[256,512]{1,0:T(8,128)(2,1)} async-done(((bf16[2048,512]{1,0:T(8,128)(2,1)}), bf16[256,512]{1,0:T(8,128)(2,1)}) %reduce-scatter.21.cloned.1.call-update) | async-done | bytes 262160 | tf_op jit(solution)/shard_map/reduce_scatter | solution.py:328
  1329.5 68.3 %reduce-scatter.23.cloned.1.call-done = bf16[256,512]{1,0:T(8,128)(2,1)} async-done(((bf16[2048,512]{1,0:T(8,128)(2,1)}), bf16[256,512]{1,0:T(8,128)(2,1)}) %reduce-scatter.23.cloned.1.call-update) | async-done | bytes 262160 | tf_op jit(solution)/shard_map/reduce_scatter | solution.py:331
  1399.7 44.3 %reduce-scatter.19.cloned.1.call-done = bf16[256,2048]{1,0:T(8,128)(2,1)} async-done(((bf16[1024,2048]{1,0:T(8,128)(2,1)}), bf16[256,2048]{1,0:T(8,128)(2,1)}) %reduce-scatter.19.cloned.1.call-update) | async-done | bytes 1048592 | tf_op jit(solution)/shard_map/reduce_scatter | solution.py:314
  1446.3 40.0 %all-reduce.9 = (f32[2048]{0:T(1024)S(1)}, f32[2048]{0:T(1024)S(1)}, f32[2048]{0:T(1024)S(1)}, f32[2048]{0:T(1024)S(1)}) all-reduce(f32[2048]{0:T(1024)S(1)} %get-tuple-element.252, f32[2048]{0:T(1024)S(1)} %get-tuple-element.257, f32[2048]{0:T(1024)S(1)} %copy-done.30, ...), channel_id=6, replica_groups=mesh['dp'=8,'tensor'=4] {'dp','tensor'}, use_global_device_ids=true, to_apply=%region_22.23.clone | all-reduce | flops 8192 | bytes 65536
  (308 shorter events, 285.0 us)
Async XLA Ops:
  7.2 85.5 %all-gather.16.cloned.1.call-start = ((), (), s32[]{:S(2)}) async-start(), calls=%async_computation.13 | async-start | bytes 2359296 | tf_op jit(solution)/shard_map/all_gather | solution.py:190
  7.9 90.6 %all-gather.12.cloned.1.call-start = ((), (), s32[]{:S(2)}) async-start(), calls=%async_computation.11 | async-start | bytes 5242880 | tf_op jit(solution)/shard_map/all_gather | solution.py:205
  58.0 92.0 %all-gather.14.cloned.1.call-start = ((), (), s32[]{:S(2)}) async-start(), calls=%async_computation.12 | async-start | bytes 2359296 | tf_op jit(solution)/shard_map/all_gather | solution.py:189
  58.7 141.0 %all-gather.18.cloned.1.call-start = ((), (), s32[]{:S(2)}) async-start(), calls=%async_computation.14 | async-start | bytes 2359296 | tf_op jit(solution)/shard_map/all_gather | solution.py:191
  59.3 192.0 %all-gather.20.cloned.1.call-start = ((), (), s32[]{:S(2)}) async-start(), calls=%async_computation.15 | async-start | bytes 2359296 | tf_op jit(solution)/shard_map/all_gather | solution.py:193
  59.9 240.5 %reduce-scatter.13.cloned.1.call-start = ((), (), s32[]{:S(2)}) async-start(), calls=%async_computation.16 | async-start | bytes 5242880 | tf_op jit(solution)/shard_map/reduce_scatter | solution.py:218
  257.5 137.9 %all-gather.26.cloned.1.call-start = ((), (), s32[]{:S(2)}) async-start(), calls=%async_computation.19 | async-start | bytes 6488064 | tf_op jit(solution)/shard_map/all_gather | solution.py:195
  258.3 172.1 %all-gather.22.cloned.1.call-start = ((), (), s32[]{:S(2)}) async-start(), calls=%async_computation.17 | async-start | bytes 5242880 | tf_op jit(solution)/shard_map/all_gather | solution.py:225
  258.4 479.6 %copy-start.21 = (f32[2048]{0:T(1024)}, f32[2048]{0:T(1024)S(1)}, u32[]{:S(2)}) copy-start(f32[2048]{0:T(1024)S(1)} %convert_element_type.188) | copy-start | bytes 24580
  302.1 435.9 %copy-start.28 = (f32[256]{0:T(256)}, f32[256]{0:T(256)S(1)}, u32[]{:S(2)}) copy-start(f32[256]{0:T(256)S(1)} %broadcast_multiply_fusion.4) | copy-start | bytes 3076
  302.6 435.4 %copy-start.34 = (f32[256]{0:T(256)}, f32[256]{0:T(256)S(1)}, u32[]{:S(2)}) copy-start(f32[256]{0:T(256)S(1)} %add_rsqrt_fusion) | copy-start | bytes 3076
  304.1 221.3 %all-gather.24.cloned.1.call-start = ((), (), s32[]{:S(2)}) async-start(), calls=%async_computation.18 | async-start | bytes 6488064 | tf_op jit(solution)/shard_map/all_gather | solution.py:194
  304.9 254.8 %all-gather.30.cloned.1.call-start = ((), (), s32[]{:S(2)}) async-start(), calls=%async_computation.22 | async-start | bytes 5242880 | tf_op jit(solution)/shard_map/all_gather | solution.py:251
  305.5 350.1 %all-gather.28.cloned.1.call-start = ((), (), s32[]{:S(2)}) async-start(), calls=%async_computation.20 | async-start | bytes 6488064 | tf_op jit(solution)/shard_map/all_gather | solution.py:196
  306.2 428.7 %reduce-scatter.17.cloned.1.call-start = ((), (), s32[]{:S(2)}) async-start(), calls=%async_computation.23 | async-start | bytes 5242880 | tf_op jit(solution)/shard_map/reduce_scatter | solution.py:266
  692.0 82.8 %all-gather.32.cloned.1.call-start = ((), (), s32[]{:S(2)}) async-start(), calls=%async_computation.24 | async-start | bytes 5242880 | tf_op jit(solution)/shard_map/all_gather | solution.py:279
  740.2 233.3 %reduce-scatter.33.cloned.1.call-start = ((), (), s32[]{:S(2)}) async-start(), calls=%async_computation.32 | async-start | bytes 6488064 | tf_op jit(solution)/shard_map/reduce_scatter | solution.py:349
  750.8 251.0 %reduce-scatter.31.cloned.1.call-start = ((), (), s32[]{:S(2)}) async-start(), calls=%async_computation.31 | async-start | bytes 6488064 | tf_op jit(solution)/shard_map/reduce_scatter | solution.py:346
  761.9 353.3 %reduce-scatter.29.cloned.1.call-start = ((), (), s32[]{:S(2)}) async-start(), calls=%async_computation.30 | async-start | bytes 6488064 | tf_op jit(solution)/shard_map/reduce_scatter | solution.py:343
  773.1 414.0 %reduce-scatter.27.cloned.1.call-start = ((), (), s32[]{:S(2)}) async-start(), calls=%async_computation.29 | async-start | bytes 2359296 | tf_op jit(solution)/shard_map/reduce_scatter | solution.py:340
  791.7 465.5 %reduce-scatter.25.cloned.1.call-start = ((), (), s32[]{:S(2)}) async-start(), calls=%async_computation.28 | async-start | bytes 2359296 | tf_op jit(solution)/shard_map/reduce_scatter | solution.py:334
  925.7 402.0 %reduce-scatter.21.cloned.1.call-start = ((), (), s32[]{:S(2)}) async-start(), calls=%async_computation.26 | async-start | bytes 2359296 | tf_op jit(solution)/shard_map/reduce_scatter | solution.py:328
  939.3 458.6 %reduce-scatter.23.cloned.1.call-start = ((), (), s32[]{:S(2)}) async-start(), calls=%async_computation.27 | async-start | bytes 2359296 | tf_op jit(solution)/shard_map/reduce_scatter | solution.py:331
  945.6 498.3 %reduce-scatter.19.cloned.1.call-start = ((), (), s32[]{:S(2)}) async-start(), calls=%async_computation.25 | async-start | bytes 5242880 | tf_op jit(solution)/shard_map/reduce_scatter | solution.py:314
  958.9 532.9 %reduce-scatter.15.cloned.1.call-start = ((), (), s32[]{:S(2)}) async-start(), calls=%async_computation.21 | async-start | bytes 5242880 | tf_op jit(solution)/shard_map/reduce_scatter | solution.py:233
  1117.4 326.5 %copy-start.6 = (bf16[256,2048]{1,0:T(8,128)(2,1)S(1)}, bf16[256,2048]{1,0:T(8,128)(2,1)}, u32[]{:S(2)}) copy-start(bf16[256,2048]{1,0:T(8,128)(2,1)} %param.19) | copy-start | bytes 3145732
  1117.4 326.5 %copy-start.26 = (f32[2048]{0:T(1024)S(1)}, f32[2048]{0:T(1024)}, u32[]{:S(2)}) copy-start(f32[2048]{0:T(1024)} %copy-done.25) | copy-start | bytes 24580
  1117.4 326.5 %copy-start.33 = (f32[256]{0:T(256)S(1)}, f32[256]{0:T(256)}, u32[]{:S(2)}) copy-start(f32[256]{0:T(256)} %copy-done.32) | copy-start | bytes 3076
  1117.4 326.5 %copy-start.37 = (f32[256]{0:T(256)S(1)}, f32[256]{0:T(256)}, u32[]{:S(2)}) copy-start(f32[256]{0:T(256)} %copy-done.36) | copy-start | bytes 3076
  1188.9 303.0 %copy-start.9 = (bf16[256,2048]{1,0:T(8,128)(2,1)S(1)}, bf16[256,2048]{1,0:T(8,128)(2,1)}, u32[]{:S(2)}) copy-start(bf16[256,2048]{1,0:T(8,128)(2,1)} %reduce-scatter.13.cloned.1.call-done) | copy-start | bytes 3145732
  1188.9 303.0 %copy-start.13 = (bf16[256,2048]{1,0:T(8,128)(2,1)S(1)}, bf16[256,2048]{1,0:T(8,128)(2,1)}, u32[]{:S(2)}) copy-start(bf16[256,2048]{1,0:T(8,128)(2,1)} %param.20) | copy-start | bytes 3145732
  1188.9 303.0 %copy-start.22 = (f32[2048]{0:T(1024)S(1)}, f32[2048]{0:T(1024)}, u32[]{:S(2)}) copy-start(f32[2048]{0:T(1024)} %copy-done.21) | copy-start | bytes 24580
  (50 other events, 2135.7 us)
Sparse Core Ops, SparseCore 0:
  10.1 53.1 all-gather.15
  65.5 32.9 all-gather.11
  100.7 49.2 all-gather.13
  152.0 47.7 all-gather.17
  201.7 49.5 all-gather.19
  257.7 42.6 reduce-scatter.12
  302.8 92.6 all-gather.25
  397.7 32.6 all-gather.21
  432.8 92.6 all-gather.23
  526.9 32.6 all-gather.29
  561.9 93.5 all-gather.27
  692.2 42.6 reduce-scatter.16
  740.3 34.4 all-gather.31
  778.4 110.2 reduce-scatter.32
  892.2 109.6 reduce-scatter.30
  1005.3 109.7 reduce-scatter.28
  1118.5 68.5 reduce-scatter.26
  1190.5 66.6 reduce-scatter.24
  1260.8 66.9 reduce-scatter.20
  1331.1 66.7 reduce-scatter.22
  1400.4 43.4 reduce-scatter.18
  1446.6 45.1 reduce-scatter.14
where the time goes:
time: 1520 us; the launch traced here: 1500 us
  waiting for transfers between devices  960 us (63%)
  matrix products  242 us (16%)
  blocking collectives  135 us (9%)
  local copies, waits for them, and re-layouts  75.8 us (5%)
  other arithmetic  73.5 us (5%)
  between operations  15.8 us (1%)
    reduce_scatter x1, waiting for transfers between devices, on_device(): lax.psum_scatter(gate_weight_grad.astype(jnp.bfloat16), 'dp', scatter_dim...  111 us
    unnamed x3, blocking collectives  104 us
    all_gather x1, waiting for transfers between devices, on_device(): lax.all_gather(w_down, 'dp', axis=1, tiled=True)  95.9 us
    all_gather x1, waiting for transfers between devices, on_device(): lax.all_gather(w_up, 'dp', axis=0, tiled=True)  89.2 us
    all_gather x1, waiting for transfers between devices, on_device(): lax.all_gather(w_gate, 'dp', axis=0, tiled=True)  83.2 us
    reduce_scatter x1, waiting for transfers between devices, on_device(): lax.psum_scatter(query_weight_grad.astype(jnp.bfloat16), 'dp', scatter_di...  68.7 us
    reduce_scatter x1, waiting for transfers between devices, on_device(): lax.psum_scatter(key_weight_grad.astype(jnp.bfloat16), 'dp', scatter_dime...  68.3 us
    reduce_scatter x1, waiting for transfers between devices, on_device(): lax.psum_scatter(value_weight_grad.astype(jnp.bfloat16), 'dp', scatter_di...  68.3 us
  transfers between devices with their start and end apart: 22, of which 20 were waited for; matrix products, arithmetic and copies ran while one was open for 22% of the time, Pallas kernels for 0%

commit v1 on v0

v1 whole, which is shorter than its diff:
```python
import functools

import jax
import jax.experimental.pallas as pl
import jax.experimental.pallas.tpu as pltpu
import jax.numpy as jnp
from jax import lax
from jax.sharding import PartitionSpec as P

HD = 64
ROT = 16
PAIR = 2 * HD
EPSILON = 1e-05
NEGATIVE = -1e30
F32 = jnp.float32
BF16 = jnp.bfloat16
MIB = 2**20


def product(left, right, left_dim, right_dim):
    return lax.dot_general(
        left, right, (((left_dim,), (right_dim,)), ((), ())), preferred_element_type=F32
    )


def turn(columns, cos_values, sin_values, opening):
    partner = jnp.where(opening, pltpu.roll(columns, PAIR - 8, 1), pltpu.roll(columns, 8, 1))
    return columns * cos_values + partner * sin_values


def opening_lanes(rows):
    return lax.broadcasted_iota(jnp.int32, (rows, PAIR), 1) % HD < 8


def qkv_body(x_ref, qk_weight, v_weight, bias_ref, cos_ref, sin_ref, qk_ref, v_ref):
    width = qk_ref.shape[1]
    rows = x_ref[...]
    opening = opening_lanes(rows.shape[0])
    cos_values = cos_ref[...]
    sin_values = sin_ref[...]
    both = product(rows, qk_weight[...], 1, 0) + bias_ref[:, :width]
    for at in range(0, width, PAIR):
        part = turn(both[:, at : at + PAIR], cos_values, sin_values, opening)
        qk_ref[:, at : at + PAIR] = part.astype(BF16)
    v_ref[...] = (product(rows, v_weight[...], 1, 0) + bias_ref[:, width:]).astype(BF16)


def project_qkv(rows, weight_qk, weight_vo, bias_row, cos_table, sin_table):
    length, depth = rows.shape
    wide = weight_qk.shape[1]
    block = min(256, length)
    by_rows = lambda columns: pl.BlockSpec((block, columns), lambda i: (i, 0))
    whole = lambda shape: pl.BlockSpec(shape, lambda i: (0, 0))
    return pl.pallas_call(
        qkv_body,
        grid=(length // block,),
        in_specs=[
            by_rows(depth),
            whole((depth, wide)),
            whole((depth, wide // 2)),
            whole((1, 3 * wide // 2)),
            by_rows(PAIR),
            by_rows(PAIR),
        ],
        out_specs=[by_rows(wide), by_rows(wide // 2)],
        out_shape=[
            jax.ShapeDtypeStruct((length, wide), BF16),
            jax.ShapeDtypeStruct((length, wide // 2), BF16),
        ],
        compiler_params=pltpu.CompilerParams(vmem_limit_bytes=48 * MIB),
        cost_estimate=pl.CostEstimate(
            flops=3 * length * depth * wide, bytes_accessed=8 * length * depth, transcendentals=0
        ),
        name="project_qkv",
    )(rows, weight_qk, weight_vo, bias_row, cos_table, sin_table)


def forward_body(block, count, place_ref, q_ref, k_ref, v_ref, down_ref, across_ref, mixed_ref, lse_ref):
    place = place_ref[0]
    lane = lax.broadcasted_iota(jnp.int32, (block, PAIR), 1)
    earlier = lax.broadcasted_iota(jnp.int32, (block, block), 0) <= lax.broadcasted_iota(
        jnp.int32, (block, block), 1
    )
    spans = [
        pl.ds(pl.multiple_of(jnp.bitwise_xor(i, place) * block, block), block) for i in range(count)
    ]
    for i in range(count):
        queries = q_ref[spans[i], :] * jnp.asarray(HD**-0.5, BF16)
        segment = across_ref[:, spans[i]]
        kept = [down_ref[spans[j], :] == segment for j in range(i + 1)]
        kept[i] = kept[i] & earlier
        sums = []
        for half in range(2):
            mine = lane < HD if half == 0 else lane >= HD
            chosen = jnp.where(mine, queries, jnp.zeros_like(queries))
            scores = [
                jnp.where(kept[j], product(k_ref[spans[j], :], chosen, 1, 1), NEGATIVE)
                for j in range(i + 1)
            ]
            top = scores[0].max(0, keepdims=True)
            for part in scores[1:]:
                top = jnp.maximum(top, part.max(0, keepdims=True))
            raised = [jnp.exp(part - top) for part in scores]
            total = raised[0].sum(0, keepdims=True)
            for part in raised[1:]:
                total = total + part.sum(0, keepdims=True)
            inverse = 1.0 / total
            out = None
            for j in range(i + 1):
                term = product((raised[j] * inverse).astype(BF16), v_ref[spans[j], :], 0, 0)
                out = term if out is None else out + term
            sums.append(out)
            lse_ref[0, half : half + 1, spans[i]] = top + jnp.log(total)
        mixed_ref[spans[i], :] = jnp.where(lane < HD, sums[0], sums[1]).astype(BF16)


def attend_forward(place, qk, values, segment_down, segment_across, count):
    length, width = values.shape
    pairs = width // PAIR
    columns = lambda first: pl.BlockSpec((length, PAIR), lambda h, place: (0, h + first))
    whole = lambda shape: pl.BlockSpec(shape, lambda h, place: (0, 0))
    return pl.pallas_call(
        functools.partial(forward_body, length // count, count),
        grid_spec=pltpu.PrefetchScalarGridSpec(
            num_scalar_prefetch=1,
            grid=(pairs,),
            in_specs=[columns(0), columns(pairs), columns(0), whole((length, 1)), whole((1, length))],
            out_specs=[columns(0), pl.BlockSpec((1, 2, length), lambda h, place: (h, 0, 0))],
        ),
        out_shape=[
            jax.ShapeDtypeStruct((length, width), BF16),
            jax.ShapeDtypeStruct((pairs, 2, length), F32),
        ],
        compiler_params=pltpu.CompilerParams(vmem_limit_bytes=48 * MIB),
        cost_estimate=pl.CostEstimate(
            flops=4 * length * length * width,
            bytes_accessed=8 * length * width,
            transcendentals=length * length * width // PAIR,
        ),
        name="attend_forward",
    )(place, qk, qk, values, segment_down, segment_across)


def backward_body(
    block,
    count,
    place_ref,
    q_ref,
    k_ref,
    v_ref,
    mixed_ref,
    grad_ref,
    lse_ref,
    down_ref,
    across_ref,
    cos_ref,
    sin_ref,
    q_grad_ref,
    k_grad_ref,
    v_grad_ref,
    bias_ref,
    q_total,
    k_total,
    v_total,
):
    place = place_ref[0]
    lane = lax.broadcasted_iota(jnp.int32, (block, PAIR), 1)
    earlier = lax.broadcasted_iota(jnp.int32, (block, block), 0) <= lax.broadcasted_iota(
        jnp.int32, (block, block), 1
    )
    spans = [
        pl.ds(pl.multiple_of(jnp.bitwise_xor(i, place) * block, block), block) for i in range(count)
    ]
    for i in range(count):
        queries = q_ref[spans[i], :] * jnp.asarray(HD**-0.5, BF16)
        upstream = grad_ref[spans[i], :]
        centres = (upstream.astype(F32) * mixed_ref[spans[i], :].astype(F32)).T
        segment = across_ref[:, spans[i]]
        kept = [down_ref[spans[j], :] == segment for j in range(i + 1)]
        kept[i] = kept[i] & earlier
        sums = []
        for half in range(2):
            mine = lane < HD if half == 0 else lane >= HD
            nothing = jnp.zeros_like(queries)
            chosen = jnp.where(mine, queries, nothing)
            chosen_grad = jnp.where(mine, upstream, nothing)
            log_total = lse_ref[0, half : half + 1, spans[i]]
            centre = centres[half * HD : (half + 1) * HD, :].sum(0, keepdims=True)
            q_sum = None
            for j in range(i + 1):
                keys = k_ref[spans[j], :]
                scores = jnp.where(kept[j], product(keys, chosen, 1, 1), NEGATIVE)
                weights = jnp.exp(scores - log_total)
                weight_grad = product(v_ref[spans[j], :], chosen_grad, 1, 1)
                score_grad = (weights * (weight_grad - centre)).astype(BF16)
                v_term = product(weights.astype(BF16), chosen_grad, 1, 0)
                k_term = product(score_grad, chosen, 1, 0)
                term = product(score_grad, keys, 0, 0)
                q_sum = term if q_sum is None else q_sum + term
                if i == j and half == 0:
                    v_total[spans[j], :] = v_term
                    k_total[spans[j], :] = k_term
                else:
                    v_total[spans[j], :] += v_term
                    k_total[spans[j], :] += k_term
            sums.append(q_sum)
        q_total[spans[i], :] = jnp.where(lane < HD, sums[0], sums[1])
    opening = opening_lanes(block * count)
    cos_values = cos_ref[...]
    sin_values = -sin_ref[...]
    q_grad = turn(q_total[...] * (HD**-0.5), cos_values, sin_values, opening).astype(BF16)
    k_grad = turn(k_total[...], cos_values, sin_values, opening).astype(BF16)
    v_grad = v_total[...].astype(BF16)
    for at, (ref, grad) in enumerate(
        ((q_grad_ref, q_grad), (k_grad_ref, k_grad), (v_grad_ref, v_grad))
    ):
        ref[...] = grad
        bias_ref[0, at : at + 1, :] = grad.astype(F32).sum(0, keepdims=True)


def attend_backward(
    place, qk, values, mixed, mixed_grad, lse, segment_down, segment_across, cos_table, sin_table, count
):
    length, width = values.shape
    pairs = width // PAIR
    columns = lambda first: pl.BlockSpec((length, PAIR), lambda h, place: (0, h + first))
    whole = lambda shape: pl.BlockSpec(shape, lambda h, place: (0, 0))
    return pl.pallas_call(
        functools.partial(backward_body, length // count, count),
        grid_spec=pltpu.PrefetchScalarGridSpec(
            num_scalar_prefetch=1,
            grid=(pairs,),
            in_specs=[
                columns(0),
                columns(pairs),
                columns(0),
                columns(0),
                columns(0),
                pl.BlockSpec((1, 2, length), lambda h, place: (h, 0, 0)),
                whole((length, 1)),
                whole((1, length)),
                whole((length, PAIR)),
                whole((length, PAIR)),
            ],
            out_specs=[
                columns(0),
                columns(0),
                columns(0),
                pl.BlockSpec((1, 3, PAIR), lambda h, place: (h, 0, 0)),
            ],
            scratch_shapes=[pltpu.VMEM((length, PAIR), F32)] * 3,
        ),
        out_shape=[jax.ShapeDtypeStruct((length, width), BF16)] * 3
        + [jax.ShapeDtypeStruct((pairs, 3, PAIR), F32)],
        compiler_params=pltpu.CompilerParams(vmem_limit_bytes=48 * MIB),
        cost_estimate=pl.CostEstimate(
            flops=10 * length * length * width,
            bytes_accessed=20 * length * width,
            transcendentals=length * length * width // PAIR,
        ),
        name="attend_backward",
    )(
        place, qk, qk, values, mixed, mixed_grad, lse, segment_down, segment_across, cos_table, sin_table
    )


class Route:
    def __init__(self, count):
        self.count = count
        self.reach = count // 2
        self.ring = list(range(0, count, 2)) + list(range(count - 1, 0, -2))
        ahead = [(self.ring[i], self.ring[(i + 1) % count]) for i in range(count)]
        self.pairs = (ahead, [(b, a) for a, b in ahead])

    def send(self, values, direction):
        return lax.ppermute(values, "dp", self.pairs[direction])


class Gathering:
    def __init__(self, route, block, longer):
        self.route = route
        self.blocks = {0: block}
        self.hops = [route.reach - (direction != longer) for direction in range(2)]
        self.done = 0
        self.flying = [block]

    def pending(self):
        return self.flying

    def resume(self, arrived):
        route = self.route
        if self.done == 0:
            self.blocks[0] = arrived[0]
            latest = [arrived[0], arrived[0]]
        else:
            arrived = list(arrived)
            latest = [None, None]
            for direction in range(2):
                if self.done <= self.hops[direction]:
                    latest[direction] = arrived.pop(0)
                    at = route.count - self.done if direction == 0 else self.done
                    self.blocks[at] = latest[direction]
        self.done += 1
        self.flying = [
            route.send(latest[direction], direction)
            for direction in range(2)
            if self.done <= self.hops[direction]
        ]

    def all(self, axis):
        return jnp.concatenate([self.blocks[j] for j in range(self.route.count)], axis=axis)


class Summing:
    def __init__(self, route, own, longer):
        self.route = route
        self.own = own
        self.hops = [route.reach - (direction != longer) for direction in range(2)]
        self.done = 0
        self.flying = None
        self.last = [None, None]

    def target(self, direction):
        left = self.hops[direction] - self.done
        return left if direction == 0 else (self.route.count - left) % self.route.count

    def pending(self):
        if self.done == 0:
            return [self.own(self.target(direction)) for direction in range(2)]
        return self.flying

    def resume(self, arrived):
        arrived = list(arrived)
        sending = []
        for direction in range(2):
            if self.done <= self.hops[direction]:
                values = arrived.pop(0)
                if self.done == self.hops[direction]:
                    self.last[direction] = values
                    continue
                if self.done:
                    own = self.own(self.target(direction))
                    values = (values.astype(F32) + own.astype(F32)).astype(BF16)
                sending.append((direction, values))
        self.done += 1
        self.flying = [self.route.send(values, direction) for direction, values in sending]

    def total(self):
        return self.own(0).astype(F32) + self.last[0].astype(F32) + self.last[1].astype(F32)


STEPS = 10


class Flow:
    def __init__(self, first, second):
        self.streams = (first, second)
        self.events = 2 * first.route.reach + 2
        self.event = 0
        self.step = 0

    def moves(self):
        self.event += 1
        event = self.event - 1
        stream = self.streams[event % 2]
        return [stream]

    def due(self):
        return self.event * STEPS < self.step * self.events


def advance(flows, *carried):
    for flow in flows:
        flow.step += 1
    first = True
    while first or any(flow.due() for flow in flows):
        first = False
        moving = [stream for flow in flows if flow.due() for stream in flow.moves()]
        waiting = [list(stream.pending()) for stream in moving]
        flat = [values for group in waiting for values in group]
        out = lax.optimization_barrier(tuple(flat) + tuple(carried))
        carried = out[len(flat) :]
        at = 0
        for stream, group in zip(moving, waiting):
            stream.resume(out[at : at + len(group)])
            at += len(group)
    return carried[0] if len(carried) == 1 else carried


def standardize(inputs):
    average = jnp.mean(inputs, axis=-1, keepdims=True)
    centred = inputs - average
    inverse = lax.rsqrt(jnp.mean(centred * centred, axis=-1, keepdims=True) + EPSILON)
    return centred * inverse, average, inverse


def norm_backward(upstream, standard, inverse, gain_vec):
    scaled = upstream * gain_vec
    inner = (
        scaled
        - jnp.mean(scaled, axis=-1, keepdims=True)
        - standard * jnp.mean(scaled * standard, axis=-1, keepdims=True)
    )
    return inverse * inner


def turning_tables(segment_ids):
    length = segment_ids.shape[0]
    places = jnp.arange(length, dtype=jnp.int32)
    starts = jnp.concatenate([jnp.ones((1,), dtype=jnp.bool_), segment_ids[1:] != segment_ids[:-1]])
    begins = lax.cummax(jnp.where(starts, places, 0), axis=0)
    return (places - begins).astype(F32)


def across_core(values):
    return lax.ppermute(values, "tensor", [(i, i ^ 1) for i in range(4)])


def across_chip(values):
    return lax.ppermute(values, "tensor", [(i, i ^ 2) for i in range(4)])


def on_device(
    route,
    activations,
    cotangent,
    segments,
    norm_one_gain,
    norm_one_bias,
    w_query,
    w_key,
    w_value,
    qkv_bias,
    w_out,
    norm_two_gain,
    norm_two_bias,
    w_gate,
    w_up,
    w_down,
):
    count = route.count
    own_rows, depth = activations.shape
    length = segments.shape[0]
    width = depth // count
    heads_wide = w_query.shape[1]
    local_heads = heads_wide // HD
    hidden_wide = w_gate.shape[1]
    shards = length // own_rows
    here = lax.axis_index("tensor")
    ring = jnp.array(route.ring, jnp.int32)
    positions = jnp.array([route.ring.index(i) for i in range(count)], jnp.int32)
    position = positions[lax.axis_index("dp")]
    order = ring[(position + jnp.arange(count, dtype=jnp.int32)) % count]
    back_order = (positions - position) % count

    def pick_columns(values, chosen):
        return jnp.concatenate(
            [
                lax.dynamic_slice_in_dim(values, chosen[j] * width, width, axis=-1)
                for j in range(count)
            ],
            axis=-1,
        )

    def pick_rows(values):
        return jnp.concatenate(
            [
                lax.dynamic_slice_in_dim(
                    values, jnp.bitwise_xor(i, here) * own_rows, own_rows, axis=0
                )
                for i in range(shards)
            ],
            axis=0,
        )

    own_bf16 = pick_columns(activations, order)
    own_grad = pick_columns(cotangent, order)
    own_inputs = own_bf16.astype(F32)

    bias_size = qkv_bias.size
    norm_part = norm_one_gain.shape[0]
    packed = jnp.concatenate(
        [norm_one_gain, norm_one_bias, norm_two_gain, norm_two_bias, qkv_bias.reshape(-1)]
    )
    packed = jnp.pad(packed, (0, 16 * 128 - packed.shape[0])).reshape(16, 128)
    small = lax.all_gather(packed, ("dp", "tensor"), axis=0, tiled=True)

    flow_one = Flow(
        Gathering(route, jnp.concatenate([w_query, w_key], axis=1), 0),
        Gathering(route, jnp.concatenate([w_value, w_out.T], axis=1), 1),
    )
    flow_two = Flow(Gathering(route, w_gate, 0), Gathering(route, w_up, 1))
    flow_three = Flow(
        Gathering(route, w_down[: hidden_wide // 2], 0),
        Gathering(route, w_down[hidden_wide // 2 :], 1),
    )

    x_chip = across_chip(own_bf16)
    x_core = across_core(own_bf16)
    advance([flow_one])
    advance([flow_one])
    within = turning_tables(segments)
    frequency = 10000.0 ** (-2.0 * jnp.arange(ROT // 2, dtype=F32) / ROT)
    within = pick_rows(within)
    angles = within[:, None] * frequency[None, :]
    cos_part, sin_part = jnp.cos(angles), jnp.sin(angles)
    rest = jnp.zeros((length, HD - ROT), F32)
    cos_table = jnp.concatenate([cos_part, cos_part, rest + 1.0] * 2, axis=1)
    sin_table = jnp.concatenate([-sin_part, sin_part, rest] * 2, axis=1)
    segment_rel = pick_rows(segments)
    segment_down, segment_across = segment_rel[:, None], segment_rel[None, :]
    place = here.astype(jnp.int32).reshape(1)
    x_core, cos_table, sin_table = advance([flow_one], x_core, cos_table, sin_table)
    x_chip, own_grad = advance([flow_one], x_chip, own_grad)
    x_far = across_core(x_chip)
    g_chip = across_chip(own_grad)
    g_core = across_core(own_grad)
    x_far, small, g_core = advance([flow_one], x_far, small, g_core)

    table = small.reshape(count, shards, 16 * 128)
    norm_values = [
        table[:, :, k * norm_part : (k + 1) * norm_part].reshape(1, depth).astype(F32)
        for k in range(4)
    ]
    gain_one, shift_one, gain_two, shift_two = (pick_columns(v, order) for v in norm_values)
    bias_row = lax.dynamic_index_in_dim(table, here, axis=1, keepdims=False)
    bias_row = bias_row[:, 4 * norm_part : 4 * norm_part + bias_size]
    bias_row = bias_row.reshape(count, 3, local_heads, HD // count).transpose(1, 2, 0, 3)
    bias_row = bias_row.reshape(1, 3 * heads_wide).astype(F32)

    x_all = jnp.concatenate([own_bf16, x_core, x_chip, x_far], axis=0)
    standard_one, mean_one, inverse_one = standardize(x_all.astype(F32))
    normed = (standard_one * gain_one + shift_one).astype(BF16)
    normed, x_all, mean_one, inverse_one, gain_two, shift_two, bias_row = advance(
        [flow_one], normed, x_all, mean_one, inverse_one, gain_two, shift_two, bias_row
    )
    g_chip = advance([flow_one, flow_two], g_chip)
    g_far = across_core(g_chip)
    g_far = advance([flow_one, flow_two], g_far)
    grad_all = jnp.concatenate([own_grad, g_core, g_chip, g_far], axis=0)
    grad_all = advance([flow_one], grad_all)
    advance([flow_one, flow_two])
    weight_qk = flow_one.streams[0].all(0)
    weight_vo = flow_one.streams[1].all(0)
    weight_out = weight_vo[:, heads_wide:]

    qk, values = project_qkv(normed, weight_qk, weight_vo, bias_row, cos_table, sin_table)
    qk, values, weight_out = advance([flow_two], qk, values, weight_out)
    mixed, lse = attend_forward(place, qk, values, segment_down, segment_across, shards)
    mixed, lse = advance([flow_two], mixed, lse)

    half = length // 2
    third = own_rows

    def sum_over_heads(far):
        crossed = across_core(far[third:])
        return (far[:third].astype(F32) + crossed.astype(F32)).astype(BF16)

    far = product(mixed[half:], weight_out, 1, 1).astype(BF16)
    far_sum = sum_over_heads(far)
    arriving = across_chip(far_sum)
    near = product(mixed[:half], weight_out, 1, 1).astype(BF16)
    near_core = across_core(near[third:])
    near, near_core = advance([flow_two], near, near_core)
    near_sum = own_inputs + near[:third].astype(F32) + near_core.astype(F32)
    arriving, near_sum = advance([flow_two], arriving, near_sum)
    middle = near_sum + arriving.astype(F32)
    standard_two, _, inverse_two = standardize(middle)
    normed_two_own = (standard_two * gain_two + shift_two).astype(BF16)
    n_chip = across_chip(normed_two_own)
    n_core = across_core(normed_two_own)
    middle, standard_two, inverse_two, normed_two_own, n_core = advance(
        [flow_two, flow_three], middle, standard_two, inverse_two, normed_two_own, n_core
    )
    n_chip = advance([flow_two, flow_three], n_chip)
    n_far = across_core(n_chip)
    n_far = advance([flow_two, flow_three], n_far)
    normed_two = jnp.concatenate([normed_two_own, n_core, n_chip, n_far], axis=0)
    normed_two = advance([flow_three], normed_two)

    weight_gate = flow_two.streams[0].all(0)
    weight_up = flow_two.streams[1].all(0)
    gate_values = product(normed_two, weight_gate, 1, 0)
    gate_values, weight_up = advance([flow_three], gate_values, weight_up)
    up_values = product(normed_two, weight_up, 1, 0)
    sigmoid_gate = jax.nn.sigmoid(gate_values)
    silu_gate = gate_values * sigmoid_gate
    hidden = (silu_gate * up_values).astype(BF16)
    hidden, up_values = advance([flow_three], hidden, up_values)
    down_grad = product(hidden, grad_all, 0, 0).astype(BF16)
    down_grad = advance([flow_three], down_grad)
    block = lambda j: slice(j * width, (j + 1) * width)
    back_one = Flow(
        Summing(route, lambda j: down_grad[: hidden_wide // 2, block(j)], 0),
        Summing(route, lambda j: down_grad[hidden_wide // 2 :, block(j)], 1),
    )
    advance([flow_three, back_one])
    advance([flow_three, back_one])
    advance([flow_three])
    down_blocks = [stream.all(1) for stream in flow_three.streams]
    weight_down = jnp.concatenate(down_blocks, axis=0)

    hidden_grad = product(grad_all, weight_down, 1, 1)
    gate_grad = (hidden_grad * up_values * (sigmoid_gate + silu_gate * (1.0 - sigmoid_gate))).astype(
        BF16
    )
    up_grad = (hidden_grad * silu_gate).astype(BF16)
    gate_grad, up_grad = advance([back_one], gate_grad, up_grad)

    def through_gates(rows):
        return (
            product(gate_grad[rows], weight_gate, 1, 1) + product(up_grad[rows], weight_up, 1, 1)
        ).astype(BF16)

    far = through_gates(slice(half, None))
    far = advance([back_one], far)
    far_sum = sum_over_heads(far)
    arriving = across_chip(far_sum)
    near = through_gates(slice(0, half))
    near_core = across_core(near[third:])
    near, near_core = advance([back_one], near, near_core)
    gate_sum = product(normed_two, gate_grad, 0, 0).astype(BF16)
    gate_sum = advance([back_one], gate_sum)
    up_sum = product(normed_two, up_grad, 0, 0).astype(BF16)
    near_sum = near[:third].astype(F32) + near_core.astype(F32)
    up_sum, near_sum, arriving = advance([back_one], up_sum, near_sum, arriving)
    back_two = Flow(
        Summing(route, lambda j: gate_sum[block(j)], 0),
        Summing(route, lambda j: up_sum[block(j)], 1),
    )
    advance([back_one, back_two])
    normed_two_grad = near_sum + arriving.astype(F32)
    middle_grad = own_grad.astype(F32) + norm_backward(
        normed_two_grad, standard_two, inverse_two, gain_two
    )
    gain_two_grad = jnp.sum(normed_two_grad * standard_two, axis=0, keepdims=True)
    shift_two_grad = jnp.sum(normed_two_grad, axis=0, keepdims=True)
    branch_own = middle_grad.astype(BF16)
    b_chip = across_chip(branch_own)
    b_core = across_core(branch_own)
    middle_grad, branch_own, gain_two_grad, shift_two_grad, b_core = advance(
        [back_one, back_two], middle_grad, branch_own, gain_two_grad, shift_two_grad, b_core
    )
    far_result = product(hidden[half:], weight_down, 1, 0).astype(BF16)
    far_result = advance([back_one, back_two], far_result)
    near_result = product(hidden[:half], weight_down, 1, 0).astype(BF16)
    near_result, b_chip = advance([back_two], near_result, b_chip)
    b_far = across_core(b_chip)
    far_sum = sum_over_heads(far_result)
    arriving_result = across_chip(far_sum)
    near_core = across_core(near_result[third:])
    b_far, near_core = advance([back_two], b_far, near_core)
    branch = jnp.concatenate([branch_own, b_core, b_chip, b_far], axis=0)
    mixed_grad = product(branch, weight_out, 1, 0).astype(BF16)
    near_sum = middle + near_result[:third].astype(F32) + near_core.astype(F32)
    mixed_grad, branch, near_sum = advance([back_two], mixed_grad, branch, near_sum)
    q_grad, k_grad, v_grad, bias_sums = attend_backward(
        place,
        qk,
        values,
        mixed,
        mixed_grad,
        lse,
        segment_down,
        segment_across,
        cos_table,
        sin_table,
        shards,
    )
    q_grad, k_grad, v_grad, bias_sums, arriving_result = advance(
        [back_two], q_grad, k_grad, v_grad, bias_sums, arriving_result
    )
    result = pick_columns((near_sum + arriving_result.astype(F32)).astype(BF16), back_order)

    def through_heads(rows):
        return (
            product(q_grad[rows], weight_qk[:, :heads_wide], 1, 1)
            + product(k_grad[rows], weight_qk[:, heads_wide:], 1, 1)
            + product(v_grad[rows], weight_vo[:, :heads_wide], 1, 1)
        )

    far_whole = through_heads(slice(half, None))
    far_sum = sum_over_heads(far_whole.astype(BF16))
    arriving = across_chip(far_sum)
    out_sum = product(branch, mixed, 0, 0).astype(BF16)
    v_sum = product(normed, v_grad, 0, 0).astype(BF16)
    out_sum, v_sum, far_whole, result = advance([back_two], out_sum, v_sum, far_whole, result)
    near_whole = through_heads(slice(0, half))
    near = near_whole.astype(BF16)
    near_core = across_core(near[third:])

    def token_sums(rows, upstream):
        standard = (x_all[rows].astype(F32) - mean_one[rows]) * inverse_one[rows]
        return jnp.concatenate(
            [
                jnp.sum(upstream * standard, axis=0, keepdims=True),
                jnp.sum(upstream, axis=0, keepdims=True),
            ],
            axis=0,
        )

    one_grads = token_sums(slice(half, None), far_whole) + token_sums(slice(0, half), near_whole)
    q_sum = product(normed, q_grad, 0, 0).astype(BF16)
    k_sum = product(normed, k_grad, 0, 0).astype(BF16)
    near, near_core, one_grads, q_sum, k_sum = advance(
        [back_two], near, near_core, one_grads, q_sum, k_sum
    )
    norm_grads = jnp.concatenate([one_grads, gain_two_grad, shift_two_grad], axis=0)
    bias_sums = bias_sums.transpose(1, 0, 2).reshape(3, local_heads, count, HD // count)
    bias_sums = jnp.take(bias_sums, order, axis=2).transpose(2, 0, 1, 3).reshape(count, bias_size)
    extras = jnp.concatenate(
        [norm_grads.reshape(4, count, width).transpose(1, 0, 2).reshape(count, 4 * width), bias_sums],
        axis=1,
    )
    wide = 2 * heads_wide
    extras = jnp.pad(extras, ((0, 0), (0, 16 * wide - extras.shape[1])))
    extras = extras.reshape(count, 16, wide).astype(BF16)
    back_three = Flow(
        Summing(
            route, lambda j: jnp.concatenate([v_sum[block(j)], out_sum[block(j)]], axis=1), 0
        ),
        Summing(
            route,
            lambda j: jnp.concatenate(
                [jnp.concatenate([q_sum[block(j)], k_sum[block(j)]], axis=1), extras[j]], axis=0
            ),
            1,
        ),
    )
    advance([back_three])
    advance([back_two, back_three])
    advance([back_three])
    near_sum = near[:third].astype(F32) + near_core.astype(F32)
    arriving, near_sum = advance([back_three], arriving, near_sum)
    normed_grad = near_sum + arriving.astype(F32)
    standard_own = (own_inputs - mean_one[:third]) * inverse_one[:third]
    input_part = norm_backward(normed_grad, standard_own, inverse_one[:third], gain_one)
    input_grad = pick_columns((middle_grad + input_part).astype(BF16), back_order)
    input_grad = advance([back_three], input_grad)
    for _ in range(5):
        input_grad = advance([back_three], input_grad)

    v_o = back_three.streams[0].total()
    q_k = back_three.streams[1].total()
    small_sums = q_k[width:].reshape(-1)
    norm_sums = small_sums[: 4 * width].reshape(4, width)
    norm_sums = norm_sums + across_core(norm_sums)
    norm_sums = norm_sums + across_chip(norm_sums)
    norm_sums = lax.dynamic_slice_in_dim(norm_sums, here * norm_part, norm_part, axis=1)
    bias_grad = small_sums[4 * width : 4 * width + bias_size].reshape(qkv_bias.shape)
    grad_down = jnp.concatenate([stream.total() for stream in back_one.streams], axis=0)
    return (
        result,
        input_grad,
        norm_sums[0],
        norm_sums[1],
        q_k[:width, :heads_wide],
        q_k[:width, heads_wide:],
        v_o[:, :heads_wide],
        bias_grad,
        v_o[:, heads_wide:].T,
        norm_sums[2],
        norm_sums[3],
        back_two.streams[0].total(),
        back_two.streams[1].total(),
        grad_down,
    )


def solution(mesh):
    both = P(("dp", "tensor"))
    tokens = P(("dp", "tensor"), None)
    rows = P("dp", "tensor")
    columns = P("tensor", "dp")
    biases = P(None, "tensor", "dp")
    return jax.shard_map(
        functools.partial(on_device, Route(mesh.shape["dp"])),
        mesh=mesh,
        in_specs=(
            tokens,
            tokens,
            P("dp"),
            both,
            both,
            rows,
            rows,
            rows,
            biases,
            columns,
            both,
            both,
            rows,
            rows,
            columns,
        ),
        out_specs=(
            tokens,
            tokens,
            both,
            both,
            rows,
            rows,
            rows,
            biases,
            columns,
            both,
            both,
            rows,
            rows,
            columns,
        ),
        check_vma=False,
    )
```

time: 1520 us -> 787 us (0.52)
  waiting for transfers between devices: 960 us -> 253 us
  starting transfers between devices: 1.06 us -> 101 us
  blocking collectives: 135 us -> 46.1 us
  matrix products: 242 us -> 154 us
  Pallas kernels: 0 us -> 54.7 us
    reduce_scatter x11 -> x0, waiting for transfers between devices: 523 us -> none  [the longest x1 111 us: on_device(): lax.psum_scatter(gate_weight_grad.astype(jnp.bfloat16), 'dp', scatter_dim...]
    all_gather x11 -> x0, waiting for transfers between devices: 432 us -> none  [the longest x1 95.9 us: on_device(): lax.all_gather(w_down, 'dp', axis=1, tiled=True)]
    ppermute x0 -> x110, waiting for transfers between devices: none -> 253 us  [the longest x84 226 us: send(): return lax.ppermute(values, 'dp', self.pairs[direction])]
    unnamed x3 -> x0, blocking collectives: 104 us -> none
    ppermute x0 -> x110, starting transfers between devices: none -> 101 us  [the longest x84 89 us: send(): return lax.ppermute(values, 'dp', self.pairs[direction])]
    dot_general x35 -> x25, matrix products: 242 us -> 154 us  [product(): lax.dot_general(left, right, (((left_dim,), (right_dim,)), ((), ())), pre...]
    pallas_call x0 -> x3, Pallas kernels: none -> 54.7 us  [the longest x1 27.6 us: attend_backward(): pl.pallas_call(functools.partial(backward_body, length // count, count),...]
    dynamic_update_slice x4 -> x0, local copies, waits for them, and re-layouts: 43.3 us -> none  [attend_forward(): lax.scan(one_block, 0, (split_blocks(query_heads, block_rows), split_bloc...]
  transfers between devices with their start and end apart: 22 -> 110, of which waited for: 20 -> 47; matrix products, arithmetic and copies ran while one was open for 22% -> 34% of each run, Pallas kernels for 0% -> 7%
where the time goes in v1:
time: 787 us; the launch traced here: 777 us
  waiting for transfers between devices  253 us (32%)
  matrix products  154 us (20%)
  starting transfers between devices  101 us (13%)
  local copies, waits for them, and re-layouts  88.2 us (11%)
  other arithmetic  66.7 us (8%)
  Pallas kernels  54.7 us (7%)
  blocking collectives  46.1 us (6%)
  between operations  13.9 us (2%)
    ppermute x84, waiting for transfers between devices, send(): return lax.ppermute(values, 'dp', self.pairs[direction])  226 us
    dot_general x25, matrix products, product(): lax.dot_general(left, right, (((left_dim,), (right_dim,)), ((), ())), pre...  154 us
    ppermute x84, starting transfers between devices, send(): return lax.ppermute(values, 'dp', self.pairs[direction])  89 us
    unnamed x372, local copies, waits for them, and re-layouts  48.7 us
    all_gather x1, blocking collectives, on_device(): small = lax.all_gather(packed, ('dp', 'tensor'), axis=0, tiled=True)  46.1 us
    pallas_call x1, Pallas kernels, attend_backward(): pl.pallas_call(functools.partial(backward_body, length // count, count),...  27.6 us
    ppermute x9, waiting for transfers between devices, across_chip(): return lax.ppermute(values, 'tensor', [(i, i ^ 2) for i in range(4)])  26.9 us
    convert_element_type x19, other arithmetic, resume(): values = (values.astype(F32) + own.astype(F32)).astype(BF16)  19.8 us
  transfers between devices with their start and end apart: 110, of which 47 were waited for; matrix products, arithmetic and copies ran while one was open for 34% of the time, Pallas kernels for 7%

profile of v1, /device:TPU:0, one launch (start us, length us, event | category | flops | bytes accessed | tf_op | source)
XLA Modules:
  0.0 777.5 jit_solution(6915550545406697634)
XLA Ops:
  55.3 46.1 %all_gather.3 = bf16[512,128]{1,0:T(8,128)(2,1)S(1)} all-gather(bf16[16,128]{1,0:T(8,128)(2,1)S(1)} %pad_bitcast_fusion), channel_id=1, replica_groups=mesh['dp'=8,'tensor'=4] {'dp','tensor'}, dimensions={0}, use_global_device_ids=true | all-gather | bytes 135168 | tf_op jit(solution)/shard_map/all_gather | solution.py:486
  111.5 16.2 %collective-permute-done.16 = bf16[256,2048]{1,0:T(8,128)(2,1)} collective-permute-done((bf16[256,2048]{1,0:T(8,128)(2,1)}, bf16[256,2048]{1,0:T(8,128)(2,1)}, u32[]{:S(2)}, u32[]{:S(2)}) %collective-permute-start.16) | collective-permute-done | bytes 1048608 | tf_op jit(solution)/shard_map/ppermute | solution.py:420
  138.1 8.1 %collective-permute-done.12 = bf16[256,1024]{1,0:T(8,128)(2,1)S(1)} collective-permute-done((bf16[256,1024]{1,0:T(8,128)(2,1)}, bf16[256,1024]{1,0:T(8,128)(2,1)S(1)}, u32[]{:S(2)}, u32[]{:S(2)}) %collective-permute-start.12) | collective-permute-done | bytes 524320 | tf_op jit(solution)/shard_map/ppermute | solution.py:276
  160.4 12.5 %collective-permute-done.19 = bf16[256,1408]{1,0:T(8,128)(2,1)S(1)} collective-permute-done((bf16[256,1408]{1,0:T(8,128)(2,1)S(1)}, bf16[256,1408]{1,0:T(8,128)(2,1)S(1)}, u32[]{:S(2)}, u32[]{:S(2)}) %collective-permute-start.19) | collective-permute-done | bytes 720928 | tf_op jit(solution)/shard_map/ppermute | solution.py:276
  172.9 17.3 %collective-permute-done.18 = bf16[256,1024]{1,0:T(8,128)(2,1)S(1)} collective-permute-done((bf16[256,1024]{1,0:T(8,128)(2,1)S(1)}, bf16[256,1024]{1,0:T(8,128)(2,1)S(1)}, u32[]{:S(2)}, u32[]{:S(2)}) %collective-permute-start.18) | collective-permute-done | bytes 524320 | tf_op jit(solution)/shard_map/ppermute | solution.py:276
  195.0 10.4 %project_qkv.1 = (bf16[1024,1024]{1,0:T(8,128)(2,1)S(1)}, bf16[1024,512]{1,0:T(8,128)(2,1)S(1)}) custom-call(bf16[1024,2048]{1,0:T(8,128)(2,1)} %fusion.5.x_ref, bf16[2048,1024]{1,0:T(8,128)(2,1)} %copy-done.13, bf16[2048,1024]{1,0:T(8,128)(2,1)} %copy-done.26, f32[1,1536]{1,0:T(1,128)S(1)} %reshape.366.bias_ref, f32[1024,128]{1,0:T(8,128)S(1)} %concatenate.179.cos_ref, ...), custom_call_target="tpu_custom_call" | custom-call | flops 6442450944 | bytes 16777216 | tf_op jit(solution)/shard_map/project_qkv/pallas_call | solution.py:54
  206.5 16.7 %attend_forward.1 = (bf16[1024,512]{1,0:T(8,128)(2,1)S(1)}, f32[4,2,1024]{2,1,0:T(2,128)S(1)}) custom-call(s32[1]{0:T(128)} %bitcast.19.place_ref, bf16[1024,1024]{1,0:T(8,128)(2,1)S(1)} %get-tuple-element.237.q_ref.k_ref, bf16[1024,1024]{1,0:T(8,128)(2,1)S(1)} %get-tuple-element.237.q_ref.k_ref, bf16[1024,512]{1,0:T(8,128)(2,1)S(1)} %get-tuple-element.238.v_ref, ...), custom_call_target="tpu_custom_call" | custom-call | flops 2147483648 | bytes 4194304 | tf_op jit(solution)/shard_map/attend_forward/pallas_call | solution.py:122
  244.1 14.6 %collective-permute-done.30 = bf16[256,1408]{1,0:T(8,128)(2,1)S(1)} collective-permute-done((bf16[256,1408]{1,0:T(8,128)(2,1)S(1)}, bf16[256,1408]{1,0:T(8,128)(2,1)S(1)}, u32[]{:S(2)}, u32[]{:S(2)}) %collective-permute-start.30) | collective-permute-done | bytes 720928 | tf_op jit(solution)/shard_map/ppermute | solution.py:276
  261.8 11.4 %collective-permute-done.26 = bf16[256,1408]{1,0:T(8,128)(2,1)S(1)} collective-permute-done((bf16[256,1408]{1,0:T(8,128)(2,1)S(1)}, bf16[256,1408]{1,0:T(8,128)(2,1)S(1)}, u32[]{:S(2)}, u32[]{:S(2)}) %collective-permute-start.26) | collective-permute-done | bytes 720928 | tf_op jit(solution)/shard_map/ppermute | solution.py:276
  282.2 15.5 %collective-permute-done.37 = bf16[256,1408]{1,0:T(8,128)(2,1)S(1)} collective-permute-done((bf16[256,1408]{1,0:T(8,128)(2,1)S(1)}, bf16[256,1408]{1,0:T(8,128)(2,1)S(1)}, u32[]{:S(2)}, u32[]{:S(2)}) %collective-permute-start.37) | collective-permute-done | bytes 720928 | tf_op jit(solution)/shard_map/ppermute | solution.py:276
  301.5 11.7 %collective-permute-done.33 = bf16[256,1408]{1,0:T(8,128)(2,1)S(1)} collective-permute-done((bf16[256,1408]{1,0:T(8,128)(2,1)S(1)}, bf16[256,1408]{1,0:T(8,128)(2,1)S(1)}, u32[]{:S(2)}, u32[]{:S(2)}) %collective-permute-start.33) | collective-permute-done | bytes 720928 | tf_op jit(solution)/shard_map/ppermute | solution.py:276
  337.2 8.4 %fusion.80 = f32[1024,1408]{1,0:T(8,128)} fusion(bf16[1024,2048]{1,0:T(8,128)(2,1)S(1)} %pad_maximum_fusion.3, bf16[2048,1408]{1,0:T(8,128)(2,1)S(1)} %constant_dynamic-update-slice_fusion.64), kind=kOutput, calls=%fused_computation.376 | convolution fusion | flops 5905580032 | bytes 15728640 | tf_op jit(solution)/shard_map/dot_general | solution.py:21
  349.5 12.1 %multiply_convert_fusion.2 = (bf16[1024,1408]{1,0:T(8,128)(2,1)S(1)}, f32[1024,1408]{1,0:T(8,128)}) fusion(f32[1024,1408]{1,0:T(8,128)} %fusion.80, bf16[1024,2048]{1,0:T(8,128)(2,1)S(1)} %pad_maximum_fusion.3, bf16[2048,1408]{1,0:T(8,128)(2,1)} %constant_dynamic-update-slice_fusion.72), kind=kOutput, calls=%fused_computation.16 | convolution fusion | flops 5914230784 | bytes 24379392 | tf_op jit(solution)/shard_map/dot_general | solution.py:21
  363.7 6.5 convolution_convert_fusion.2
  384.7 17.7 %multiply_convert_fusion = (bf16[1024,1408]{1,0:T(8,128)(2,1)}, bf16[1024,1408]{1,0:T(8,128)(2,1)}) fusion(f32[1024,1408]{1,0:T(8,128)} %fusion.80, f32[1024,1408]{1,0:T(8,128)} %get-tuple-element.288, bf16[1024,2048]{1,0:T(8,128)(2,1)} %pad_maximum_fusion.2, bf16[704,2048]{1,0:T(8,128)(2,1)} %copy-done.112, ...), kind=kOutput, calls=%fused_computation.14 | convolution fusion | flops 5934415872 | bytes 27262976 | tf_op jit(solution)/shard_map/dot_general | solution.py:21
  402.4 8.7 %fusion.29 = f32[512,2048]{1,0:T(8,128)} fusion(bf16[2048,1408]{1,0:T(8,128)(2,1)} %constant_dynamic-update-slice_fusion.72, bf16[1024,1408]{1,0:T(8,128)(2,1)} %get-tuple-element.292), kind=kOutput, calls=%fused_computation.92 | convolution fusion | flops 2952790016 | bytes 11403264 | tf_op jit(solution)/shard_map/dot_general | solution.py:21
  411.1 7.8 %fusion.32 = f32[512,2048]{1,0:T(8,128)} fusion(bf16[2048,1408]{1,0:T(8,128)(2,1)} %constant_dynamic-update-slice_fusion.72, bf16[1024,1408]{1,0:T(8,128)(2,1)S(1)} %copy-done.130), kind=kOutput, calls=%fused_computation.95 | convolution fusion | flops 2952790016 | bytes 11403264 | tf_op jit(solution)/shard_map/dot_general | solution.py:21
  418.9 7.0 convolution_convert_fusion.1
  428.0 7.2 convolution_convert_fusion
  435.3 9.8 %add_convert_fusion = bf16[512,2048]{1,0:T(8,128)(2,1)S(1)} fusion(f32[512,2048]{1,0:T(8,128)} %fusion.29, bf16[2048,1408]{1,0:T(8,128)(2,1)} %copy-done.109, bf16[1024,1408]{1,0:T(8,128)(2,1)} %get-tuple-element.291), kind=kOutput, calls=%fused_computation.26 | convolution fusion | flops 2954887168 | bytes 13500416 | tf_op jit(solution)/shard_map/dot_general | solution.py:21
  445.1 9.2 %add_convert_fusion.1 = bf16[512,2048]{1,0:T(8,128)(2,1)} fusion(f32[512,2048]{1,0:T(8,128)} %fusion.32, bf16[2048,1408]{1,0:T(8,128)(2,1)} %copy-done.109, bf16[1024,1408]{1,0:T(8,128)(2,1)} %get-tuple-element.291), kind=kOutput, calls=%fused_computation.27 | convolution fusion | flops 2954887168 | bytes 13500416 | tf_op jit(solution)/shard_map/dot_general | solution.py:21
  456.1 6.7 convolution_convert_fusion.10
  468.6 6.5 convolution_convert_fusion.9
  479.6 5.7 collective-permute-done.56
  492.6 5.7 collective-permute-done.74
  536.8 22.1 %collective-permute-done.67 = bf16[256,1408]{1,0:T(8,128)(2,1)S(1)} collective-permute-done((bf16[256,1408]{1,0:T(8,128)(2,1)S(1)}, bf16[256,1408]{1,0:T(8,128)(2,1)S(1)}, u32[]{:S(2)}, u32[]{:S(2)}) %collective-permute-start.67) | collective-permute-done | bytes 720928 | tf_op jit(solution)/shard_map/ppermute | solution.py:276
  571.1 8.0 %collective-permute-done.70 = bf16[256,1408]{1,0:T(8,128)(2,1)S(1)} collective-permute-done((bf16[256,1408]{1,0:T(8,128)(2,1)S(1)}, bf16[256,1408]{1,0:T(8,128)(2,1)S(1)}, u32[]{:S(2)}, u32[]{:S(2)}) %collective-permute-start.70) | collective-permute-done | bytes 720928 | tf_op jit(solution)/shard_map/ppermute | solution.py:276
  589.0 27.6 %attend_backward.1 = (bf16[1024,512]{1,0:T(8,128)(2,1)S(1)}, bf16[1024,512]{1,0:T(8,128)(2,1)S(1)}, bf16[1024,512]{1,0:T(8,128)(2,1)S(1)}, f32[4,3,128]{2,1,0:T(4,128)S(1)}) custom-call(s32[1]{0:T(128)} %bitcast.19.place_ref, bf16[1024,1024]{1,0:T(8,128)(2,1)} %copy-done.6, bf16[1024,1024]{1,0:T(8,128)(2,1)} %copy-done.6, bf16[1024,512]{1,0:T(8,128)(2,1)S(1)} %copy-done.8, ...), custom_call_target="tpu_custom_call" | custom-call | flops 5368709120 | bytes 10485760 | tf_op jit(solution)/shard_map/attend_backward/pallas_call | solution.py:228
  616.7 6.1 convolution_convert_fusion.6
  653.5 8.2 %multiply_reduce_fusion = (f32[2048]{0:T(1024)S(1)}, f32[2048]{0:T(1024)S(1)}, f32[2048]{0:T(1024)S(1)}, f32[2048]{0:T(1024)S(1)}, bf16[512,2048]{1,0:T(8,128)(2,1)S(1)}) fusion(f32[512]{0:T(512)S(1)} %bitcast.144, f32[512]{0:T(512)S(1)} %bitcast.146, bf16[1024,2048]{1,0:T(8,128)(2,1)} %copy-done.11, f32[512,2048]{1,0:T(8,128)} %get-tuple-element.347, ...), kind=kOutput, calls=%fused_computation.22 | convolution fusion | flops 1089462272 | bytes 21536768 | tf_op jit(solution)/shard_map/dot_general | solution.py:21
  672.6 7.0 collective-permute-done.98
  745.6 8.2 %collective-permute-done.102 = bf16[272,1024]{1,0:T(8,128)(2,1)S(1)} collective-permute-done((bf16[272,1024]{1,0:T(8,128)(2,1)S(1)}, bf16[272,1024]{1,0:T(8,128)(2,1)S(1)}, u32[]{:S(2)}, u32[]{:S(2)}) %collective-permute-start.102) | collective-permute-done | bytes 557088 | tf_op jit(solution)/shard_map/ppermute | solution.py:276
  (758 shorter events, 376.8 us)
Async XLA Ops:
  3.6 35.0 %collective-permute-start = (bf16[256,1024]{1,0:T(8,128)(2,1)}, bf16[256,1024]{1,0:T(8,128)(2,1)}, u32[]{:S(2)}, u32[]{:S(2)}) collective-permute-start(bf16[256,1024]{1,0:T(8,128)(2,1)} %pad_maximum_fusion.10), channel_id=1, source_target_pairs={{0,8},{8,16},{16,24},{24,28},{28,20},{20,12},{12,4},{4,0},{1,9},{9... | collective-permute-start | bytes 1572872 | tf_op jit(solution)/shard_map/ppermute | solution.py:276
  6.7 37.8 %collective-permute-start.1 = (bf16[256,1024]{1,0:T(8,128)(2,1)}, bf16[256,1024]{1,0:T(8,128)(2,1)}, u32[]{:S(2)}, u32[]{:S(2)}) collective-permute-start(bf16[256,1024]{1,0:T(8,128)(2,1)} %pad_maximum_fusion.10), channel_id=1, source_target_pairs={{8,0},{16,8},{24,16},{28,24},{20,28},{12,20},{4,12},{0,4},{9,1},{1... | collective-permute-start | bytes 1572872 | tf_op jit(solution)/shard_map/ppermute | solution.py:276
  48.0 56.6 %collective-permute-start.10 = (bf16[256,2048]{1,0:T(8,128)(2,1)}, bf16[256,2048]{1,0:T(8,128)(2,1)}, u32[]{:S(2)}, u32[]{:S(2)}) collective-permute-start(bf16[256,2048]{1,0:T(8,128)(2,1)} %collective-permute-done.2), channel_id=1, source_target_pairs={{0,1},{1,0},{2,3},{3,2},{4,5},{5,4},{6,7},{7,6},{8,9},{9,8},{10,11... | collective-permute-start | bytes 3145736 | tf_op jit(solution)/shard_map/ppermute | solution.py:416
  48.0 56.6 %collective-permute-start.11 = (bf16[256,2048]{1,0:T(8,128)(2,1)}, bf16[256,2048]{1,0:T(8,128)(2,1)}, u32[]{:S(2)}, u32[]{:S(2)}) collective-permute-start(bf16[256,2048]{1,0:T(8,128)(2,1)} %copy-done.28), channel_id=1, source_target_pairs={{0,1},{1,0},{2,3},{3,2},{4,5},{5,4},{6,7},{7,6},{8,9},{9,8},{10,11... | collective-permute-start | bytes 3145736 | tf_op jit(solution)/shard_map/ppermute | solution.py:416
  53.1 49.5 %collective-permute-start.8 = (bf16[256,1024]{1,0:T(8,128)(2,1)}, bf16[256,1024]{1,0:T(8,128)(2,1)S(1)}, u32[]{:S(2)}, u32[]{:S(2)}) collective-permute-start(bf16[256,1024]{1,0:T(8,128)(2,1)} %collective-permute-done.5), channel_id=1, source_target_pairs={{0,8},{8,16},{16,24},{24,28},{28,20},{20,12},{12,4},{4,0},{1,9},{9... | collective-permute-start | bytes 1572872 | tf_op jit(solution)/shard_map/ppermute | solution.py:276
  54.8 47.8 %collective-permute-start.9 = (bf16[256,1024]{1,0:T(8,128)(2,1)}, bf16[256,1024]{1,0:T(8,128)(2,1)}, u32[]{:S(2)}, u32[]{:S(2)}) collective-permute-start(bf16[256,1024]{1,0:T(8,128)(2,1)} %collective-permute-done.6), channel_id=1, source_target_pairs={{8,0},{16,8},{24,16},{28,24},{20,28},{12,20},{4,12},{0,4},{9,1},{1... | collective-permute-start | bytes 1572872 | tf_op jit(solution)/shard_map/ppermute | solution.py:276
  102.6 28.6 %collective-permute-start.3 = (bf16[256,1024]{1,0:T(8,128)(2,1)}, bf16[256,1024]{1,0:T(8,128)(2,1)}, u32[]{:S(2)}, u32[]{:S(2)}) collective-permute-start(bf16[256,1024]{1,0:T(8,128)(2,1)} %collective-permute-done), channel_id=1, source_target_pairs={{0,8},{8,16},{16,24},{24,28},{28,20},{20,12},{12,4},{4,0},{1,9},{9... | collective-permute-start | bytes 1572872 | tf_op jit(solution)/shard_map/ppermute | solution.py:276
  102.6 28.6 %collective-permute-start.4 = (bf16[256,1024]{1,0:T(8,128)(2,1)}, bf16[256,1024]{1,0:T(8,128)(2,1)}, u32[]{:S(2)}, u32[]{:S(2)}) collective-permute-start(bf16[256,1024]{1,0:T(8,128)(2,1)} %collective-permute-done.1), channel_id=1, source_target_pairs={{8,0},{16,8},{24,16},{28,24},{20,28},{12,20},{4,12},{0,4},{9,1},{1... | collective-permute-start | bytes 1572872 | tf_op jit(solution)/shard_map/ppermute | solution.py:276
  137.9 35.0 %collective-permute-start.19 = (bf16[256,1408]{1,0:T(8,128)(2,1)S(1)}, bf16[256,1408]{1,0:T(8,128)(2,1)S(1)}, u32[]{:S(2)}, u32[]{:S(2)}) collective-permute-start(bf16[256,1408]{1,0:T(8,128)(2,1)S(1)} %copy-done.70), channel_id=1, source_target_pairs={{0,8},{8,16},{16,24},{24,28},{28,20},{20,12},{12,4},{4,0},{1,9},{9... | collective-permute-start | bytes 2162696 | tf_op jit(solution)/shard_map/ppermute | solution.py:276
  147.9 57.6 %collective-permute-start.23 = (bf16[256,1408]{1,0:T(8,128)(2,1)S(1)}, bf16[256,1408]{1,0:T(8,128)(2,1)S(1)}, u32[]{:S(2)}, u32[]{:S(2)}) collective-permute-start(bf16[256,1408]{1,0:T(8,128)(2,1)S(1)} %copy-done.72), channel_id=1, source_target_pairs={{0,8},{8,16},{16,24},{24,28},{28,20},{20,12},{12,4},{4,0},{1,9},{9... | collective-permute-start | bytes 2162696 | tf_op jit(solution)/shard_map/ppermute | solution.py:276
  148.3 57.2 %collective-permute-start.24 = (bf16[256,1408]{1,0:T(8,128)(2,1)S(1)}, bf16[256,1408]{1,0:T(8,128)(2,1)S(1)}, u32[]{:S(2)}, u32[]{:S(2)}) collective-permute-start(bf16[256,1408]{1,0:T(8,128)(2,1)S(1)} %copy-done.72), channel_id=1, source_target_pairs={{8,0},{16,8},{24,16},{28,24},{20,28},{12,20},{4,12},{0,4},{9,1},{1... | collective-permute-start | bytes 2162696 | tf_op jit(solution)/shard_map/ppermute | solution.py:276
  157.5 32.8 %collective-permute-start.18 = (bf16[256,1024]{1,0:T(8,128)(2,1)S(1)}, bf16[256,1024]{1,0:T(8,128)(2,1)S(1)}, u32[]{:S(2)}, u32[]{:S(2)}) collective-permute-start(bf16[256,1024]{1,0:T(8,128)(2,1)S(1)} %collective-permute-done.13), channel_id=1, source_target_pairs={{8,0},{16,8},{24,16},{28,24},{20,28},{12,20},{4,12},{0,4},{9,1},{1... | collective-permute-start | bytes 1572872 | tf_op jit(solution)/shard_map/ppermute | solution.py:276
  192.8 30.4 %collective-permute-start.21 = (bf16[256,1408]{1,0:T(8,128)(2,1)S(1)}, bf16[256,1408]{1,0:T(8,128)(2,1)S(1)}, u32[]{:S(2)}, u32[]{:S(2)}) collective-permute-start(bf16[256,1408]{1,0:T(8,128)(2,1)S(1)} %collective-permute-done.19), channel_id=1, source_target_pairs={{0,8},{8,16},{16,24},{24,28},{28,20},{20,12},{12,4},{4,0},{1,9},{9... | collective-permute-start | bytes 2162696 | tf_op jit(solution)/shard_map/ppermute | solution.py:276
  193.2 30.0 %collective-permute-start.22 = (bf16[256,1408]{1,0:T(8,128)(2,1)S(1)}, bf16[256,1408]{1,0:T(8,128)(2,1)S(1)}, u32[]{:S(2)}, u32[]{:S(2)}) collective-permute-start(bf16[256,1408]{1,0:T(8,128)(2,1)S(1)} %collective-permute-done.20), channel_id=1, source_target_pairs={{8,0},{16,8},{24,16},{28,24},{20,28},{12,20},{4,12},{0,4},{9,1},{1... | collective-permute-start | bytes 2162696 | tf_op jit(solution)/shard_map/ppermute | solution.py:276
  242.1 32.8 %collective-permute-start.29 = (bf16[256,2048]{1,0:T(8,128)(2,1)S(1)}, bf16[256,2048]{1,0:T(8,128)(2,1)S(1)}, u32[]{:S(2)}, u32[]{:S(2)}) collective-permute-start(bf16[256,2048]{1,0:T(8,128)(2,1)S(1)} %add_convert_fusion.7), channel_id=1, source_target_pairs={{0,2},{1,3},{2,0},{3,1},{4,6},{5,7},{6,4},{7,5},{8,10},{9,11},{10,... | collective-permute-start | bytes 3145736 | tf_op jit(solution)/shard_map/ppermute | solution.py:420
  243.7 29.4 %collective-permute-start.26 = (bf16[256,1408]{1,0:T(8,128)(2,1)S(1)}, bf16[256,1408]{1,0:T(8,128)(2,1)S(1)}, u32[]{:S(2)}, u32[]{:S(2)}) collective-permute-start(bf16[256,1408]{1,0:T(8,128)(2,1)S(1)} %copy-done.79), channel_id=1, source_target_pairs={{0,8},{8,16},{16,24},{24,28},{28,20},{20,12},{12,4},{4,0},{1,9},{9... | collective-permute-start | bytes 2162696 | tf_op jit(solution)/shard_map/ppermute | solution.py:276
  276.2 37.0 %collective-permute-start.34 = (bf16[256,2048]{1,0:T(8,128)(2,1)S(1)}, bf16[256,2048]{1,0:T(8,128)(2,1)S(1)}, u32[]{:S(2)}, u32[]{:S(2)}) collective-permute-start(bf16[256,2048]{1,0:T(8,128)(2,1)S(1)} %get-tuple-element.257), channel_id=1, source_target_pairs={{0,2},{1,3},{2,0},{3,1},{4,6},{5,7},{6,4},{7,5},{8,10},{9,11},{10,... | collective-permute-start | bytes 3145736 | tf_op jit(solution)/shard_map/ppermute | solution.py:420
  280.8 32.4 %collective-permute-start.33 = (bf16[256,1408]{1,0:T(8,128)(2,1)S(1)}, bf16[256,1408]{1,0:T(8,128)(2,1)S(1)}, u32[]{:S(2)}, u32[]{:S(2)}) collective-permute-start(bf16[256,1408]{1,0:T(8,128)(2,1)S(1)} %collective-permute-done.26), channel_id=1, source_target_pairs={{0,8},{8,16},{16,24},{24,28},{28,20},{20,12},{12,4},{4,0},{1,9},{9... | collective-permute-start | bytes 2162696 | tf_op jit(solution)/shard_map/ppermute | solution.py:276
  425.9 28.4 %collective-permute-start.61 = (bf16[704,256]{1,0:T(8,128)(2,1)}, bf16[704,256]{1,0:T(8,128)(2,1)S(1)}, u32[]{:S(2)}, u32[]{:S(2)}) collective-permute-start(bf16[704,256]{1,0:T(8,128)(2,1)} %get-tuple-element.297), channel_id=1, source_target_pairs={{0,8},{8,16},{16,24},{24,28},{28,20},{20,12},{12,4},{4,0},{1,9},{9... | collective-permute-start | bytes 1081352 | tf_op jit(solution)/shard_map/ppermute | solution.py:276
  478.9 28.4 %collective-permute-start.64 = (bf16[256,2048]{1,0:T(8,128)(2,1)S(1)}, bf16[256,2048]{1,0:T(8,128)(2,1)S(1)}, u32[]{:S(2)}, u32[]{:S(2)}) collective-permute-start(bf16[256,2048]{1,0:T(8,128)(2,1)S(1)} %add_convert_fusion.5), channel_id=1, source_target_pairs={{0,2},{1,3},{2,0},{3,1},{4,6},{5,7},{6,4},{7,5},{8,10},{9,11},{10,... | collective-permute-start | bytes 3145736 | tf_op jit(solution)/shard_map/ppermute | solution.py:420
  528.0 33.3 %collective-permute-start.79 = (bf16[256,1408]{1,0:T(8,128)(2,1)S(1)}, bf16[256,1408]{1,0:T(8,128)(2,1)S(1)}, u32[]{:S(2)}, u32[]{:S(2)}) collective-permute-start(bf16[256,1408]{1,0:T(8,128)(2,1)S(1)} %get-tuple-element.487), channel_id=1, source_target_pairs={{0,8},{8,16},{16,24},{24,28},{28,20},{20,12},{12,4},{4,0},{1,9},{9... | collective-permute-start | bytes 2162696 | tf_op jit(solution)/shard_map/ppermute | solution.py:276
  529.7 29.9 %collective-permute-start.87 = (bf16[256,2048]{1,0:T(8,128)(2,1)S(1)}, bf16[256,2048]{1,0:T(8,128)(2,1)S(1)}, u32[]{:S(2)}, u32[]{:S(2)}) collective-permute-start(bf16[256,2048]{1,0:T(8,128)(2,1)S(1)} %slice.587), channel_id=1, source_target_pairs={{0,1},{1,0},{2,3},{3,2},{4,5},{5,4},{6,7},{7,6},{8,9},{9,8},{10,11... | collective-permute-start | bytes 3145736 | tf_op jit(solution)/shard_map/ppermute | solution.py:416
  529.8 29.1 %collective-permute-start.67 = (bf16[256,1408]{1,0:T(8,128)(2,1)S(1)}, bf16[256,1408]{1,0:T(8,128)(2,1)S(1)}, u32[]{:S(2)}, u32[]{:S(2)}) collective-permute-start(bf16[256,1408]{1,0:T(8,128)(2,1)S(1)} %get-tuple-element.306), channel_id=1, source_target_pairs={{0,8},{8,16},{16,24},{24,28},{28,20},{20,12},{12,4},{4,0},{1,9},{9... | collective-permute-start | bytes 2162696 | tf_op jit(solution)/shard_map/ppermute | solution.py:276
  536.1 29.2 %collective-permute-start.80 = (bf16[256,1408]{1,0:T(8,128)(2,1)S(1)}, bf16[256,1408]{1,0:T(8,128)(2,1)S(1)}, u32[]{:S(2)}, u32[]{:S(2)}) collective-permute-start(bf16[256,1408]{1,0:T(8,128)(2,1)S(1)} %get-tuple-element.486), channel_id=1, source_target_pairs={{8,0},{16,8},{24,16},{28,24},{20,28},{12,20},{4,12},{0,4},{9,1},{1... | collective-permute-start | bytes 2162696 | tf_op jit(solution)/shard_map/ppermute | solution.py:276
  560.0 62.8 %collective-permute-start.88 = (bf16[256,2048]{1,0:T(8,128)(2,1)S(1)}, bf16[256,2048]{1,0:T(8,128)(2,1)S(1)}, u32[]{:S(2)}, u32[]{:S(2)}) collective-permute-start(bf16[256,2048]{1,0:T(8,128)(2,1)S(1)} %add_convert_fusion.4), channel_id=1, source_target_pairs={{0,2},{1,3},{2,0},{3,1},{4,6},{5,7},{6,4},{7,5},{8,10},{9,11},{10,... | collective-permute-start | bytes 3145736 | tf_op jit(solution)/shard_map/ppermute | solution.py:420
  584.5 61.6 %collective-permute-start.83 = (bf16[256,1408]{1,0:T(8,128)(2,1)}, bf16[256,1408]{1,0:T(8,128)(2,1)S(1)}, u32[]{:S(2)}, u32[]{:S(2)}) collective-permute-start(bf16[256,1408]{1,0:T(8,128)(2,1)} %get-tuple-element.485), channel_id=1, source_target_pairs={{0,8},{8,16},{16,24},{24,28},{28,20},{20,12},{12,4},{4,0},{1,9},{9... | collective-permute-start | bytes 2162696 | tf_op jit(solution)/shard_map/ppermute | solution.py:276
  586.2 60.0 %collective-permute-start.84 = (bf16[256,1408]{1,0:T(8,128)(2,1)}, bf16[256,1408]{1,0:T(8,128)(2,1)}, u32[]{:S(2)}, u32[]{:S(2)}) collective-permute-start(bf16[256,1408]{1,0:T(8,128)(2,1)} %get-tuple-element.484), channel_id=1, source_target_pairs={{8,0},{16,8},{24,16},{28,24},{20,28},{12,20},{4,12},{0,4},{9,1},{1... | collective-permute-start | bytes 2162696 | tf_op jit(solution)/shard_map/ppermute | solution.py:276
  587.0 35.8 %collective-permute-start.85 = (bf16[256,1408]{1,0:T(8,128)(2,1)S(1)}, bf16[256,1408]{1,0:T(8,128)(2,1)S(1)}, u32[]{:S(2)}, u32[]{:S(2)}) collective-permute-start(bf16[256,1408]{1,0:T(8,128)(2,1)S(1)} %get-tuple-element.483), channel_id=1, source_target_pairs={{0,8},{8,16},{16,24},{24,28},{28,20},{20,12},{12,4},{4,0},{1,9},{9... | collective-permute-start | bytes 2162696 | tf_op jit(solution)/shard_map/ppermute | solution.py:276
  588.7 34.2 %collective-permute-start.86 = (bf16[256,1408]{1,0:T(8,128)(2,1)S(1)}, bf16[256,1408]{1,0:T(8,128)(2,1)S(1)}, u32[]{:S(2)}, u32[]{:S(2)}) collective-permute-start(bf16[256,1408]{1,0:T(8,128)(2,1)S(1)} %get-tuple-element.482), channel_id=1, source_target_pairs={{8,0},{16,8},{24,16},{28,24},{20,28},{12,20},{4,12},{0,4},{9,1},{1... | collective-permute-start | bytes 2162696 | tf_op jit(solution)/shard_map/ppermute | solution.py:276
  648.8 44.1 %collective-permute-start.89 = (bf16[256,1408]{1,0:T(8,128)(2,1)}, bf16[256,1408]{1,0:T(8,128)(2,1)}, u32[]{:S(2)}, u32[]{:S(2)}) collective-permute-start(bf16[256,1408]{1,0:T(8,128)(2,1)} %add_convert_fusion.9), channel_id=1, source_target_pairs={{8,0},{16,8},{24,16},{28,24},{20,28},{12,20},{4,12},{0,4},{9,1},{1... | collective-permute-start | bytes 2162696 | tf_op jit(solution)/shard_map/ppermute | solution.py:276
  651.7 30.9 %collective-permute-start.90 = (bf16[256,1408]{1,0:T(8,128)(2,1)S(1)}, bf16[256,1408]{1,0:T(8,128)(2,1)S(1)}, u32[]{:S(2)}, u32[]{:S(2)}) collective-permute-start(bf16[256,1408]{1,0:T(8,128)(2,1)S(1)} %add_convert_fusion.8), channel_id=1, source_target_pairs={{0,8},{8,16},{16,24},{24,28},{28,20},{20,12},{12,4},{4,0},{1,9},{9... | collective-permute-start | bytes 2162696 | tf_op jit(solution)/shard_map/ppermute | solution.py:276
  682.0 38.9 %collective-permute-start.100 = (bf16[256,1024]{1,0:T(8,128)(2,1)}, bf16[256,1024]{1,0:T(8,128)(2,1)}, u32[]{:S(2)}, u32[]{:S(2)}) collective-permute-start(bf16[256,1024]{1,0:T(8,128)(2,1)} %add_convert_fusion.27), channel_id=1, source_target_pairs={{0,8},{8,16},{16,24},{24,28},{28,20},{20,12},{12,4},{4,0},{1,9},{9... | collective-permute-start | bytes 1572872 | tf_op jit(solution)/shard_map/ppermute | solution.py:276
  (212 other events, 3533.5 us)

commit v2 on v1

v2 whole, which is shorter than its diff:
```python
import functools

import jax
import jax.experimental.pallas as pl
import jax.experimental.pallas.tpu as pltpu
import jax.numpy as jnp
from jax import lax
from jax.sharding import PartitionSpec as P

HD = 64
ROT = 16
PAIR = 2 * HD
EPSILON = 1e-05
NEGATIVE = -1e30
F32 = jnp.float32
BF16 = jnp.bfloat16
MIB = 2**20
LIGHT = pl.CostEstimate(flops=10**9, bytes_accessed=1, transcendentals=1)
LONG = pl.CostEstimate(flops=5 * 10**10, bytes_accessed=1, transcendentals=1)


def product(left, right, left_dim, right_dim):
    return lax.dot_general(
        left, right, (((left_dim,), (right_dim,)), ((), ())), preferred_element_type=F32
    )


def turn(columns, cos_values, sin_values, opening):
    partner = jnp.where(opening, pltpu.roll(columns, PAIR - 8, 1), pltpu.roll(columns, 8, 1))
    return columns * cos_values + partner * sin_values


def opening_lanes(rows):
    return lax.broadcasted_iota(jnp.int32, (rows, PAIR), 1) % HD < 8


def forward_body(block, count, q_ref, k_ref, v_ref, down_ref, across_ref, mixed_ref, lse_ref):
    lane = lax.broadcasted_iota(jnp.int32, (block, PAIR), 1)
    earlier = lax.broadcasted_iota(jnp.int32, (block, block), 0) <= lax.broadcasted_iota(
        jnp.int32, (block, block), 1
    )
    spans = [pl.ds(i * block, block) for i in range(count)]
    for i in range(count):
        queries = q_ref[spans[i], :] * jnp.asarray(HD**-0.5, BF16)
        segment = across_ref[:, spans[i]]
        kept = [down_ref[spans[j], :] == segment for j in range(i + 1)]
        kept[i] = kept[i] & earlier
        sums = []
        for half in range(2):
            mine = lane < HD if half == 0 else lane >= HD
            chosen = jnp.where(mine, queries, jnp.zeros_like(queries))
            scores = [
                jnp.where(kept[j], product(k_ref[spans[j], :], chosen, 1, 1), NEGATIVE)
                for j in range(i + 1)
            ]
            top = scores[0].max(0, keepdims=True)
            for part in scores[1:]:
                top = jnp.maximum(top, part.max(0, keepdims=True))
            raised = [jnp.exp(part - top) for part in scores]
            total = raised[0].sum(0, keepdims=True)
            for part in raised[1:]:
                total = total + part.sum(0, keepdims=True)
            inverse = 1.0 / total
            out = None
            for j in range(i + 1):
                term = product((raised[j] * inverse).astype(BF16), v_ref[spans[j], :], 0, 0)
                out = term if out is None else out + term
            sums.append(out)
            lse_ref[0, half : half + 1, spans[i]] = top + jnp.log(total)
        mixed_ref[spans[i], :] = jnp.where(lane < HD, sums[0], sums[1]).astype(BF16)


def attend_forward(qk, values, segment_down, segment_across, count):
    length, width = values.shape
    pairs = width // PAIR
    columns = lambda first: pl.BlockSpec((length, PAIR), lambda h: (0, h + first))
    whole = lambda shape: pl.BlockSpec(shape, lambda h: (0, 0))
    return pl.pallas_call(
        functools.partial(forward_body, length // count, count),
        grid_spec=pltpu.PrefetchScalarGridSpec(
            num_scalar_prefetch=0,
            grid=(pairs,),
            in_specs=[columns(0), columns(pairs), columns(0), whole((length, 1)), whole((1, length))],
            out_specs=[columns(0), pl.BlockSpec((1, 2, length), lambda h: (h, 0, 0))],
        ),
        out_shape=[
            jax.ShapeDtypeStruct((length, width), BF16),
            jax.ShapeDtypeStruct((pairs, 2, length), F32),
        ],
        compiler_params=pltpu.CompilerParams(vmem_limit_bytes=60 * MIB),
        cost_estimate=LIGHT,
        name="attend_forward",
    )(qk, qk, values, segment_down, segment_across)


def backward_body(
    block,
    count,
    q_ref,
    k_ref,
    v_ref,
    mixed_ref,
    grad_ref,
    lse_ref,
    down_ref,
    across_ref,
    cos_ref,
    sin_ref,
    q_grad_ref,
    k_grad_ref,
    v_grad_ref,
    bias_ref,
    q_total,
    k_total,
    v_total,
):
    lane = lax.broadcasted_iota(jnp.int32, (block, PAIR), 1)
    earlier = lax.broadcasted_iota(jnp.int32, (block, block), 0) <= lax.broadcasted_iota(
        jnp.int32, (block, block), 1
    )
    spans = [pl.ds(i * block, block) for i in range(count)]
    for i in range(count):
        queries = q_ref[spans[i], :] * jnp.asarray(HD**-0.5, BF16)
        upstream = grad_ref[spans[i], :]
        centres = (upstream.astype(F32) * mixed_ref[spans[i], :].astype(F32)).T
        segment = across_ref[:, spans[i]]
        kept = [down_ref[spans[j], :] == segment for j in range(i + 1)]
        kept[i] = kept[i] & earlier
        sums = []
        for half in range(2):
            mine = lane < HD if half == 0 else lane >= HD
            nothing = jnp.zeros_like(queries)
            chosen = jnp.where(mine, queries, nothing)
            chosen_grad = jnp.where(mine, upstream, nothing)
            log_total = lse_ref[0, half : half + 1, spans[i]]
            centre = centres[half * HD : (half + 1) * HD, :].sum(0, keepdims=True)
            q_sum = None
            for j in range(i + 1):
                keys = k_ref[spans[j], :]
                scores = jnp.where(kept[j], product(keys, chosen, 1, 1), NEGATIVE)
                weights = jnp.exp(scores - log_total)
                weight_grad = product(v_ref[spans[j], :], chosen_grad, 1, 1)
                score_grad = (weights * (weight_grad - centre)).astype(BF16)
                v_term = product(weights.astype(BF16), chosen_grad, 1, 0)
                k_term = product(score_grad, chosen, 1, 0)
                term = product(score_grad, keys, 0, 0)
                q_sum = term if q_sum is None else q_sum + term
                if i == j and half == 0:
                    v_total[spans[j], :] = v_term
                    k_total[spans[j], :] = k_term
                else:
                    v_total[spans[j], :] += v_term
                    k_total[spans[j], :] += k_term
            sums.append(q_sum)
        q_total[spans[i], :] = jnp.where(lane < HD, sums[0], sums[1])
    opening = opening_lanes(block * count)
    cos_values = cos_ref[...]
    sin_values = -sin_ref[...]
    q_grad = turn(q_total[...] * (HD**-0.5), cos_values, sin_values, opening).astype(BF16)
    k_grad = turn(k_total[...], cos_values, sin_values, opening).astype(BF16)
    v_grad = v_total[...].astype(BF16)
    for at, (ref, grad) in enumerate(
        ((q_grad_ref, q_grad), (k_grad_ref, k_grad), (v_grad_ref, v_grad))
    ):
        ref[...] = grad
        bias_ref[0, at : at + 1, :] = grad.astype(F32).sum(0, keepdims=True)


def attend_backward(
    qk, values, mixed, mixed_grad, lse, segment_down, segment_across, cos_table, sin_table, count
):
    length, width = values.shape
    pairs = width // PAIR
    columns = lambda first: pl.BlockSpec((length, PAIR), lambda h: (0, h + first))
    whole = lambda shape: pl.BlockSpec(shape, lambda h: (0, 0))
    return pl.pallas_call(
        functools.partial(backward_body, length // count, count),
        grid_spec=pltpu.PrefetchScalarGridSpec(
            num_scalar_prefetch=0,
            grid=(pairs,),
            in_specs=[
                columns(0),
                columns(pairs),
                columns(0),
                columns(0),
                columns(0),
                pl.BlockSpec((1, 2, length), lambda h: (h, 0, 0)),
                whole((length, 1)),
                whole((1, length)),
                whole((length, PAIR)),
                whole((length, PAIR)),
            ],
            out_specs=[
                columns(0),
                columns(0),
                columns(0),
                pl.BlockSpec((1, 3, PAIR), lambda h: (h, 0, 0)),
            ],
            scratch_shapes=[pltpu.VMEM((length, PAIR), F32)] * 3,
        ),
        out_shape=[jax.ShapeDtypeStruct((length, width), BF16)] * 3
        + [jax.ShapeDtypeStruct((pairs, 3, PAIR), F32)],
        compiler_params=pltpu.CompilerParams(vmem_limit_bytes=60 * MIB),
        cost_estimate=LONG,
        name="attend_backward",
    )(
        qk, qk, values, mixed, mixed_grad, lse, segment_down, segment_across, cos_table, sin_table
    )


HBM = pl.BlockSpec(memory_space=pl.ANY)


def whole(shape):
    return pl.BlockSpec(shape, lambda *_: (0,) * len(shape), pipeline_mode=pl.Buffered(1))


def shaped(shape, dtype=BF16):
    return jax.ShapeDtypeStruct(shape, dtype)


def kernel_call(body, name, operands, in_specs, out_specs, out_shape, grid=(), scratch=(), scalars=(), aliases=None, vmem=40, flops=1, kept=False):
    return pl.pallas_call(
        body,
        grid_spec=pltpu.PrefetchScalarGridSpec(
            num_scalar_prefetch=len(scalars),
            grid=grid,
            in_specs=in_specs,
            out_specs=out_specs,
            scratch_shapes=list(scratch),
        ),
        out_shape=out_shape,
        input_output_aliases=aliases or {},
        compiler_params=pltpu.CompilerParams(vmem_limit_bytes=vmem * MIB, has_side_effects=kept),
        cost_estimate=pl.CostEstimate(flops=flops, bytes_accessed=1, transcendentals=1),
        name=name,
    )(*scalars, *operands)


def copies_into(blocks, target, semaphores, first, columns=None, rows=None):
    copies, at = [], 0
    for i, block in enumerate(blocks):
        deep = rows or block.shape[0]
        source = block if columns is None else block.at[pl.ds(0, deep), columns]
        copies.append(
            pltpu.make_async_copy(source, target.at[pl.ds(at, deep), :], semaphores.at[first + i])
        )
        at += deep
    return copies


def start_all(step, copies):
    @pl.when(step == 0)
    def _():
        for copy in copies:
            copy.start()


def wait_at(step, when, copies):
    @pl.when(step == when)
    def _():
        for copy in copies:
            copy.wait()


def halves(copies):
    return copies[: len(copies) // 2], copies[len(copies) // 2 :]


def mark_body(in_ref, out_ref):
    out_ref[...] = in_ref[...]


def mark(token, flops):
    return kernel_call(
        mark_body,
        "mark",
        [token],
        [whole(token.shape)],
        whole(token.shape),
        shaped(token.shape, token.dtype),
        grid=(1,),
        flops=flops,
        kept=True,
    )


def pick_columns(order, values):
    count = order.shape[0]
    width = values.shape[1] // count
    parts = [lax.dynamic_slice_in_dim(values, order[j] * width, width, 1) for j in range(count)]
    return jnp.concatenate(parts, axis=1)


def back_in_place(order, values):
    count = order.shape[0]
    if values.shape[1] // count % 128 == 0:
        return values
    places = jnp.arange(count, dtype=jnp.int32)
    back = jnp.sum(jnp.where(order[:, None] == places[None, :], places[:, None], 0), axis=0)
    return pick_columns(back, values)


def reorder_body(count, width, order_ref, in_ref, out_ref):
    for j in range(count):
        source = pl.ds(pl.multiple_of(order_ref[j] * width, width), width)
        out_ref[:, j * width : (j + 1) * width] = in_ref[:, source]


def reorder(order, values):
    count = order.shape[0]
    if values.shape[1] // count % 128:
        return pick_columns(order, values)
    return kernel_call(
        functools.partial(reorder_body, count, values.shape[1] // count),
        "reorder",
        [values],
        [whole(values.shape)],
        whole(values.shape),
        shaped(values.shape),
        grid=(1,),
        scalars=[order],
    )


def put_back(order_ref, out_ref, values):
    count = order_ref.shape[0]
    width = values.shape[1] // count
    if width % 128:
        out_ref[...] = values.astype(out_ref.dtype)
        return
    for j in range(count):
        target = pl.ds(pl.multiple_of(order_ref[j] * width, width), width)
        out_ref[:, target] = values[:, j * width : (j + 1) * width].astype(out_ref.dtype)


def stats_body(x_ref, mean_ref, inverse_ref):
    values = x_ref[...].astype(F32)
    mean = jnp.mean(values, axis=-1, keepdims=True)
    centred = values - mean
    mean_ref[...] = mean
    inverse_ref[...] = lax.rsqrt(jnp.mean(centred * centred, axis=-1, keepdims=True) + EPSILON)


def row_stats(inputs):
    length, depth = inputs.shape
    by_rows = lambda columns: pl.BlockSpec((length // 4, columns), lambda i: (i, 0))
    return kernel_call(
        stats_body,
        "row_stats",
        [inputs],
        [by_rows(depth)],
        [by_rows(1)] * 2,
        [shaped((length, 1), F32)] * 2,
        grid=(4,),
    )


def decode_body(count, chunk, order_ref, *refs):
    blocks, norm_ref, bias_ref = refs[:count], refs[-2], refs[-1]
    width = norm_ref.shape[1] // count
    wide = bias_ref.shape[1]
    small = wide // count
    rows = []
    for j, block in enumerate(blocks):
        norm_ref[:, j * width : (j + 1) * width] = block[0:4, :width].astype(F32)
        rows.append(block[4:5, :small].astype(F32))
    lane = lax.broadcasted_iota(jnp.int32, (small, wide), 1)
    source = lax.broadcasted_iota(jnp.int32, (small, wide), 0)
    spread = (lane // HD * chunk + lane % chunk == source).astype(BF16)
    spread = product(jnp.concatenate(rows, axis=0).astype(BF16), spread, 1, 0)
    lane = lax.broadcasted_iota(jnp.int32, (1, wide), 1)
    total = jnp.zeros((1, wide), F32)
    for j in range(count):
        total = jnp.where(lane % HD // chunk == order_ref[j], spread[j : j + 1, :], total)
    bias_ref[...] = total


def decode(order, blocks, depth, bias_wide):
    count = len(blocks)
    rows, wide = blocks[0].shape
    return kernel_call(
        functools.partial(decode_body, count, HD // count),
        "decode",
        blocks,
        [pl.BlockSpec((16, wide), lambda i, order: (rows // 16 - 1, 0))] * count,
        [whole((4, depth)), whole((1, bias_wide))],
        [shaped((4, depth), F32), shaped((1, bias_wide), F32)],
        grid=(1,),
        scalars=[order],
    )


def qkv_body(count, x_ref, norm_ref, bias_ref, mean_ref, inverse_ref, cos_ref, sin_ref, *refs):
    blocks_a, blocks_b, refs = refs[:count], refs[count : 2 * count], refs[2 * count :]
    qk_ref, v_ref, normed_ref, weight_a, weight_v, semaphores = refs
    step = pl.program_id(0)
    width = qk_ref.shape[1]
    deep = weight_a.shape[0] // count
    copies_a = copies_into(blocks_a, weight_a, semaphores, 0, rows=deep)
    copies_v = copies_into(blocks_b, weight_v, semaphores, count, pl.ds(0, width // 2), deep)
    start_all(step, copies_a + copies_v)
    values = (x_ref[...].astype(F32) - mean_ref[...]) * inverse_ref[...]
    normed = (values * norm_ref[0:1, :] + norm_ref[1:2, :]).astype(BF16)
    normed_ref[...] = normed
    wait_at(step, 0, copies_a)
    both = product(normed, weight_a[...], 1, 0) + bias_ref[:, :width]
    opening = opening_lanes(normed.shape[0])
    cos_values = cos_ref[...]
    sin_values = sin_ref[...]
    for at in range(0, width, PAIR):
        part = turn(both[:, at : at + PAIR], cos_values, sin_values, opening)
        qk_ref[:, at : at + PAIR] = part.astype(BF16)
    wait_at(step, 0, copies_v)
    v_ref[...] = (product(normed, weight_v[...], 1, 0) + bias_ref[:, width:]).astype(BF16)


def project_qkv(inputs, mean, inverse, norm_rows, bias_row, cos_table, sin_table, blocks_a, blocks_b):
    length, depth = inputs.shape
    rows = length // 4
    wide = blocks_a[0].shape[1]
    count = len(blocks_a)
    by_rows = lambda columns: pl.BlockSpec((rows, columns), lambda i: (i, 0))
    return kernel_call(
        functools.partial(qkv_body, count),
        "project_qkv",
        [inputs, norm_rows, bias_row, mean, inverse, cos_table, sin_table, *blocks_a, *blocks_b],
        [
            by_rows(depth),
            whole(norm_rows.shape),
            whole(bias_row.shape),
            by_rows(1),
            by_rows(1),
            by_rows(PAIR),
            by_rows(PAIR),
        ]
        + [HBM] * (2 * count),
        [by_rows(wide), by_rows(wide // 2), by_rows(depth)],
        [shaped((length, wide)), shaped((length, wide // 2)), shaped((length, depth))],
        grid=(4,),
        flops=10**9,
        scratch=[
            pltpu.VMEM((depth, wide), BF16),
            pltpu.VMEM((depth, wide // 2), BF16),
            pltpu.SemaphoreType.DMA((2 * count,)),
        ],
        vmem=60,
    )


def gated_body(count, x_ref, *refs):
    gate_blocks, up_blocks, refs = refs[:count], refs[count : 2 * count], refs[2 * count :]
    gate_ref, up_ref, hidden_ref, gate_weight, up_weight, semaphores = refs[-6:]
    step = pl.program_id(0)
    early, late = halves(copies_into(gate_blocks, gate_weight, semaphores, 0))
    early_up, late_up = halves(copies_into(up_blocks, up_weight, semaphores, count))
    start_all(step, early + late + early_up + late_up)
    half = gate_weight.shape[0] // 2
    wait_at(step, 0, early)
    gate = product(x_ref[:, :half], gate_weight[:half, :], 1, 0)
    wait_at(step, 0, late)
    gate = gate + product(x_ref[:, half:], gate_weight[half:, :], 1, 0)
    gate_ref[...] = gate.astype(BF16)
    wait_at(step, 0, early_up + late_up)
    up = product(x_ref[...], up_weight[...], 1, 0)
    up_ref[...] = up.astype(BF16)
    hidden_ref[...] = (gate * jax.nn.sigmoid(gate) * up).astype(BF16)


def gated_forward(inputs, gate_blocks, up_blocks, half, kept):
    length, depth = inputs.shape
    rows = length // 4
    wide = gate_blocks[0].shape[1]
    count = len(gate_blocks)
    kept = list(kept or [])
    place = lambda columns: pl.BlockSpec((rows, columns), lambda i: (2 * half + i, 0))
    first = 1 + 2 * count
    return kernel_call(
        functools.partial(gated_body, count),
        "gated_forward",
        [inputs, *gate_blocks, *up_blocks, *kept],
        [place(depth)] + [HBM] * (2 * count + len(kept)),
        [place(wide)] * 3,
        [shaped((length, wide))] * 3,
        grid=(2,),
        flops=10**9,
        scratch=[
            pltpu.VMEM((depth, wide), BF16),
            pltpu.VMEM((depth, wide), BF16),
            pltpu.SemaphoreType.DMA((2 * count,)),
        ],
        aliases={first + i: i for i in range(len(kept))},
        vmem=60,
    )


def gated_back_body(count, *refs):
    grad_ref, gate_ref, up_ref, refs = refs[0], refs[1], refs[2], refs[3:]
    blocks = refs[:count]
    gate_grad_ref, up_grad_ref, weight, semaphores = refs[-4:]
    step = pl.program_id(0)
    early, late = halves(copies_into(blocks, weight, semaphores, 0))
    start_all(step, early + late)
    gate = gate_ref[...].astype(F32)
    sigmoid = jax.nn.sigmoid(gate)
    silu = gate * sigmoid
    slope = sigmoid + silu * (1.0 - sigmoid)
    half = weight.shape[0] // 2
    wait_at(step, 0, early)
    hidden_grad = product(grad_ref[:, :half], weight[:half, :], 1, 0)
    wait_at(step, 0, late)
    hidden_grad = hidden_grad + product(grad_ref[:, half:], weight[half:, :], 1, 0)
    up_grad_ref[...] = (hidden_grad * silu).astype(BF16)
    gate_grad_ref[...] = (hidden_grad * up_ref[...].astype(F32) * slope).astype(BF16)


def gated_backward(grads, gate, up, blocks):
    length, wide = gate.shape
    rows = length // 4
    depth = grads.shape[1]
    count = len(blocks)
    by_rows = lambda columns: pl.BlockSpec((rows, columns), lambda i: (i, 0))
    return kernel_call(
        functools.partial(gated_back_body, count),
        "gated_backward",
        [grads, gate, up, *blocks],
        [by_rows(depth), by_rows(wide), by_rows(wide)] + [HBM] * count,
        [by_rows(wide)] * 2,
        [shaped((length, wide))] * 2,
        grid=(4,),
        flops=10**9,
        scratch=[pltpu.VMEM((depth, wide), BF16), pltpu.SemaphoreType.DMA((count,))],
        vmem=60,
    )


STRIPES = 4


def outward_body(shape, columns, deep, *refs):
    lefts, refs = refs[: len(shape)], refs[len(shape) :]
    out_ref = refs[sum(shape)]
    weights, semaphores = refs[sum(shape) + 1 : -1], refs[-1]
    step = pl.program_id(0)
    at, groups = 0, []
    for count, weight, column in zip(shape, weights, columns):
        groups.append(
            copies_into(refs[at : at + count], weight, semaphores, at, column, deep)
        )
        at += count
    for stripe in range(STRIPES):
        start_all(
            step,
            [
                copy
                for group in groups
                for copy in group[stripe * len(group) // STRIPES : (stripe + 1) * len(group) // STRIPES]
            ],
        )
    for stripe in range(STRIPES):
        for group in groups:
            wait_at(
                step,
                stripe,
                group[stripe * len(group) // STRIPES : (stripe + 1) * len(group) // STRIPES],
            )
    tall = weights[0].shape[0] // STRIPES
    span = pl.ds(pl.multiple_of(step * tall, tall), tall)
    total = None
    for left, weight in zip(lefts, weights):
        term = product(left[...], weight[span, :], 1, 1)
        total = term if total is None else total + term
    out_ref[...] = total.astype(BF16)


def outward(parts, depth, name):
    lefts = [left for left, _, _ in parts]
    length = lefts[0].shape[0]
    shape = [len(blocks) for _, blocks, _ in parts]
    deep = None
    columns = []
    for left, blocks, column in parts:
        if column is None:
            columns.append(None)
        else:
            columns.append(pl.ds(column, left.shape[1]))
            deep = depth // len(blocks)
    return kernel_call(
        functools.partial(outward_body, shape, columns, deep),
        name,
        [*lefts, *(block for _, blocks, _ in parts for block in blocks)],
        [whole(left.shape) for left in lefts] + [HBM] * sum(shape),
        pl.BlockSpec((length, depth // STRIPES), lambda i: (0, i)),
        shaped((length, depth)),
        grid=(STRIPES,),
        flops=10**9,
        scratch=[pltpu.VMEM((depth, left.shape[1]), BF16) for left in lefts]
        + [pltpu.SemaphoreType.DMA((sum(shape),))],
        vmem=60,
    )


def mixed_grad_body(count, rows_ref, *refs):
    blocks = refs[:count]
    out_ref, weight, semaphores = refs[count:]
    step = pl.program_id(0)
    wide = weight.shape[1]
    copies = copies_into(blocks, weight, semaphores, 0, pl.ds(wide, wide), weight.shape[0] // count)
    start_all(step, copies)
    wait_at(step, 0, copies)
    out_ref[...] = product(rows_ref[...], weight[...], 1, 0).astype(BF16)


def through_out(branch, blocks):
    length, depth = branch.shape
    rows = length // 4
    wide = blocks[0].shape[1] // 2
    count = len(blocks)
    return kernel_call(
        functools.partial(mixed_grad_body, count),
        "through_out",
        [branch, *blocks],
        [pl.BlockSpec((rows, depth), lambda i: (i, 0))] + [HBM] * count,
        pl.BlockSpec((rows, wide), lambda i: (i, 0)),
        shaped((length, wide)),
        grid=(4,),
        flops=10**9,
        scratch=[pltpu.VMEM((depth, wide), BF16), pltpu.SemaphoreType.DMA((count,))],
        vmem=60,
    )


def heads_body(count, q_ref, k_ref, v_ref, x_ref, mean_ref, inverse_ref, *refs):
    blocks_a, blocks_b = refs[:count], refs[count : 2 * count]
    out_ref, sums_ref, weight_a, weight_v, semaphores = refs[2 * count :]
    step = pl.program_id(0)
    wide = q_ref.shape[1]
    deep = weight_a.shape[0] // count
    copies_a = copies_into(blocks_a, weight_a, semaphores, 0, rows=deep)
    copies_v = copies_into(blocks_b, weight_v, semaphores, count, pl.ds(0, wide), deep)
    start_all(step, [copy for pair in zip(copies_a, copies_v) for copy in pair])
    for stripe in range(STRIPES):
        span = slice(stripe * count // STRIPES, (stripe + 1) * count // STRIPES)
        wait_at(step, stripe, copies_a[span] + copies_v[span])
    tall = weight_a.shape[0] // STRIPES
    span = pl.ds(pl.multiple_of(step * tall, tall), tall)
    total = product(q_ref[...], weight_a[span, :wide], 1, 1)
    total = total + product(k_ref[...], weight_a[span, wide:], 1, 1)
    total = total + product(v_ref[...], weight_v[span, :], 1, 1)
    out_ref[...] = total.astype(BF16)
    standard = (x_ref[...].astype(F32) - mean_ref[...]) * inverse_ref[...]
    sums_ref[0:1, :] = (total * standard).sum(0, keepdims=True)
    sums_ref[1:2, :] = total.sum(0, keepdims=True)


def through_heads(grads, inputs, mean, inverse, blocks_a, blocks_b):
    length, wide = grads[0].shape
    depth = inputs.shape[1]
    count = len(blocks_a)
    striped = lambda tall: pl.BlockSpec((tall, depth // STRIPES), lambda i: (0, i))
    return kernel_call(
        functools.partial(heads_body, count),
        "through_heads",
        [*grads, inputs, mean, inverse, *blocks_a, *blocks_b],
        [whole((length, wide))] * 3
        + [striped(length), whole((length, 1)), whole((length, 1))]
        + [HBM] * (2 * count),
        [striped(length), striped(2)],
        [shaped((length, depth)), shaped((2, depth), F32)],
        grid=(STRIPES,),
        flops=10**9,
        scratch=[
            pltpu.VMEM((depth, 2 * wide), BF16),
            pltpu.VMEM((depth, wide), BF16),
            pltpu.SemaphoreType.DMA((2 * count,)),
        ],
        vmem=60,
    )


def added(refs):
    total = refs[0][...].astype(F32)
    for ref in refs[1:]:
        total = total + ref[...].astype(F32)
    return total


def second_norm_body(x_ref, term_ref, norm_ref, middle_ref, mean_ref, inverse_ref, out_ref):
    middle = added([x_ref, term_ref])
    middle_ref[...] = middle
    mean = jnp.mean(middle, axis=-1, keepdims=True)
    centred = middle - mean
    inverse = lax.rsqrt(jnp.mean(centred * centred, axis=-1, keepdims=True) + EPSILON)
    mean_ref[...] = mean
    inverse_ref[...] = inverse
    out_ref[...] = (centred * inverse * norm_ref[2:3, :] + norm_ref[3:4, :]).astype(BF16)


def second_norm(inputs, term, norm_rows):
    shape = inputs.shape
    column = (shape[0], 1)
    return kernel_call(
        second_norm_body,
        "second_norm",
        [inputs, term, norm_rows],
        [whole(shape)] * 2 + [whole(norm_rows.shape)],
        [whole(shape), whole(column), whole(column), whole(shape)],
        [shaped(shape, F32), shaped(column, F32), shaped(column, F32), shaped(shape)],
        grid=(1,),
    )


def norm_gradient(upstream, standard, inverse, gain):
    scaled = upstream * gain
    inner = (
        scaled
        - jnp.mean(scaled, axis=-1, keepdims=True)
        - standard * jnp.mean(scaled * standard, axis=-1, keepdims=True)
    )
    return inverse * inner


def second_back_body(upstream_ref, middle_ref, mean_ref, inverse_ref, norm_ref, grad_ref, full_ref, branch_ref, sums_ref):
    upstream = upstream_ref[...].astype(F32)
    inverse = inverse_ref[...]
    standard = (middle_ref[...] - mean_ref[...]) * inverse
    sums_ref[0:1, :] = (upstream * standard).sum(0, keepdims=True)
    sums_ref[1:2, :] = upstream.sum(0, keepdims=True)
    grad = grad_ref[...].astype(F32) + norm_gradient(upstream, standard, inverse, norm_ref[2:3, :])
    full_ref[...] = grad
    branch_ref[...] = grad.astype(BF16)


def second_norm_back(upstream, middle, mean, inverse, norm_rows, grads):
    shape = middle.shape
    column = (shape[0], 1)
    return kernel_call(
        second_back_body,
        "second_norm_back",
        [upstream, middle, mean, inverse, norm_rows, grads],
        [whole(shape)] * 2 + [whole(column)] * 2 + [whole(norm_rows.shape), whole(shape)],
        [whole(shape), whole(shape), whole((2, shape[1]))],
        [shaped(shape, F32), shaped(shape), shaped((2, shape[1]), F32)],
        grid=(1,),
    )


def input_back_body(order_ref, upstream_ref, x_ref, norm_ref, grad_ref, out_ref):
    values = x_ref[...].astype(F32)
    centred = values - jnp.mean(values, axis=-1, keepdims=True)
    inverse = lax.rsqrt(jnp.mean(centred * centred, axis=-1, keepdims=True) + EPSILON)
    upstream = upstream_ref[...].astype(F32)
    grad = grad_ref[...] + norm_gradient(upstream, centred * inverse, inverse, norm_ref[0:1, :])
    put_back(order_ref, out_ref, grad)


def input_back(order, upstream, inputs, norm_rows, grads):
    shape = inputs.shape
    out = kernel_call(
        input_back_body,
        "input_back",
        [upstream, inputs, norm_rows, grads],
        [whole(shape)] * 2 + [whole(norm_rows.shape), whole(shape)],
        whole(shape),
        shaped(shape),
        grid=(1,),
        scalars=[order],
    )
    return back_in_place(order, out)


def result_body(order_ref, middle_ref, term_ref, out_ref):
    put_back(order_ref, out_ref, added([middle_ref, term_ref]))


def finish_result(order, middle, term):
    shape = middle.shape
    out = kernel_call(
        result_body,
        "finish_result",
        [middle, term],
        [whole(shape)] * 2,
        whole(shape),
        shaped(shape),
        grid=(1,),
        scalars=[order],
    )
    return back_in_place(order, out)


def hand_on_body(arrivals, sides, *refs):
    arrived, own, outs = refs[:arrivals], refs[arrivals : -sides], refs[-sides:]
    parts = len(own) // sides
    for side in range(sides):
        first = 0
        for part in own[side * parts : (side + 1) * parts]:
            span = slice(first, first + part.shape[1])
            values = part[...]
            if arrivals:
                values = (values.astype(F32) + arrived[side][:, span].astype(F32)).astype(BF16)
            outs[side][:, span] = values
            first += part.shape[1]


def hand_on(arrived, own, rows, places):
    shape = (rows, sum(part.shape[1] for part in own))
    sides = len(places)
    return kernel_call(
        functools.partial(hand_on_body, len(arrived), sides),
        "hand_on",
        [*arrived, *(part for _ in places for part in own)],
        [whole(shape)] * len(arrived)
        + [
            pl.BlockSpec((rows, part.shape[1]), lambda i, at=at: (at, 0))
            for at in places
            for part in own
        ],
        [whole(shape)] * sides,
        [shaped(shape)] * sides,
        grid=(1,),
    )


class Route:
    def __init__(self, count):
        self.count = count
        self.reach = count // 2
        self.ring = list(range(0, count, 2)) + list(range(count - 1, 0, -2))
        ahead = [(self.ring[i], self.ring[(i + 1) % count]) for i in range(count)]
        self.pairs = (ahead, [(b, a) for a, b in ahead])

    def send(self, values, direction):
        return lax.ppermute(values, "dp", self.pairs[direction])


class Gathering:
    def __init__(self, route, block, longer):
        self.route = route
        self.blocks = {0: block}
        self.steps = 0
        self.hops = [route.reach - (direction != longer) for direction in range(2)]
        self.done = 0
        self.flying = [block]

    def pending(self):
        return self.flying

    def resume(self, arrived):
        route = self.route
        if self.done == 0:
            self.blocks[0] = arrived[0]
            latest = [arrived[0], arrived[0]]
        else:
            arrived = list(arrived)
            latest = [None, None]
            for direction in range(2):
                if self.done <= self.hops[direction]:
                    latest[direction] = arrived.pop(0)
                    at = route.count - self.done if direction == 0 else self.done
                    self.blocks[at] = latest[direction]
        self.done += 1
        self.flying = [
            route.send(latest[direction], direction)
            for direction in range(2)
            if self.done <= self.hops[direction]
        ]

    def all(self):
        return [self.blocks[j] for j in range(self.route.count)]


class Summing:
    def __init__(self, route, own, rows, per, offset, longer):
        self.route = route
        self.own = own
        self.rows = rows
        self.place = lambda j: per * j + offset
        self.hops = [route.reach - (direction != longer) for direction in range(2)]
        self.steps = 0
        self.done = 0
        self.flying = None
        self.last = [None, None]

    def terms(self, arrived, directions):
        places = []
        for direction in directions:
            left = self.hops[direction] - self.done
            at = left if direction == 0 else (self.route.count - left) % self.route.count
            places.append(self.place(at))
        return hand_on(arrived, self.own(), self.rows, places)

    def pending(self):
        return self.flying if self.done else self.terms([], range(2))

    def resume(self, arrived):
        arrived = list(arrived)
        onward = range(2)
        if self.done:
            landed = [direction for direction in range(2) if self.done <= self.hops[direction]]
            onward = [direction for direction in landed if self.done < self.hops[direction]]
            by_way = dict(zip(landed, arrived))
            for direction in landed:
                if self.done == self.hops[direction]:
                    self.last[direction] = by_way[direction]
            if onward:
                arrived = self.terms([by_way[direction] for direction in onward], onward)
        self.done += 1
        self.flying = [self.route.send(values, way) for way, values in zip(onward, arrived)]

    def total(self, part, first):
        at = self.place(0) * self.rows
        own = part[at : at + self.rows].astype(F32)
        span = slice(first, first + part.shape[1])
        return own + self.last[0][:, span].astype(F32) + self.last[1][:, span].astype(F32)


STEPS = 5


class Pace:
    def __init__(self, token):
        self.token = token

    def __call__(self, streams, *carried, busy=False, long=False):
        last = {}
        for stream in streams:
            stream.steps += 1
            last[stream] = (stream.steps * (stream.route.reach + 1)) // STEPS
        first = True
        while first or any(stream.done < last[stream] for stream in streams):
            first = False
            moving = [stream for stream in streams if stream.done < last[stream]]
            waiting = [list(stream.pending()) for stream in moving]
            flat = [values for group in waiting for values in group]
            self.token, *out = lax.optimization_barrier((self.token, *flat, *carried))
            carried = out[len(flat) :]
            at = 0
            for stream, group in zip(moving, waiting):
                stream.resume(out[at : at + len(group)])
                at += len(group)
        if not busy:
            self.token = mark(self.token, 5 * 10**10 if long else 10**9)
            self.token, *carried = lax.optimization_barrier((self.token, *carried))
        return carried[0] if len(carried) == 1 else carried


def across_core(values):
    return lax.ppermute(values, "tensor", [(i, i ^ 1) for i in range(4)])


def across_chip(values):
    return lax.ppermute(values, "tensor", [(i, i ^ 2) for i in range(4)])


def spread_over_dp(route, table):
    left = route.count
    while left > 1:
        left //= 2
        pairs = [
            (route.ring[i], route.ring[(i + left) % route.count]) for i in range(route.count)
        ]
        table = table[:left] + lax.ppermute(table[left:], "dp", pairs)
    return table[0]


def on_device(
    route,
    activations,
    cotangent,
    segments,
    norm_one_gain,
    norm_one_bias,
    w_query,
    w_key,
    w_value,
    qkv_bias,
    w_out,
    norm_two_gain,
    norm_two_bias,
    w_gate,
    w_up,
    w_down,
):
    count = route.count
    third, depth = activations.shape
    length = segments.shape[0]
    width = depth // count
    part = width // 2
    heads_wide = w_query.shape[1]
    local_heads = heads_wide // HD
    shards = length // third
    here = lax.axis_index("tensor")
    advance = Pace(jnp.zeros((8, 128), jnp.int32) + here)
    device = lax.axis_index("dp").astype(jnp.int32)
    position = jnp.where(device % 2 == 0, device // 2, count - 1 - device // 2)
    ahead = (position + jnp.arange(count, dtype=jnp.int32)) % count
    order = jnp.where(ahead < count // 2, 2 * ahead, 2 * (count - 1 - ahead) + 1)

    def gather(values):
        return lax.all_gather(values, "tensor", axis=0, tiled=True)

    def scatter(values):
        return lax.psum_scatter(values, "tensor", scatter_dimension=0, tiled=True)

    def relative(values):
        def pick(entries):
            return jnp.concatenate([values[i : i + 1] for i in entries], axis=0)

        values = jnp.where(here % 2 == 1, pick((1, 0, 3, 2)), values)
        return jnp.where(here >= 2, pick((2, 3, 0, 1)), values)

    bias_size = qkv_bias.size
    norm_part = norm_one_gain.shape[0]
    ring_qk = Gathering(route, jnp.concatenate([w_query, w_key], axis=1), 0)
    ring_vo = Gathering(route, None, 1)
    ring_gate = Gathering(route, w_gate, 0)
    ring_up = Gathering(route, w_up, 1)
    ring_down = [Gathering(route, None, 0), Gathering(route, None, 1)]

    packed = jnp.stack([norm_one_gain, norm_one_bias, norm_two_gain, norm_two_bias])
    packed_core = across_core(packed)
    own_bf16 = reorder(order, activations)
    x_all = gather(own_bf16)
    packed = jnp.concatenate([packed, packed_core], axis=0)
    packed, w_down, w_value, w_out, cotangent = advance(
        [], packed, w_down, w_value, w_out, cotangent
    )
    packed_chip = across_chip(packed)
    weight_vo = jnp.concatenate([w_value, w_out.T], axis=1)
    packed_chip, weight_vo, cotangent, w_down = advance(
        [], packed_chip, weight_vo, cotangent, w_down
    )
    packed = jnp.concatenate([packed, packed_chip], axis=0).reshape(shards, 4, norm_part)
    packed = relative(packed).transpose(1, 0, 2).reshape(4, width)
    wide = 2 * heads_wide
    packed = jnp.concatenate(
        [
            jnp.pad(packed, ((0, 0), (0, wide - width))),
            jnp.pad(qkv_bias.reshape(1, bias_size), ((0, 11), (0, wide - bias_size))),
        ],
        axis=0,
    )
    ring_vo.flying = [jnp.concatenate([weight_vo, packed], axis=0)]
    cotangent, w_down = advance([ring_qk, ring_vo], cotangent, w_down, long=True)
    own_grad = reorder(order, cotangent)
    own_grad, w_down = advance([ring_qk], own_grad, w_down)
    down_rows = w_down.T
    ring_down[0].flying = [down_rows[:part]]
    ring_down[1].flying = [down_rows[part:]]
    x_all, own_grad = advance([ring_vo], x_all, own_grad)
    grad_all = gather(own_grad)
    mean_one, inverse_one = row_stats(x_all)
    mean_one, inverse_one, segments = advance([ring_qk], mean_one, inverse_one, segments)
    segment_down, segment_across = segments[:, None], segments[None, :]
    begins = jnp.sum((segment_across < segment_down).astype(F32), axis=1, keepdims=True)
    places = jnp.arange(length, dtype=jnp.int32)[:, None].astype(F32)
    lanes = jnp.arange(PAIR, dtype=jnp.int32) % HD
    frequency = 10000.0 ** (-2.0 * (lanes % (ROT // 2)).astype(F32) / ROT)
    angles = (places - begins) * frequency[None, :]
    cos_table = jnp.where(lanes < ROT, jnp.cos(angles), 1.0)
    sin_table = jnp.where(
        lanes < ROT, jnp.where(lanes < ROT // 2, -1.0, 1.0) * jnp.sin(angles), 0.0
    )
    cos_table, sin_table, segment_down, segment_across = advance(
        [ring_vo], cos_table, sin_table, segment_down, segment_across
    )
    advance([ring_qk], long=True)
    grad_all = advance([ring_vo, ring_gate], grad_all)
    advance([ring_qk])
    advance([ring_vo, ring_up], busy=True)
    blocks_a = ring_qk.all()
    blocks_b = ring_vo.all()
    norm_rows, bias_row = decode(order, blocks_b, depth, 3 * heads_wide)
    qk, values, normed = project_qkv(
        x_all, mean_one, inverse_one, norm_rows, bias_row, cos_table, sin_table, blocks_a, blocks_b
    )
    qk, values = advance([ring_gate], qk, values, busy=True)
    mixed, lse = attend_forward(qk, values, segment_down, segment_across, shards)
    mixed, lse = advance([ring_up], mixed, lse, busy=True)
    arriving = scatter(outward([(mixed, blocks_b, heads_wide)], depth, "from_heads"))
    advance([ring_gate])
    advance([ring_up], long=True)
    arriving = advance([ring_gate], arriving)
    middle, mean_two, inverse_two, n_own = second_norm(own_bf16, arriving, norm_rows)
    normed_two = gather(n_own)
    middle = advance([ring_up, ring_down[0]], middle)
    advance([ring_gate], long=True)
    normed_two = advance([ring_up, ring_down[1]], normed_two, busy=True)
    gate_blocks = ring_gate.all()
    up_blocks = ring_up.all()
    kept = gated_forward(normed_two, gate_blocks, up_blocks, 0, None)
    kept = advance([ring_down[0]], *kept)
    kept = advance([ring_down[1]], *kept, busy=True)
    gate, up, hidden = gated_forward(normed_two, gate_blocks, up_blocks, 1, kept)
    gate, up, hidden = advance([ring_down[0]], gate, up, hidden)
    hidden = advance([ring_down[1]], hidden)
    down_sum = product(grad_all, hidden, 0, 0).astype(BF16)
    down_sum = advance([ring_down[0]], down_sum)
    sum_down = Summing(route, lambda: [down_sum], width, 1, 0, 0)
    advance([ring_down[1], sum_down])
    advance([ring_down[0]])
    advance([ring_down[1]], busy=True)
    down_blocks = [block for pair in zip(*(ring.all() for ring in ring_down)) for block in pair]

    gate_grad, up_grad = gated_backward(grad_all, gate, up, down_blocks)
    gate_grad, up_grad = advance([sum_down], gate_grad, up_grad, busy=True)
    arriving = scatter(
        outward([(gate_grad, gate_blocks, None), (up_grad, up_blocks, None)], depth, "from_gates")
    )
    gate_grad, up_grad = advance([sum_down], gate_grad, up_grad)
    gate_sum = product(normed_two, gate_grad, 0, 0).astype(BF16)
    sum_gate = Summing(route, lambda: [gate_sum], width, 1, 0, 1)
    gate_sum, up_grad = advance([sum_gate], gate_sum, up_grad, long=True)
    up_sum = product(normed_two, up_grad, 0, 0).astype(BF16)
    sum_up = Summing(route, lambda: [up_sum], width, 1, 0, 0)
    up_sum = advance([sum_down], up_sum)
    arriving = advance([sum_gate], arriving)
    middle_grad, b_own, two_sums = second_norm_back(
        arriving, middle, mean_two, inverse_two, norm_rows, own_grad
    )
    branch = gather(b_own)
    hidden = advance([sum_down], hidden, busy=True)
    result_terms = outward([(hidden, down_blocks, None)], depth, "from_hidden")
    result_terms = advance([sum_gate, sum_up], result_terms, long=True)
    branch, result_terms = advance([sum_gate], branch, result_terms, busy=True)
    arriving_result = scatter(result_terms)
    mixed_grad = through_out(branch, blocks_b)
    mixed_grad, branch = advance([sum_up], mixed_grad, branch, busy=True)
    q_grad, k_grad, v_grad, bias_sums = attend_backward(
        qk,
        values,
        mixed,
        mixed_grad,
        lse,
        segment_down,
        segment_across,
        cos_table,
        sin_table,
        shards,
    )
    q_grad, k_grad, v_grad, bias_sums = advance([sum_gate], q_grad, k_grad, v_grad, bias_sums)
    q_sum = product(normed, q_grad, 0, 0).astype(BF16)
    k_sum = product(normed, k_grad, 0, 0).astype(BF16)
    sum_qk = Summing(route, lambda: [q_sum, k_sum], width, 1, 0, 1)
    q_sum, k_sum, v_grad, branch, arriving_result = advance(
        [sum_up, sum_qk], q_sum, k_sum, v_grad, branch, arriving_result
    )
    out_sum = product(branch, mixed, 0, 0).astype(BF16)
    v_sum = product(normed, v_grad, 0, 0).astype(BF16)
    sum_vo = Summing(route, lambda: [v_sum, out_sum], width, 1, 0, 0)
    out_sum, v_sum, q_grad = advance([sum_up], out_sum, v_sum, q_grad)
    q_grad = advance([sum_vo, sum_qk], q_grad, busy=True)
    heads_terms, one_sums = through_heads(
        [q_grad, k_grad, v_grad], x_all, mean_one, inverse_one, blocks_a, blocks_b
    )
    arriving = scatter(heads_terms)
    one_sums, middle, arriving_result = advance([sum_up], one_sums, middle, arriving_result, long=True)
    norm_grads = jnp.concatenate([one_sums, two_sums], axis=0)
    bias_sums = bias_sums.transpose(1, 0, 2).reshape(3, local_heads, count, HD // count)
    bias_sums = bias_sums.transpose(2, 0, 1, 3).reshape(count, bias_size)[order]
    extras = jnp.concatenate(
        [norm_grads.reshape(4, count, width).transpose(1, 0, 2).reshape(count, 4 * width), bias_sums],
        axis=1,
    )
    extras = jnp.pad(extras, ((0, 0), (0, -extras.shape[1] % 128)))
    result = finish_result(order, middle, arriving_result)
    grad_down = sum_down.total(down_sum, 0).T
    grad_gate = sum_gate.total(gate_sum, 0)
    extras, result, grad_down, grad_gate = advance(
        [sum_vo, sum_qk], extras, result, grad_down, grad_gate
    )
    extras = spread_over_dp(route, extras)
    grad_up = sum_up.total(up_sum, 0)
    grad_up = advance([sum_vo, sum_qk], grad_up)
    arriving, extras = advance([sum_vo, sum_qk], arriving, extras)
    input_grad = input_back(order, arriving, own_bf16, norm_rows, middle_grad)
    norm_sums = extras[: 4 * width].reshape(4, width)
    norm_sums = norm_sums + across_core(norm_sums)
    norm_sums = norm_sums + across_chip(norm_sums)
    norm_sums = lax.dynamic_slice_in_dim(norm_sums, here * norm_part, norm_part, axis=1)
    bias_grad = extras[4 * width : 4 * width + bias_size].reshape(qkv_bias.shape)
    input_grad, norm_sums = advance([sum_vo], input_grad, norm_sums)

    return (
        result,
        input_grad,
        norm_sums[0],
        norm_sums[1],
        sum_qk.total(q_sum, 0),
        sum_qk.total(k_sum, heads_wide),
        sum_vo.total(v_sum, 0),
        bias_grad,
        sum_vo.total(out_sum, heads_wide).T,
        norm_sums[2],
        norm_sums[3],
        grad_gate,
        grad_up,
        grad_down,
    )


def solution(mesh):
    both = P(("dp", "tensor"))
    tokens = P(("dp", "tensor"), None)
    rows = P("dp", "tensor")
    columns = P("tensor", "dp")
    biases = P(None, "tensor", "dp")
    return jax.shard_map(
        functools.partial(on_device, Route(mesh.shape["dp"])),
        mesh=mesh,
        in_specs=(
            tokens,
            tokens,
            P("dp"),
            both,
            both,
            rows,
            rows,
            rows,
            biases,
            columns,
            both,
            both,
            rows,
            rows,
            columns,
        ),
        out_specs=(
            tokens,
            tokens,
            both,
            both,
            rows,
            rows,
            rows,
            biases,
            columns,
            both,
            both,
            rows,
            rows,
            columns,
        ),
        check_vma=False,
    )
```

time: 787 us -> 706 us (0.90)
  Pallas kernels: 54.7 us -> 191 us
  matrix products: 154 us -> 38 us
  other arithmetic: 66.7 us -> 18.8 us
  blocking collectives: 46.1 us -> 0 us
  waiting for transfers between devices: 253 us -> 270 us
  local copies, waits for them, and re-layouts: 88.2 us -> 72.6 us
    pallas_call x1 -> x71, Pallas kernels: 10.4 us -> 146 us  [kernel_call(): pl.pallas_call(body, grid_spec=pltpu.PrefetchScalarGridSpec(num_scalar_pr...]
    dot_general x25 -> x7, matrix products: 154 us -> 38 us  [product(): lax.dot_general(left, right, (((left_dim,), (right_dim,)), ((), ())), pre...]
    all_gather x1 -> x0, blocking collectives: 46.1 us -> none  [on_device(): small = lax.all_gather(packed, ('dp', 'tensor'), axis=0, tiled=True)]
    convert_element_type x31 -> x0, other arithmetic: 30.9 us -> none  [the longest x19 19.8 us: resume(): values = (values.astype(F32) + own.astype(F32)).astype(BF16)]
    ppermute x84 -> x77, waiting for transfers between devices: 226 us -> 255 us  [send(): return lax.ppermute(values, 'dp', self.pairs[direction])]
    ppermute x9 -> x2, waiting for transfers between devices: 26.9 us -> 1.49 us  [across_chip(): return lax.ppermute(values, 'tensor', [(i, i ^ 2) for i in range(4)])]
    unnamed x372 -> x263, local copies, waits for them, and re-layouts: 48.7 us -> 64.8 us
    slice x30 -> x10, local copies, waits for them, and re-layouts: 18.1 us -> 2.04 us  [the longest x1 1.99 us: on_device(): ring_down[1].flying = [down_rows[part:]]]
  transfers between devices with their start and end apart: 110 -> 92, of which waited for: 47 -> 54; matrix products, arithmetic and copies ran while one was open for 34% -> 9% of each run, Pallas kernels for 7% -> 23%
where the time goes in v2:
time: 706 us; the launch traced here: 700 us
  waiting for transfers between devices  270 us (38%)
  Pallas kernels  191 us (27%)
  starting transfers between devices  94.4 us (13%)
  local copies, waits for them, and re-layouts  72.6 us (10%)
  matrix products  38 us (5%)
  other arithmetic  18.8 us (3%)
  between operations  16.1 us (2%)
    ppermute x77, waiting for transfers between devices, send(): return lax.ppermute(values, 'dp', self.pairs[direction])  255 us
    pallas_call x71, Pallas kernels, kernel_call(): pl.pallas_call(body, grid_spec=pltpu.PrefetchScalarGridSpec(num_scalar_pr...  146 us
    ppermute x77, starting transfers between devices, send(): return lax.ppermute(values, 'dp', self.pairs[direction])  80.7 us
    unnamed x263, local copies, waits for them, and re-layouts  64.8 us
    dot_general x7, matrix products, product(): lax.dot_general(left, right, (((left_dim,), (right_dim,)), ((), ())), pre...  38 us
    pallas_call x1, Pallas kernels, attend_backward(): pl.pallas_call(functools.partial(backward_body, length // count, count),...  26.7 us
    pallas_call x1, Pallas kernels, attend_forward(): pl.pallas_call(functools.partial(forward_body, length // count, count), g...  17.9 us
  transfers between devices with their start and end apart: 92, of which 54 were waited for; matrix products, arithmetic and copies ran while one was open for 9% of the time, Pallas kernels for 23%

profile of v2, /device:TPU:0, one launch (start us, length us, event | category | flops | bytes accessed | tf_op | source)
XLA Modules:
  0.0 700.3 jit_solution(12451515111923953971)
XLA Ops:
  22.8 9.1 %collective-permute-done.2.refs_7_ = bf16[256,1024]{1,0:T(8,128)(2,1)S(1)} collective-permute-done((bf16[256,1024]{1,0:T(8,128)(2,1)S(1)}, bf16[256,1024]{1,0:T(8,128)(2,1)S(1)}, u32[]{:S(2)}, u32[]{:S(2)}) %collective-permute-start.2) | collective-permute-done | bytes 524320 | tf_op jit(solution)/shard_map/ppermute | solution.py:833
  34.0 8.4 %collective-permute-done.4.refs_7_.refs_15_.refs_8_ = bf16[272,1024]{1,0:T(8,128)(2,1)S(1)} collective-permute-done((bf16[272,1024]{1,0:T(8,128)(2,1)S(1)}, bf16[272,1024]{1,0:T(8,128)(2,1)S(1)}, u32[]{:S(2)}, u32[]{:S(2)}) %collective-permute-start.4) | collective-permute-done | bytes 557088 | tf_op jit(solution)/shard_map/ppermute | solution.py:833
  55.3 7.5 %collective-permute-done.6.refs_6_ = bf16[256,1024]{1,0:T(8,128)(2,1)S(1)} collective-permute-done((bf16[256,1024]{1,0:T(8,128)(2,1)S(1)}, bf16[256,1024]{1,0:T(8,128)(2,1)S(1)}, u32[]{:S(2)}, u32[]{:S(2)}) %collective-permute-start.6) | collective-permute-done | bytes 524320 | tf_op jit(solution)/shard_map/ppermute | solution.py:833
  71.7 7.9 %collective-permute-done.8.refs_6_.refs_14_.refs_7_ = bf16[272,1024]{1,0:T(8,128)(2,1)S(1)} collective-permute-done((bf16[272,1024]{1,0:T(8,128)(2,1)S(1)}, bf16[272,1024]{1,0:T(8,128)(2,1)S(1)}, u32[]{:S(2)}, u32[]{:S(2)}) %collective-permute-start.8) | collective-permute-done | bytes 557088 | tf_op jit(solution)/shard_map/ppermute | solution.py:833
  81.0 8.0 %collective-permute-done.10.refs_5_ = bf16[256,1024]{1,0:T(8,128)(2,1)} collective-permute-done((bf16[256,1024]{1,0:T(8,128)(2,1)S(1)}, bf16[256,1024]{1,0:T(8,128)(2,1)}, u32[]{:S(2)}, u32[]{:S(2)}) %collective-permute-start.10) | collective-permute-done | bytes 524320 | tf_op jit(solution)/shard_map/ppermute | solution.py:833
  93.8 12.0 %collective-permute-done.12.refs_5_.refs_13_.refs_6_ = bf16[272,1024]{1,0:T(8,128)(2,1)S(1)} collective-permute-done((bf16[272,1024]{1,0:T(8,128)(2,1)S(1)}, bf16[272,1024]{1,0:T(8,128)(2,1)S(1)}, u32[]{:S(2)}, u32[]{:S(2)}) %collective-permute-start.12) | collective-permute-done | bytes 557088 | tf_op jit(solution)/shard_map/ppermute | solution.py:833
  108.4 8.7 %collective-permute-done.14.refs_4_ = bf16[256,1024]{1,0:T(8,128)(2,1)} collective-permute-done((bf16[256,1024]{1,0:T(8,128)(2,1)}, bf16[256,1024]{1,0:T(8,128)(2,1)}, u32[]{:S(2)}, u32[]{:S(2)}) %collective-permute-start.14) | collective-permute-done | bytes 524320 | tf_op jit(solution)/shard_map/ppermute | solution.py:833
  129.5 15.7 %project_qkv.1 = (bf16[1024,1024]{1,0:T(8,128)(2,1)}, bf16[1024,512]{1,0:T(8,128)(2,1)}, bf16[1024,2048]{1,0:T(8,128)(2,1)}) custom-call(bf16[1024,2048]{1,0:T(8,128)(2,1)} %all-gather.5.cloned.1.call-done.x_ref, f32[4,2048]{1,0:T(4,128)} %copy-done.41, f32[1,1536]{1,0:T(1,128)} %copy-done.55, f32[1024,1]{1,0:T(8,128)} %copy-done.29, f32[1024,1]{1,0:T(8,128)} %copy-done.30, ...), custom_call_target="tpu_custom_call" | custom-call | flops 1000000000 | bytes 1 | tf_op jit(solution)/shard_map/project_qkv/pallas_call | solution.py:223
  145.2 17.9 %attend_forward.1 = (bf16[1024,512]{1,0:T(8,128)(2,1)}, f32[4,2,1024]{2,1,0:T(2,128)}) custom-call(bf16[1024,1024]{1,0:T(8,128)(2,1)} %get-tuple-element.468.q_ref.k_ref, bf16[1024,1024]{1,0:T(8,128)(2,1)} %get-tuple-element.468.q_ref.k_ref, bf16[1024,512]{1,0:T(8,128)(2,1)} %get-tuple-element.469.v_ref, s32[1024,1]{1,0:T(8,128)} %copy.48.down_ref, ...), custom_call_target="tpu_custom_call" | custom-call | flops 1000000000 | bytes 1 | tf_op jit(solution)/shard_map/attend_forward/pallas_call | solution.py:78
  163.1 6.7 from_heads.1
  174.0 15.2 %collective-permute-done.20.refs_6_.refs_8_ = bf16[256,1408]{1,0:T(8,128)(2,1)S(1)} collective-permute-done((bf16[256,1408]{1,0:T(8,128)(2,1)}, bf16[256,1408]{1,0:T(8,128)(2,1)S(1)}, u32[]{:S(2)}, u32[]{:S(2)}) %collective-permute-start.20) | collective-permute-done | bytes 720928 | tf_op jit(solution)/shard_map/ppermute | solution.py:833
  192.7 7.7 %collective-permute-done.22.refs_14_.refs_16_ = bf16[256,1408]{1,0:T(8,128)(2,1)S(1)} collective-permute-done((bf16[256,1408]{1,0:T(8,128)(2,1)}, bf16[256,1408]{1,0:T(8,128)(2,1)S(1)}, u32[]{:S(2)}, u32[]{:S(2)}) %collective-permute-start.22) | collective-permute-done | bytes 720928 | tf_op jit(solution)/shard_map/ppermute | solution.py:833
  226.1 11.4 %collective-permute-done.26.refs_13_.refs_15_ = bf16[256,1408]{1,0:T(8,128)(2,1)} collective-permute-done((bf16[256,1408]{1,0:T(8,128)(2,1)S(1)}, bf16[256,1408]{1,0:T(8,128)(2,1)}, u32[]{:S(2)}, u32[]{:S(2)}) %collective-permute-start.26) | collective-permute-done | bytes 720928 | tf_op jit(solution)/shard_map/ppermute | solution.py:833
  241.0 12.0 %collective-permute-done.28.refs_4_.refs_6_ = bf16[256,1408]{1,0:T(8,128)(2,1)} collective-permute-done((bf16[256,1408]{1,0:T(8,128)(2,1)}, bf16[256,1408]{1,0:T(8,128)(2,1)}, u32[]{:S(2)}, u32[]{:S(2)}) %collective-permute-start.28) | collective-permute-done | bytes 720928 | tf_op jit(solution)/shard_map/ppermute | solution.py:833
  253.0 10.6 %collective-permute-done.29.refs_12_.refs_14_ = bf16[256,1408]{1,0:T(8,128)(2,1)S(1)} collective-permute-done((bf16[256,1408]{1,0:T(8,128)(2,1)}, bf16[256,1408]{1,0:T(8,128)(2,1)S(1)}, u32[]{:S(2)}, u32[]{:S(2)}) %collective-permute-start.29) | collective-permute-done | bytes 720928 | tf_op jit(solution)/shard_map/ppermute | solution.py:833
  265.9 12.7 %gated_forward.2 = (bf16[1024,1408]{1,0:T(8,128)(2,1)}, bf16[1024,1408]{1,0:T(8,128)(2,1)}, bf16[1024,1408]{1,0:T(8,128)(2,1)}) custom-call(bf16[1024,2048]{1,0:T(8,128)(2,1)} %all-gather.9.cloned.1.call-done.x_ref, bf16[256,1408]{1,0:T(8,128)(2,1)} %refs_2_, bf16[256,1408]{1,0:T(8,128)(2,1)} %collective-permute-done.17.refs_1_.refs_3_, ...), custom_call_target="tpu_custom_call" | custom-call | flops 1000000000 | bytes 1 | tf_op jit(solution)/shard_map/gated_forward/pallas_call | solution.py:223
  282.8 12.7 %gated_forward.3 = (bf16[1024,1408]{1,0:T(8,128)(2,1)}, bf16[1024,1408]{1,0:T(8,128)(2,1)}, bf16[1024,1408]{1,0:T(8,128)(2,1)}) custom-call(bf16[1024,2048]{1,0:T(8,128)(2,1)} %all-gather.9.cloned.1.call-done.x_ref, bf16[256,1408]{1,0:T(8,128)(2,1)} %refs_2_, ...), custom_call_target="tpu_custom_call", output_to_operand_aliasing={{0}: (17, {}), {1}: (18, {}), {2}: (19, {})} | custom-call | flops 1000000000 | bytes 1 | tf_op jit(solution)/shard_map/gated_forward/pallas_call | solution.py:223
  299.8 7.1 %convolution_convert_fusion.2.refs_0_.refs_1_.refs_2_.refs_3_ = bf16[2048,1408]{1,0:T(8,128)(2,1)S(1)} fusion(bf16[1024,2048]{1,0:T(8,128)(2,1)S(1)} %copy-done.83, bf16[1024,1408]{1,0:T(8,128)(2,1)S(1)} %copy-done.73), kind=kOutput, calls=%fused_computation.3 | convolution fusion | flops 5908463616 | bytes 12845056 | tf_op jit(solution)/shard_map/dot_general | solution.py:23
  316.5 16.1 %collective-permute-done.42.refs_11_.refs_9_ = bf16[128,1408]{1,0:T(8,128)(2,1)S(1)} collective-permute-done((bf16[128,1408]{1,0:T(8,128)(2,1)S(1)}, bf16[128,1408]{1,0:T(8,128)(2,1)S(1)}, u32[]{:S(2)}, u32[]{:S(2)}) %collective-permute-start.42) | collective-permute-done | bytes 360480 | tf_op jit(solution)/shard_map/ppermute | solution.py:833
  333.9 16.3 %gated_backward.1 = (bf16[1024,1408]{1,0:T(8,128)(2,1)}, bf16[1024,1408]{1,0:T(8,128)(2,1)}) custom-call(bf16[1024,2048]{1,0:T(8,128)(2,1)} %all-gather.7.cloned.1.call-done.refs_0_, bf16[1024,1408]{1,0:T(8,128)(2,1)} %get-tuple-element.557.refs_1_, bf16[1024,1408]{1,0:T(8,128)(2,1)} %get-tuple-element.558.refs_2_, ...), custom_call_target="tpu_custom_call" | custom-call | flops 1000000000 | bytes 1 | tf_op jit(solution)/shard_map/gated_backward/pallas_call | solution.py:223
  356.1 19.6 %from_gates.1 = bf16[1024,2048]{1,0:T(8,128)(2,1)} custom-call(bf16[1024,1408]{1,0:T(8,128)(2,1)} %get-tuple-element.576.refs_0_, bf16[1024,1408]{1,0:T(8,128)(2,1)} %get-tuple-element.588.refs_1_, bf16[256,1408]{1,0:T(8,128)(2,1)} %refs_2_, bf16[256,1408]{1,0:T(8,128)(2,1)} %collective-permute-done.17.refs_1_.refs_3_, bf16[256,1408]{1,0:T(8,128)(2,1)} %copy-done.75, ...), custom_call_target="tpu_custom_call" | custom-call | flops 1000000000 | bytes 1 | tf_op jit(solution)/shard_map/from_gates/pallas_call | solution.py:223
  377.6 10.4 %convolution_convert_fusion.1.refs_0_.refs_1_.refs_2_.refs_3_ = bf16[2048,1408]{1,0:T(8,128)(2,1)S(1)} fusion(bf16[1024,2048]{1,0:T(8,128)(2,1)} %all-gather.9.cloned.1.call-done.x_ref, bf16[1024,1408]{1,0:T(8,128)(2,1)S(1)} %copy-done.86), kind=kOutput, calls=%fused_computation.2 | convolution fusion | flops 5908463616 | bytes 12845056 | tf_op jit(solution)/shard_map/dot_general | solution.py:23
  395.2 8.7 %convolution_convert_fusion.refs_0_.refs_1_.refs_2_.refs_3_ = bf16[2048,1408]{1,0:T(8,128)(2,1)} fusion(bf16[1024,2048]{1,0:T(8,128)(2,1)S(1)} %copy-done.72, bf16[1024,1408]{1,0:T(8,128)(2,1)S(1)} %copy-done.85), kind=kOutput, calls=%fused_computation.1 | convolution fusion | flops 5908463616 | bytes 12845056 | tf_op jit(solution)/shard_map/dot_general | solution.py:23
  439.0 9.4 %collective-permute-done.52 = bf16[256,1408]{1,0:T(8,128)(2,1)} collective-permute-done((bf16[256,1408]{1,0:T(8,128)(2,1)S(1)}, bf16[256,1408]{1,0:T(8,128)(2,1)}, u32[]{:S(2)}, u32[]{:S(2)}) %collective-permute-start.52) | collective-permute-done | bytes 720928 | tf_op jit(solution)/shard_map/ppermute | solution.py:833
  448.5 11.8 %from_hidden.1 = bf16[1024,2048]{1,0:T(8,128)(2,1)} custom-call(bf16[1024,1408]{1,0:T(8,128)(2,1)} %get-tuple-element.607.refs_0_, bf16[128,1408]{1,0:T(8,128)(2,1)} %get-tuple-element.500.refs_3_.refs_1_, bf16[128,1408]{1,0:T(8,128)(2,1)} %copy-done.84, bf16[128,1408]{1,0:T(8,128)(2,1)} %collective-permute-done.31.refs_5_.refs_3_, ...), custom_call_target="tpu_custom_call" | custom-call | flops 1000000000 | bytes 1 | tf_op jit(solution)/shard_map/from_hidden/pallas_call | solution.py:223
  465.5 13.6 %collective-permute-done.55 = bf16[256,1408]{1,0:T(8,128)(2,1)S(1)} collective-permute-done((bf16[256,1408]{1,0:T(8,128)(2,1)S(1)}, bf16[256,1408]{1,0:T(8,128)(2,1)S(1)}, u32[]{:S(2)}, u32[]{:S(2)}) %collective-permute-start.55) | collective-permute-done | bytes 720928 | tf_op jit(solution)/shard_map/ppermute | solution.py:833
  485.8 7.6 %through_out.1.grad_ref = bf16[1024,512]{1,0:T(8,128)(2,1)} custom-call(bf16[1024,2048]{1,0:T(8,128)(2,1)} %all-gather.11.cloned.1.call-done.rows_ref, bf16[272,1024]{1,0:T(8,128)(2,1)} %copy-done.19, bf16[272,1024]{1,0:T(8,128)(2,1)} %copy-done.21, bf16[272,1024]{1,0:T(8,128)(2,1)} %copy-done.23, ...), custom_call_target="tpu_custom_call" | custom-call | flops 1000000000 | bytes 1 | tf_op jit(solution)/shard_map/through_out/pallas_call | solution.py:223
  506.1 26.7 %attend_backward.1 = (bf16[1024,512]{1,0:T(8,128)(2,1)}, bf16[1024,512]{1,0:T(8,128)(2,1)}, bf16[1024,512]{1,0:T(8,128)(2,1)}, f32[4,3,128]{2,1,0:T(4,128)}) custom-call(bf16[1024,1024]{1,0:T(8,128)(2,1)} %get-tuple-element.468.q_ref.k_ref, bf16[1024,1024]{1,0:T(8,128)(2,1)} %get-tuple-element.468.q_ref.k_ref, bf16[1024,512]{1,0:T(8,128)(2,1)} %get-tuple-element.469.v_ref, ...), custom_call_target="tpu_custom_call" | custom-call | flops 49999998976 | bytes 1 | tf_op jit(solution)/shard_map/attend_backward/pallas_call | solution.py:176
  557.1 9.8 %collective-permute-done.62.refs_0_ = bf16[256,1408]{1,0:T(8,128)(2,1)S(1)} collective-permute-done((bf16[256,1408]{1,0:T(8,128)(2,1)S(1)}, bf16[256,1408]{1,0:T(8,128)(2,1)S(1)}, u32[]{:S(2)}, u32[]{:S(2)}) %collective-permute-start.62) | collective-permute-done | bytes 720928 | tf_op jit(solution)/shard_map/ppermute | solution.py:833
  574.4 13.0 %through_heads.1 = (bf16[1024,2048]{1,0:T(8,128)(2,1)}, f32[2,2048]{1,0:T(2,128)}) custom-call(bf16[1024,512]{1,0:T(8,128)(2,1)} %get-tuple-element.678.q_ref, bf16[1024,512]{1,0:T(8,128)(2,1)} %get-tuple-element.645.k_ref, bf16[1024,512]{1,0:T(8,128)(2,1)} %get-tuple-element.663.v_ref, bf16[1024,2048]{1,0:T(8,128)(2,1)} %all-gather.5.cloned.1.call-done.x_ref, ...), custom_call_target="tpu_custom_call" | custom-call | flops 1000000000 | bytes 1 | tf_op jit(solution)/shard_map/through_heads/pallas_call | solution.py:223
  613.8 6.4 collective-permute-done.69.refs_0_
  644.1 7.1 %collective-permute-done.71.refs_0_ = bf16[256,1024]{1,0:T(8,128)(2,1)S(1)} collective-permute-done((bf16[256,1024]{1,0:T(8,128)(2,1)S(1)}, bf16[256,1024]{1,0:T(8,128)(2,1)S(1)}, u32[]{:S(2)}, u32[]{:S(2)}) %collective-permute-start.71) | collective-permute-done | bytes 524320 | tf_op jit(solution)/shard_map/ppermute | solution.py:833
  (557 shorter events, 316.5 us)
Async XLA Ops:
  7.2 41.3 %all-gather.5.cloned.1.call-start = ((), (), s32[]{:S(2)}) async-start(), calls=%async_computation.4 | async-start | bytes 5242880 | tf_op jit(solution)/shard_map/all_gather | solution.py:1000
  11.5 94.3 %all-gather.7.cloned.1.call-start = ((), (), s32[]{:S(2)}) async-start(), calls=%async_computation.5 | async-start | bytes 5242880 | tf_op jit(solution)/shard_map/all_gather | solution.py:1000
  19.1 23.3 %collective-permute-start.4 = (bf16[272,1024]{1,0:T(8,128)(2,1)S(1)}, bf16[272,1024]{1,0:T(8,128)(2,1)S(1)}, u32[]{:S(2)}, u32[]{:S(2)}) collective-permute-start(bf16[272,1024]{1,0:T(8,128)(2,1)S(1)} %fusion.4.refs_0_.refs_8_.refs_1_), channel_id=1, source_target_pairs={{0,8},{8,16},{16,24},{24,28},{28,20},{20,12},{12,4},{4,0},{1,9},{9... | collective-permute-start | bytes 1671176 | tf_op jit(solution)/shard_map/ppermute | solution.py:833
  48.6 164.1 %reduce-scatter.5.cloned.1.call-start = ((), (), s32[]{:S(2)}) async-start(), calls=%async_computation.6 | async-start | bytes 5242880 | tf_op jit(solution)/shard_map/reduce_scatter | solution.py:1003
  66.0 23.1 %collective-permute-start.10 = (bf16[256,1024]{1,0:T(8,128)(2,1)S(1)}, bf16[256,1024]{1,0:T(8,128)(2,1)}, u32[]{:S(2)}, u32[]{:S(2)}) collective-permute-start(bf16[256,1024]{1,0:T(8,128)(2,1)S(1)} %collective-permute-done.6.refs_6_), channel_id=1, source_target_pairs={{0,8},{8,16},{16,24},{24,28},{28,20},{20,12},{12,4},{4,0},{1,9},{9... | collective-permute-start | bytes 1572872 | tf_op jit(solution)/shard_map/ppermute | solution.py:833
  67.5 22.8 %collective-permute-start.11 = (bf16[256,1024]{1,0:T(8,128)(2,1)S(1)}, bf16[256,1024]{1,0:T(8,128)(2,1)}, u32[]{:S(2)}, u32[]{:S(2)}) collective-permute-start(bf16[256,1024]{1,0:T(8,128)(2,1)S(1)} %collective-permute-done.7.refs_2_), channel_id=1, source_target_pairs={{8,0},{16,8},{24,16},{28,24},{20,28},{12,20},{4,12},{0,4},{9,1},{1... | collective-permute-start | bytes 1572872 | tf_op jit(solution)/shard_map/ppermute | solution.py:833
  92.3 24.9 %collective-permute-start.14 = (bf16[256,1024]{1,0:T(8,128)(2,1)}, bf16[256,1024]{1,0:T(8,128)(2,1)}, u32[]{:S(2)}, u32[]{:S(2)}) collective-permute-start(bf16[256,1024]{1,0:T(8,128)(2,1)} %collective-permute-done.10.refs_5_), channel_id=1, source_target_pairs={{0,8},{8,16},{16,24},{24,28},{28,20},{20,12},{12,4},{4,0},{1,9},{9... | collective-permute-start | bytes 1572872 | tf_op jit(solution)/shard_map/ppermute | solution.py:833
  106.4 38.8 %collective-permute-start.16 = (bf16[256,1408]{1,0:T(8,128)(2,1)}, bf16[256,1408]{1,0:T(8,128)(2,1)}, u32[]{:S(2)}, u32[]{:S(2)}) collective-permute-start(bf16[256,1408]{1,0:T(8,128)(2,1)} %refs_2_), channel_id=1, source_target_pairs={{0,8},{8,16},{16,24},{24,28},{28,20},{20,12},{12,4},{4,0},{1,9},{9... | collective-permute-start | bytes 2162696 | tf_op jit(solution)/shard_map/ppermute | solution.py:833
  107.9 37.3 %collective-permute-start.17 = (bf16[256,1408]{1,0:T(8,128)(2,1)}, bf16[256,1408]{1,0:T(8,128)(2,1)}, u32[]{:S(2)}, u32[]{:S(2)}) collective-permute-start(bf16[256,1408]{1,0:T(8,128)(2,1)} %refs_2_), channel_id=1, source_target_pairs={{8,0},{16,8},{24,16},{28,24},{20,28},{12,20},{4,12},{0,4},{9,1},{1... | collective-permute-start | bytes 2162696 | tf_op jit(solution)/shard_map/ppermute | solution.py:833
  122.4 40.6 %collective-permute-start.18 = (bf16[256,1408]{1,0:T(8,128)(2,1)}, bf16[256,1408]{1,0:T(8,128)(2,1)}, u32[]{:S(2)}, u32[]{:S(2)}) collective-permute-start(bf16[256,1408]{1,0:T(8,128)(2,1)} %refs_10_), channel_id=1, source_target_pairs={{0,8},{8,16},{16,24},{24,28},{28,20},{20,12},{12,4},{4,0},{1,9},{9... | collective-permute-start | bytes 2162696 | tf_op jit(solution)/shard_map/ppermute | solution.py:833
  123.9 39.1 %collective-permute-start.19 = (bf16[256,1408]{1,0:T(8,128)(2,1)}, bf16[256,1408]{1,0:T(8,128)(2,1)}, u32[]{:S(2)}, u32[]{:S(2)}) collective-permute-start(bf16[256,1408]{1,0:T(8,128)(2,1)} %refs_10_), channel_id=1, source_target_pairs={{8,0},{16,8},{24,16},{28,24},{20,28},{12,20},{4,12},{0,4},{9,1},{1... | collective-permute-start | bytes 2162696 | tf_op jit(solution)/shard_map/ppermute | solution.py:833
  169.8 93.8 %all-gather.9.cloned.1.call-start = ((), (), s32[]{:S(2)}) async-start(), calls=%async_computation.7 | async-start | bytes 5242880 | tf_op jit(solution)/shard_map/all_gather | solution.py:1000
  171.9 28.5 %collective-permute-start.22 = (bf16[256,1408]{1,0:T(8,128)(2,1)}, bf16[256,1408]{1,0:T(8,128)(2,1)S(1)}, u32[]{:S(2)}, u32[]{:S(2)}) collective-permute-start(bf16[256,1408]{1,0:T(8,128)(2,1)} %collective-permute-done.18.refs_15_.refs_17_), channel_id=1, source_target_pairs={{0,8},{8,16},{16,24},{24,28},{28,20},{20,12},{12,4},{4,0},{1,9},{9... | collective-permute-start | bytes 2162696 | tf_op jit(solution)/shard_map/ppermute | solution.py:833
  173.4 28.2 %collective-permute-start.23 = (bf16[256,1408]{1,0:T(8,128)(2,1)}, bf16[256,1408]{1,0:T(8,128)(2,1)S(1)}, u32[]{:S(2)}, u32[]{:S(2)}) collective-permute-start(bf16[256,1408]{1,0:T(8,128)(2,1)} %collective-permute-done.19.refs_9_.refs_11_), channel_id=1, source_target_pairs={{8,0},{16,8},{24,16},{28,24},{20,28},{12,20},{4,12},{0,4},{9,1},{1... | collective-permute-start | bytes 2162696 | tf_op jit(solution)/shard_map/ppermute | solution.py:833
  218.3 201.9 %reduce-scatter.7.cloned.1.call-start = ((), (), s32[]{:S(2)}) async-start(), calls=%async_computation.8 | async-start | bytes 5242880 | tf_op jit(solution)/shard_map/reduce_scatter | solution.py:1003
  220.4 32.6 %collective-permute-start.28 = (bf16[256,1408]{1,0:T(8,128)(2,1)}, bf16[256,1408]{1,0:T(8,128)(2,1)}, u32[]{:S(2)}, u32[]{:S(2)}) collective-permute-start(bf16[256,1408]{1,0:T(8,128)(2,1)} %copy-done.79), channel_id=1, source_target_pairs={{0,8},{8,16},{16,24},{24,28},{28,20},{20,12},{12,4},{4,0},{1,9},{9... | collective-permute-start | bytes 2162696 | tf_op jit(solution)/shard_map/ppermute | solution.py:833
  237.8 40.8 %collective-permute-start.30 = (bf16[128,1408]{1,0:T(8,128)(2,1)}, bf16[128,1408]{1,0:T(8,128)(2,1)}, u32[]{:S(2)}, u32[]{:S(2)}) collective-permute-start(bf16[128,1408]{1,0:T(8,128)(2,1)} %get-tuple-element.500.refs_3_.refs_1_), channel_id=1, source_target_pairs={{0,8},{8,16},{16,24},{24,28},{28,20},{20,12},{12,4},{4,0},{1,9},{9... | collective-permute-start | bytes 1081352 | tf_op jit(solution)/shard_map/ppermute | solution.py:833
  239.3 39.3 %collective-permute-start.31 = (bf16[128,1408]{1,0:T(8,128)(2,1)}, bf16[128,1408]{1,0:T(8,128)(2,1)}, u32[]{:S(2)}, u32[]{:S(2)}) collective-permute-start(bf16[128,1408]{1,0:T(8,128)(2,1)} %get-tuple-element.500.refs_3_.refs_1_), channel_id=1, source_target_pairs={{8,0},{16,8},{24,16},{28,24},{20,28},{12,20},{4,12},{0,4},{9,1},{1... | collective-permute-start | bytes 1081352 | tf_op jit(solution)/shard_map/ppermute | solution.py:833
  239.8 23.8 %collective-permute-start.29 = (bf16[256,1408]{1,0:T(8,128)(2,1)}, bf16[256,1408]{1,0:T(8,128)(2,1)S(1)}, u32[]{:S(2)}, u32[]{:S(2)}) collective-permute-start(bf16[256,1408]{1,0:T(8,128)(2,1)} %collective-permute-done.27.refs_11_.refs_13_), channel_id=1, source_target_pairs={{8,0},{16,8},{24,16},{28,24},{20,28},{12,20},{4,12},{0,4},{9,1},{1... | collective-permute-start | bytes 2162696 | tf_op jit(solution)/shard_map/ppermute | solution.py:833
  312.0 38.2 %collective-permute-start.44 = (bf16[256,1408]{1,0:T(8,128)(2,1)}, bf16[256,1408]{1,0:T(8,128)(2,1)S(1)}, u32[]{:S(2)}, u32[]{:S(2)}) collective-permute-start(bf16[256,1408]{1,0:T(8,128)(2,1)} %get-tuple-element.555), channel_id=1, source_target_pairs={{0,8},{8,16},{16,24},{24,28},{28,20},{20,12},{12,4},{4,0},{1,9},{9... | collective-permute-start | bytes 2162696 | tf_op jit(solution)/shard_map/ppermute | solution.py:833
  313.4 36.7 %collective-permute-start.45 = (bf16[256,1408]{1,0:T(8,128)(2,1)}, bf16[256,1408]{1,0:T(8,128)(2,1)S(1)}, u32[]{:S(2)}, u32[]{:S(2)}) collective-permute-start(bf16[256,1408]{1,0:T(8,128)(2,1)} %get-tuple-element.556), channel_id=1, source_target_pairs={{8,0},{16,8},{24,16},{28,24},{20,28},{12,20},{4,12},{0,4},{9,1},{1... | collective-permute-start | bytes 2162696 | tf_op jit(solution)/shard_map/ppermute | solution.py:833
  375.7 104.8 %all-gather.11.cloned.1.call-start = ((), (), s32[]{:S(2)}) async-start(), calls=%async_computation.9 | async-start | bytes 5242880 | tf_op jit(solution)/shard_map/all_gather | solution.py:1000
  393.0 24.8 %collective-permute-start.50 = (bf16[256,1408]{1,0:T(8,128)(2,1)S(1)}, bf16[256,1408]{1,0:T(8,128)(2,1)S(1)}, u32[]{:S(2)}, u32[]{:S(2)}) collective-permute-start(bf16[256,1408]{1,0:T(8,128)(2,1)S(1)} %get-tuple-element.592), channel_id=1, source_target_pairs={{0,8},{8,16},{16,24},{24,28},{28,20},{20,12},{12,4},{4,0},{1,9},{9... | collective-permute-start | bytes 2162696 | tf_op jit(solution)/shard_map/ppermute | solution.py:833
  394.4 24.9 %collective-permute-start.51 = (bf16[256,1408]{1,0:T(8,128)(2,1)S(1)}, bf16[256,1408]{1,0:T(8,128)(2,1)S(1)}, u32[]{:S(2)}, u32[]{:S(2)}) collective-permute-start(bf16[256,1408]{1,0:T(8,128)(2,1)S(1)} %get-tuple-element.593), channel_id=1, source_target_pairs={{8,0},{16,8},{24,16},{28,24},{20,28},{12,20},{4,12},{0,4},{9,1},{1... | collective-permute-start | bytes 2162696 | tf_op jit(solution)/shard_map/ppermute | solution.py:833
  426.4 117.8 %reduce-scatter.9.cloned.1.call-start = ((), (), s32[]{:S(2)}) async-start(), calls=%async_computation.10 | async-start | bytes 5242880 | tf_op jit(solution)/shard_map/reduce_scatter | solution.py:1003
  436.0 24.4 %collective-permute-start.53 = (bf16[256,1408]{1,0:T(8,128)(2,1)}, bf16[256,1408]{1,0:T(8,128)(2,1)S(1)}, u32[]{:S(2)}, u32[]{:S(2)}) collective-permute-start(bf16[256,1408]{1,0:T(8,128)(2,1)} %get-tuple-element.602), channel_id=1, source_target_pairs={{0,8},{8,16},{16,24},{24,28},{28,20},{20,12},{12,4},{4,0},{1,9},{9... | collective-permute-start | bytes 2162696 | tf_op jit(solution)/shard_map/ppermute | solution.py:833
  436.8 23.6 %collective-permute-start.54 = (bf16[256,1408]{1,0:T(8,128)(2,1)S(1)}, bf16[256,1408]{1,0:T(8,128)(2,1)S(1)}, u32[]{:S(2)}, u32[]{:S(2)}) collective-permute-start(bf16[256,1408]{1,0:T(8,128)(2,1)S(1)} %get-tuple-element.603), channel_id=1, source_target_pairs={{8,0},{16,8},{24,16},{28,24},{20,28},{12,20},{4,12},{0,4},{9,1},{1... | collective-permute-start | bytes 2162696 | tf_op jit(solution)/shard_map/ppermute | solution.py:833
  480.5 190.7 %reduce-scatter.11.cloned.1.call-start = ((), (), s32[]{:S(2)}) async-start(), calls=%async_computation.11 | async-start | bytes 5242880 | tf_op jit(solution)/shard_map/reduce_scatter | solution.py:1003
  499.3 33.5 %collective-permute-start.59 = (bf16[256,1408]{1,0:T(8,128)(2,1)S(1)}, bf16[256,1408]{1,0:T(8,128)(2,1)}, u32[]{:S(2)}, u32[]{:S(2)}) collective-permute-start(bf16[256,1408]{1,0:T(8,128)(2,1)S(1)} %hand_on.28), channel_id=1, source_target_pairs={{8,0},{16,8},{24,16},{28,24},{20,28},{12,20},{4,12},{0,4},{9,1},{1... | collective-permute-start | bytes 2162696 | tf_op jit(solution)/shard_map/ppermute | solution.py:833
  503.8 40.3 %collective-permute-start.60 = (bf16[256,1408]{1,0:T(8,128)(2,1)}, bf16[256,1408]{1,0:T(8,128)(2,1)S(1)}, u32[]{:S(2)}, u32[]{:S(2)}) collective-permute-start(bf16[256,1408]{1,0:T(8,128)(2,1)} %get-tuple-element.641), channel_id=1, source_target_pairs={{0,8},{8,16},{16,24},{24,28},{28,20},{20,12},{12,4},{4,0},{1,9},{9... | collective-permute-start | bytes 2162696 | tf_op jit(solution)/shard_map/ppermute | solution.py:833
  505.8 38.3 %collective-permute-start.61 = (bf16[256,1408]{1,0:T(8,128)(2,1)}, bf16[256,1408]{1,0:T(8,128)(2,1)S(1)}, u32[]{:S(2)}, u32[]{:S(2)}) collective-permute-start(bf16[256,1408]{1,0:T(8,128)(2,1)} %get-tuple-element.642), channel_id=1, source_target_pairs={{8,0},{16,8},{24,16},{28,24},{20,28},{12,20},{4,12},{0,4},{9,1},{1... | collective-permute-start | bytes 2162696 | tf_op jit(solution)/shard_map/ppermute | solution.py:833
  601.9 24.5 %collective-permute-start.67 = (bf16[256,1024]{1,0:T(8,128)(2,1)S(1)}, bf16[256,1024]{1,0:T(8,128)(2,1)S(1)}, u32[]{:S(2)}, u32[]{:S(2)}) collective-permute-start(bf16[256,1024]{1,0:T(8,128)(2,1)S(1)} %copy-done.59), channel_id=1, source_target_pairs={{0,8},{8,16},{16,24},{24,28},{28,20},{20,12},{12,4},{4,0},{1,9},{9... | collective-permute-start | bytes 1572872 | tf_op jit(solution)/shard_map/ppermute | solution.py:833
  (190 other events, 2317.2 us)
Sparse Core Ops, SparseCore 0:
  11.6 36.8 all-gather.4
  50.7 34.4 all-gather.6
  169.9 42.7 reduce-scatter.4
  218.4 34.4 all-gather.8
  375.8 42.0 reduce-scatter.6
  426.5 32.2 all-gather.10
  480.6 45.3 reduce-scatter.8
  587.6 44.4 reduce-scatter.10

commit v3 on v2

--- a/solution.py
+++ b/solution.py
@@ -16,7 +16,7 @@
 BF16 = jnp.bfloat16
 MIB = 2**20
 LIGHT = pl.CostEstimate(flops=10**9, bytes_accessed=1, transcendentals=1)
-LONG = pl.CostEstimate(flops=5 * 10**10, bytes_accessed=1, transcendentals=1)
+LONG = pl.CostEstimate(flops=10**12, bytes_accessed=1, transcendentals=1)
 
 
 def product(left, right, left_dim, right_dim):
@@ -96,6 +96,7 @@
 def backward_body(
     block,
     count,
+    kept,
     q_ref,
     k_ref,
     v_ref,
@@ -106,14 +107,9 @@
     across_ref,
     cos_ref,
     sin_ref,
-    q_grad_ref,
-    k_grad_ref,
-    v_grad_ref,
-    bias_ref,
-    q_total,
-    k_total,
-    v_total,
+    *refs,
 ):
+    q_grad_ref, k_grad_ref, v_grad_ref, bias_ref, q_total, k_total, v_total = refs[kept:]
     lane = lax.broadcasted_iota(jnp.int32, (block, PAIR), 1)
     earlier = lax.broadcasted_iota(jnp.int32, (block, block), 0) <= lax.broadcasted_iota(
         jnp.int32, (block, block), 1
@@ -124,8 +120,8 @@
         upstream = grad_ref[spans[i], :]
         centres = (upstream.astype(F32) * mixed_ref[spans[i], :].astype(F32)).T
         segment = across_ref[:, spans[i]]
-        kept = [down_ref[spans[j], :] == segment for j in range(i + 1)]
-        kept[i] = kept[i] & earlier
+        allowed = [down_ref[spans[j], :] == segment for j in range(i + 1)]
+        allowed[i] = allowed[i] & earlier
         sums = []
         for half in range(2):
             mine = lane < HD if half == 0 else lane >= HD
@@ -137,7 +133,7 @@
             q_sum = None
             for j in range(i + 1):
                 keys = k_ref[spans[j], :]
-                scores = jnp.where(kept[j], product(keys, chosen, 1, 1), NEGATIVE)
+                scores = jnp.where(allowed[j], product(keys, chosen, 1, 1), NEGATIVE)
                 weights = jnp.exp(scores - log_total)
                 weight_grad = product(v_ref[spans[j], :], chosen_grad, 1, 1)
                 score_grad = (weights * (weight_grad - centre)).astype(BF16)
@@ -167,44 +163,49 @@
 
 
 def attend_backward(
-    qk, values, mixed, mixed_grad, lse, segment_down, segment_across, cos_table, sin_table, count
+    qk, values, mixed, mixed_grad, lse, segment_down, segment_across, cos_table, sin_table, count, half, kept
 ):
     length, width = values.shape
     pairs = width // PAIR
-    columns = lambda first: pl.BlockSpec((length, PAIR), lambda h: (0, h + first))
+    kept = list(kept or [])
+    some = pairs // 2
+    start = half * some
+    columns = lambda first: pl.BlockSpec((length, PAIR), lambda h: (0, h + first + start))
     whole = lambda shape: pl.BlockSpec(shape, lambda h: (0, 0))
     return pl.pallas_call(
-        functools.partial(backward_body, length // count, count),
+        functools.partial(backward_body, length // count, count, len(kept)),
         grid_spec=pltpu.PrefetchScalarGridSpec(
             num_scalar_prefetch=0,
-            grid=(pairs,),
+            grid=(some,),
             in_specs=[
                 columns(0),
                 columns(pairs),
                 columns(0),
                 columns(0),
                 columns(0),
-                pl.BlockSpec((1, 2, length), lambda h: (h, 0, 0)),
+                pl.BlockSpec((1, 2, length), lambda h: (h + start, 0, 0)),
                 whole((length, 1)),
                 whole((1, length)),
                 whole((length, PAIR)),
                 whole((length, PAIR)),
-            ],
+            ]
+            + [pl.BlockSpec(memory_space=pl.ANY)] * len(kept),
             out_specs=[
                 columns(0),
                 columns(0),
                 columns(0),
-                pl.BlockSpec((1, 3, PAIR), lambda h: (h, 0, 0)),
+                pl.BlockSpec((1, 3, PAIR), lambda h: (h + start, 0, 0)),
             ],
             scratch_shapes=[pltpu.VMEM((length, PAIR), F32)] * 3,
         ),
         out_shape=[jax.ShapeDtypeStruct((length, width), BF16)] * 3
         + [jax.ShapeDtypeStruct((pairs, 3, PAIR), F32)],
+        input_output_aliases={10 + i: i for i in range(len(kept))},
         compiler_params=pltpu.CompilerParams(vmem_limit_bytes=60 * MIB),
         cost_estimate=LONG,
         name="attend_backward",
     )(
-        qk, qk, values, mixed, mixed_grad, lse, segment_down, segment_across, cos_table, sin_table
+        qk, qk, values, mixed, mixed_grad, lse, segment_down, segment_across, cos_table, sin_table, *kept
     )
 
 
@@ -537,10 +538,12 @@
 STRIPES = 4
 
 
-def outward_body(shape, columns, deep, *refs):
+def outward_body(shape, columns, deep, apart, *refs):
+    if apart:
+        here, refs = refs[0][0], refs[1:]
     lefts, refs = refs[: len(shape)], refs[len(shape) :]
-    out_ref = refs[sum(shape)]
-    weights, semaphores = refs[sum(shape) + 1 : -1], refs[-1]
+    outs = refs[sum(shape) : sum(shape) + 1 + apart]
+    weights, semaphores = refs[sum(shape) + 1 + apart : -1], refs[-1]
     step = pl.program_id(0)
     at, groups = 0, []
     for count, weight, column in zip(shape, weights, columns):
@@ -570,13 +573,26 @@
     for left, weight in zip(lefts, weights):
         term = product(left[...], weight[span, :], 1, 1)
         total = term if total is None else total + term
-    out_ref[...] = total.astype(BF16)
-
-
-def outward(parts, depth, name):
+    if not apart:
+        outs[0][...] = total.astype(BF16)
+        return
+    rows = total.shape[0] // 4
+    for i in range(4):
+        away = jnp.bitwise_xor(here, i)
+        span = pl.ds(pl.multiple_of((1 - away // 2) * rows, rows), rows)
+        values = total[i * rows : (i + 1) * rows].astype(BF16)
+        for other, out_ref in enumerate(outs):
+
+            @pl.when(away % 2 == other)
+            def _():
+                out_ref[span, :] = values
+
+
+def outward(parts, depth, name, place=None):
     lefts = [left for left, _, _ in parts]
     length = lefts[0].shape[0]
     shape = [len(blocks) for _, blocks, _ in parts]
+    tall = (0,) if place is None else (0, 1)
     deep = None
     columns = []
     for left, blocks, column in parts:
@@ -586,12 +602,13 @@
             columns.append(pl.ds(column, left.shape[1]))
             deep = depth // len(blocks)
     return kernel_call(
-        functools.partial(outward_body, shape, columns, deep),
+        functools.partial(outward_body, shape, columns, deep, place is not None),
         name,
         [*lefts, *(block for _, blocks, _ in parts for block in blocks)],
         [whole(left.shape) for left in lefts] + [HBM] * sum(shape),
-        pl.BlockSpec((length, depth // STRIPES), lambda i: (0, i)),
-        shaped((length, depth)),
+        [pl.BlockSpec((length // len(tall), depth // STRIPES), lambda i, *_: (0, i)) for _ in tall],
+        [shaped((length // len(tall), depth)) for _ in tall],
+        scalars=() if place is None else (place,),
         grid=(STRIPES,),
         flops=10**9,
         scratch=[pltpu.VMEM((depth, left.shape[1]), BF16) for left in lefts]
@@ -685,6 +702,27 @@
     return total
 
 
+def meet_body(own_ref, arrived_ref, far_ref, near_ref):
+    rows = far_ref.shape[0]
+    total = own_ref[...].astype(F32) + arrived_ref[...].astype(F32)
+    far_ref[...] = total[:rows].astype(BF16)
+    near_ref[...] = total[rows:]
+
+
+def meet(own, arrived):
+    length, depth = own.shape
+    half = (length // 2, depth)
+    return kernel_call(
+        meet_body,
+        "meet",
+        [own, arrived],
+        [whole(own.shape)] * 2,
+        [whole(half)] * 2,
+        [shaped(half), shaped(half, F32)],
+        grid=(1,),
+    )
+
+
 def second_norm_body(x_ref, term_ref, norm_ref, middle_ref, mean_ref, inverse_ref, out_ref):
     middle = added([x_ref, term_ref])
     middle_ref[...] = middle
@@ -696,13 +734,13 @@
     out_ref[...] = (centred * inverse * norm_ref[2:3, :] + norm_ref[3:4, :]).astype(BF16)
 
 
-def second_norm(inputs, term, norm_rows):
+def second_norm(inputs, terms, norm_rows):
     shape = inputs.shape
     column = (shape[0], 1)
     return kernel_call(
         second_norm_body,
         "second_norm",
-        [inputs, term, norm_rows],
+        [inputs, *terms, norm_rows],
         [whole(shape)] * 2 + [whole(norm_rows.shape)],
         [whole(shape), whole(column), whole(column), whole(shape)],
         [shaped(shape, F32), shaped(column, F32), shaped(column, F32), shaped(shape)],
@@ -720,8 +758,8 @@
     return inverse * inner
 
 
-def second_back_body(upstream_ref, middle_ref, mean_ref, inverse_ref, norm_ref, grad_ref, full_ref, branch_ref, sums_ref):
-    upstream = upstream_ref[...].astype(F32)
+def second_back_body(near_ref, far_ref, middle_ref, mean_ref, inverse_ref, norm_ref, grad_ref, full_ref, branch_ref, sums_ref):
+    upstream = added([near_ref, far_ref])
     inverse = inverse_ref[...]
     standard = (middle_ref[...] - mean_ref[...]) * inverse
     sums_ref[0:1, :] = (upstream * standard).sum(0, keepdims=True)
@@ -731,14 +769,14 @@
     branch_ref[...] = grad.astype(BF16)
 
 
-def second_norm_back(upstream, middle, mean, inverse, norm_rows, grads):
+def second_norm_back(terms, middle, mean, inverse, norm_rows, grads):
     shape = middle.shape
     column = (shape[0], 1)
     return kernel_call(
         second_back_body,
         "second_norm_back",
-        [upstream, middle, mean, inverse, norm_rows, grads],
-        [whole(shape)] * 2 + [whole(column)] * 2 + [whole(norm_rows.shape), whole(shape)],
+        [*terms, middle, mean, inverse, norm_rows, grads],
+        [whole(shape)] * 3 + [whole(column)] * 2 + [whole(norm_rows.shape), whole(shape)],
         [whole(shape), whole(shape), whole((2, shape[1]))],
         [shaped(shape, F32), shaped(shape), shaped((2, shape[1]), F32)],
         grid=(1,),
@@ -805,19 +843,22 @@
 def hand_on(arrived, own, rows, places):
     shape = (rows, sum(part.shape[1] for part in own))
     sides = len(places)
+    half = (rows // 2, shape[1])
+    by_halves = pl.BlockSpec(half, lambda i: (i, 0))
     return kernel_call(
         functools.partial(hand_on_body, len(arrived), sides),
         "hand_on",
         [*arrived, *(part for _ in places for part in own)],
-        [whole(shape)] * len(arrived)
+        [by_halves] * len(arrived)
         + [
-            pl.BlockSpec((rows, part.shape[1]), lambda i, at=at: (at, 0))
+            pl.BlockSpec((rows // 2, part.shape[1]), lambda i, at=at: (2 * at + i, 0))
             for at in places
             for part in own
         ],
-        [whole(shape)] * sides,
+        [by_halves] * sides,
         [shaped(shape)] * sides,
-        grid=(1,),
+        grid=(2,),
+        vmem=60,
     )
 
 
@@ -939,7 +980,7 @@
                 stream.resume(out[at : at + len(group)])
                 at += len(group)
         if not busy:
-            self.token = mark(self.token, 5 * 10**10 if long else 10**9)
+            self.token = mark(self.token, 10**12 if long else 10**9)
             self.token, *carried = lax.optimization_barrier((self.token, *carried))
         return carried[0] if len(carried) == 1 else carried
 
@@ -952,15 +993,10 @@
     return lax.ppermute(values, "tensor", [(i, i ^ 2) for i in range(4)])
 
 
-def spread_over_dp(route, table):
-    left = route.count
-    while left > 1:
-        left //= 2
-        pairs = [
-            (route.ring[i], route.ring[(i + left) % route.count]) for i in range(route.count)
-        ]
-        table = table[:left] + lax.ppermute(table[left:], "dp", pairs)
-    return table[0]
+def halve(route, table):
+    left = table.shape[0] // 2
+    pairs = [(route.ring[i], route.ring[(i + left) % route.count]) for i in range(route.count)]
+    return lax.ppermute(table[left:], "dp", pairs)
 
 
 def on_device(
@@ -990,6 +1026,7 @@
     local_heads = heads_wide // HD
     shards = length // third
     here = lax.axis_index("tensor")
+    place = here.astype(jnp.int32).reshape(1)
     advance = Pace(jnp.zeros((8, 128), jnp.int32) + here)
     device = lax.axis_index("dp").astype(jnp.int32)
     position = jnp.where(device % 2 == 0, device // 2, count - 1 - device // 2)
@@ -1065,8 +1102,8 @@
         [ring_vo], cos_table, sin_table, segment_down, segment_across
     )
     advance([ring_qk], long=True)
-    grad_all = advance([ring_vo, ring_gate], grad_all)
-    advance([ring_qk])
+    grad_all = advance([ring_vo], grad_all)
+    advance([ring_qk, ring_gate])
     advance([ring_vo, ring_up], busy=True)
     blocks_a = ring_qk.all()
     blocks_b = ring_vo.all()
@@ -1077,15 +1114,18 @@
     qk, values = advance([ring_gate], qk, values, busy=True)
     mixed, lse = attend_forward(qk, values, segment_down, segment_across, shards)
     mixed, lse = advance([ring_up], mixed, lse, busy=True)
-    arriving = scatter(outward([(mixed, blocks_b, heads_wide)], depth, "from_heads"))
+    arriving = scatter(outward([(mixed, blocks_b, heads_wide)], depth, "from_heads")[0])
     advance([ring_gate])
     advance([ring_up], long=True)
     arriving = advance([ring_gate], arriving)
-    middle, mean_two, inverse_two, n_own = second_norm(own_bf16, arriving, norm_rows)
+    middle, mean_two, inverse_two, n_own = second_norm(own_bf16, [arriving], norm_rows)
     normed_two = gather(n_own)
-    middle = advance([ring_up, ring_down[0]], middle)
-    advance([ring_gate], long=True)
-    normed_two = advance([ring_up, ring_down[1]], normed_two, busy=True)
+    middle = advance([], middle, long=True)
+    advance([ring_up, ring_down[0]])
+    advance([ring_gate])
+    advance([ring_up, ring_down[1]])
+    advance([ring_down[0]])
+    normed_two = advance([ring_down[1]], normed_two, busy=True)
     gate_blocks = ring_gate.all()
     up_blocks = ring_up.all()
     kept = gated_forward(normed_two, gate_blocks, up_blocks, 0, None)
@@ -1095,66 +1135,77 @@
     gate, up, hidden = advance([ring_down[0]], gate, up, hidden)
     hidden = advance([ring_down[1]], hidden)
     down_sum = product(grad_all, hidden, 0, 0).astype(BF16)
+    sum_down = Summing(route, lambda: [down_sum], width, 1, 0, 0)
     down_sum = advance([ring_down[0]], down_sum)
-    sum_down = Summing(route, lambda: [down_sum], width, 1, 0, 0)
-    advance([ring_down[1], sum_down])
-    advance([ring_down[0]])
-    advance([ring_down[1]], busy=True)
+    advance([ring_down[1], sum_down], busy=True)
     down_blocks = [block for pair in zip(*(ring.all() for ring in ring_down)) for block in pair]
 
     gate_grad, up_grad = gated_backward(grad_all, gate, up, down_blocks)
-    gate_grad, up_grad = advance([sum_down], gate_grad, up_grad, busy=True)
-    arriving = scatter(
-        outward([(gate_grad, gate_blocks, None), (up_grad, up_blocks, None)], depth, "from_gates")
-    )
     gate_grad, up_grad = advance([sum_down], gate_grad, up_grad)
     gate_sum = product(normed_two, gate_grad, 0, 0).astype(BF16)
     sum_gate = Summing(route, lambda: [gate_sum], width, 1, 0, 1)
-    gate_sum, up_grad = advance([sum_gate], gate_sum, up_grad, long=True)
+    gate_sum, gate_grad, up_grad = advance([sum_gate], gate_sum, gate_grad, up_grad, busy=True)
+    own, cross = outward(
+        [(gate_grad, gate_blocks, None), (up_grad, up_blocks, None)], depth, "from_gates", place
+    )
+    own, cross = advance([sum_down], own, cross)
+    own, cross, up_grad = advance([sum_gate], own, cross, up_grad, busy=True)
+    arrived = across_core(cross)
+    own, arrived, up_grad = advance([], own, arrived, up_grad, busy=True)
+    far, near = meet(own, arrived)
+    arriving = across_chip(far)
+    near, up_grad = advance([], near, up_grad)
     up_sum = product(normed_two, up_grad, 0, 0).astype(BF16)
     sum_up = Summing(route, lambda: [up_sum], width, 1, 0, 0)
     up_sum = advance([sum_down], up_sum)
     arriving = advance([sum_gate], arriving)
     middle_grad, b_own, two_sums = second_norm_back(
-        arriving, middle, mean_two, inverse_two, norm_rows, own_grad
+        [near, arriving], middle, mean_two, inverse_two, norm_rows, own_grad
     )
     branch = gather(b_own)
-    hidden = advance([sum_down], hidden, busy=True)
-    result_terms = outward([(hidden, down_blocks, None)], depth, "from_hidden")
-    result_terms = advance([sum_gate, sum_up], result_terms, long=True)
-    branch, result_terms = advance([sum_gate], branch, result_terms, busy=True)
+    hidden, middle_grad = advance([], hidden, middle_grad, long=True)
+    (result_terms,) = outward([(hidden, down_blocks, None)], depth, "from_hidden")
+    result_terms = advance([sum_down, sum_up], result_terms)
+    advance([sum_gate])
+    branch, result_terms = advance([sum_up], branch, result_terms, busy=True)
     arriving_result = scatter(result_terms)
     mixed_grad = through_out(branch, blocks_b)
-    mixed_grad, branch = advance([sum_up], mixed_grad, branch, busy=True)
-    q_grad, k_grad, v_grad, bias_sums = attend_backward(
-        qk,
-        values,
-        mixed,
-        mixed_grad,
-        lse,
-        segment_down,
-        segment_across,
-        cos_table,
-        sin_table,
-        shards,
-    )
-    q_grad, k_grad, v_grad, bias_sums = advance([sum_gate], q_grad, k_grad, v_grad, bias_sums)
+    mixed_grad, branch = advance([sum_gate], mixed_grad, branch, busy=True)
+    grads = None
+    for half in range(2):
+        grads = attend_backward(
+            qk,
+            values,
+            mixed,
+            mixed_grad,
+            lse,
+            segment_down,
+            segment_across,
+            cos_table,
+            sin_table,
+            shards,
+            half,
+            grads,
+        )
+        grads = advance([sum_up], *grads, busy=half == 0)
+    q_grad, k_grad, v_grad, bias_sums = grads
     q_sum = product(normed, q_grad, 0, 0).astype(BF16)
     k_sum = product(normed, k_grad, 0, 0).astype(BF16)
     sum_qk = Summing(route, lambda: [q_sum, k_sum], width, 1, 0, 1)
-    q_sum, k_sum, v_grad, branch, arriving_result = advance(
-        [sum_up, sum_qk], q_sum, k_sum, v_grad, branch, arriving_result
-    )
+    q_sum, k_sum, v_grad, branch = advance([sum_qk], q_sum, k_sum, v_grad, branch)
     out_sum = product(branch, mixed, 0, 0).astype(BF16)
     v_sum = product(normed, v_grad, 0, 0).astype(BF16)
     sum_vo = Summing(route, lambda: [v_sum, out_sum], width, 1, 0, 0)
-    out_sum, v_sum, q_grad = advance([sum_up], out_sum, v_sum, q_grad)
-    q_grad = advance([sum_vo, sum_qk], q_grad, busy=True)
+    out_sum, v_sum, q_grad, arriving_result = advance(
+        [sum_qk, sum_vo], out_sum, v_sum, q_grad, arriving_result, busy=True
+    )
     heads_terms, one_sums = through_heads(
         [q_grad, k_grad, v_grad], x_all, mean_one, inverse_one, blocks_a, blocks_b
     )
     arriving = scatter(heads_terms)
-    one_sums, middle, arriving_result = advance([sum_up], one_sums, middle, arriving_result, long=True)
+    one_sums, middle, arriving_result, down_sum = advance(
+        [sum_up, sum_vo], one_sums, middle, arriving_result, down_sum, long=True
+    )
     norm_grads = jnp.concatenate([one_sums, two_sums], axis=0)
     bias_sums = bias_sums.transpose(1, 0, 2).reshape(3, local_heads, count, HD // count)
     bias_sums = bias_sums.transpose(2, 0, 1, 3).reshape(count, bias_size)[order]
@@ -1164,21 +1215,33 @@
     )
     extras = jnp.pad(extras, ((0, 0), (0, -extras.shape[1] % 128)))
     result = finish_result(order, middle, arriving_result)
+    moved = halve(route, extras)
+    extras, moved, result, down_sum, gate_sum = advance(
+        [sum_qk], extras, moved, result, down_sum, gate_sum
+    )
     grad_down = sum_down.total(down_sum, 0).T
+    extras = extras[: moved.shape[0]] + moved
+    moved = halve(route, extras)
+    extras, moved, grad_down, gate_sum = advance([sum_vo], extras, moved, grad_down, gate_sum)
     grad_gate = sum_gate.total(gate_sum, 0)
-    extras, result, grad_down, grad_gate = advance(
-        [sum_vo, sum_qk], extras, result, grad_down, grad_gate
-    )
-    extras = spread_over_dp(route, extras)
+    extras = extras[: moved.shape[0]] + moved
+    while extras.shape[0] > 2:
+        extras = extras[: extras.shape[0] // 2] + halve(route, extras)
+    moved = halve(route, extras)
+    extras, moved, grad_gate, up_sum = advance([sum_qk], extras, moved, grad_gate, up_sum)
     grad_up = sum_up.total(up_sum, 0)
-    grad_up = advance([sum_vo, sum_qk], grad_up)
-    arriving, extras = advance([sum_vo, sum_qk], arriving, extras)
+    extras = (extras[:1] + moved)[0]
+    bias_grad = extras[4 * width : 4 * width + bias_size].reshape(qkv_bias.shape)
+    norm_sums = extras[: 4 * width].reshape(4, width)
+    moved = across_core(norm_sums)
+    grad_up, moved = advance([sum_vo], grad_up, moved)
+    norm_sums = norm_sums + moved
+    moved = across_chip(norm_sums)
+    moved = advance([sum_qk], moved)
+    norm_sums = norm_sums + moved
+    norm_sums = lax.dynamic_slice_in_dim(norm_sums, here * norm_part, norm_part, axis=1)
+    arriving = advance([], arriving)
     input_grad = input_back(order, arriving, own_bf16, norm_rows, middle_grad)
-    norm_sums = extras[: 4 * width].reshape(4, width)
-    norm_sums = norm_sums + across_core(norm_sums)
-    norm_sums = norm_sums + across_chip(norm_sums)
-    norm_sums = lax.dynamic_slice_in_dim(norm_sums, here * norm_part, norm_part, axis=1)
-    bias_grad = extras[4 * width : 4 * width + bias_size].reshape(qkv_bias.shape)
     input_grad, norm_sums = advance([sum_vo], input_grad, norm_sums)
 
     return (

time: 706 us -> 632 us (0.90)
  waiting for transfers between devices: 270 us -> 181 us
  Pallas kernels: 191 us -> 236 us
  local copies, waits for them, and re-layouts: 72.6 us -> 34.1 us
  matrix products: 38 us -> 48.4 us
    ppermute x77, waiting for transfers between devices: 255 us -> 150 us  [send(): return lax.ppermute(values, 'dp', self.pairs[direction])]
    pallas_call x71 -> x78, Pallas kernels: 146 us -> 188 us  [kernel_call(): pl.pallas_call(body, grid_spec=pltpu.PrefetchScalarGridSpec(num_scalar_pr...]
    unnamed x263 -> x147, local copies, waits for them, and re-layouts: 64.8 us -> 25.7 us
    reduce_scatter x4 -> x3, waiting for transfers between devices: 3.28 us -> 21.5 us  [scatter(): return lax.psum_scatter(values, 'tensor', scatter_dimension=0, tiled=True)]
    dot_general x7, matrix products: 38 us -> 48.4 us  [product(): lax.dot_general(left, right, (((left_dim,), (right_dim,)), ((), ())), pre...]
    pallas_call x1 -> x2, Pallas kernels: 26.7 us -> 29.6 us  [attend_backward(): pl.pallas_call(functools.partial(backward_body, length // count, count, l...]
  transfers between devices with their start and end apart: 92 -> 93, of which waited for: 54 -> 38; matrix products, arithmetic and copies ran while one was open for 9% -> 12% of each run, Pallas kernels for 23% -> 37%
where the time goes in v3:
time: 632 us; the launch traced here: 621 us
  Pallas kernels  236 us (37%)
  waiting for transfers between devices  181 us (29%)
  starting transfers between devices  88.3 us (14%)
  matrix products  48.4 us (8%)
  local copies, waits for them, and re-layouts  34.1 us (5%)
  other arithmetic  18.5 us (3%)
  between operations  15.4 us (2%)
    pallas_call x78, Pallas kernels, kernel_call(): pl.pallas_call(body, grid_spec=pltpu.PrefetchScalarGridSpec(num_scalar_pr...  188 us
    ppermute x77, waiting for transfers between devices, send(): return lax.ppermute(values, 'dp', self.pairs[direction])  150 us
    ppermute x77, starting transfers between devices, send(): return lax.ppermute(values, 'dp', self.pairs[direction])  79.4 us
    dot_general x7, matrix products, product(): lax.dot_general(left, right, (((left_dim,), (right_dim,)), ((), ())), pre...  48.4 us
    pallas_call x2, Pallas kernels, attend_backward(): pl.pallas_call(functools.partial(backward_body, length // count, count, l...  29.6 us
    unnamed x147, local copies, waits for them, and re-layouts  25.7 us
    reduce_scatter x3, waiting for transfers between devices, scatter(): return lax.psum_scatter(values, 'tensor', scatter_dimension=0, tiled=True)  21.5 us
    pallas_call x1, Pallas kernels, attend_forward(): pl.pallas_call(functools.partial(forward_body, length // count, count), g...  17.8 us
  transfers between devices with their start and end apart: 93, of which 38 were waited for; matrix products, arithmetic and copies ran while one was open for 12% of the time, Pallas kernels for 37%

profile of v3, /device:TPU:0, one launch (start us, length us, event | category | flops | bytes accessed | tf_op | source)
XLA Modules:
  0.0 621.2 jit_solution(4485220428421912961)
XLA Ops:
  25.4 8.1 %collective-permute-done.2.refs_7_ = bf16[256,1024]{1,0:T(8,128)(2,1)} collective-permute-done((bf16[256,1024]{1,0:T(8,128)(2,1)}, bf16[256,1024]{1,0:T(8,128)(2,1)}, u32[]{:S(2)}, u32[]{:S(2)}) %collective-permute-start.2) | collective-permute-done | bytes 524320 | tf_op jit(solution)/shard_map/ppermute | solution.py:874
  37.7 7.8 %collective-permute-done.4.refs_7_.refs_15_.refs_8_ = bf16[272,1024]{1,0:T(8,128)(2,1)} collective-permute-done((bf16[272,1024]{1,0:T(8,128)(2,1)}, bf16[272,1024]{1,0:T(8,128)(2,1)}, u32[]{:S(2)}, u32[]{:S(2)}) %collective-permute-start.4) | collective-permute-done | bytes 557088 | tf_op jit(solution)/shard_map/ppermute | solution.py:874
  64.5 8.1 %collective-permute-done.8.refs_6_.refs_14_.refs_7_ = bf16[272,1024]{1,0:T(8,128)(2,1)} collective-permute-done((bf16[272,1024]{1,0:T(8,128)(2,1)}, bf16[272,1024]{1,0:T(8,128)(2,1)}, u32[]{:S(2)}, u32[]{:S(2)}) %collective-permute-start.8) | collective-permute-done | bytes 557088 | tf_op jit(solution)/shard_map/ppermute | solution.py:874
  74.2 7.4 %collective-permute-done.10.refs_5_ = bf16[256,1024]{1,0:T(8,128)(2,1)} collective-permute-done((bf16[256,1024]{1,0:T(8,128)(2,1)S(1)}, bf16[256,1024]{1,0:T(8,128)(2,1)}, u32[]{:S(2)}, u32[]{:S(2)}) %collective-permute-start.10) | collective-permute-done | bytes 524320 | tf_op jit(solution)/shard_map/ppermute | solution.py:874
  86.2 12.3 %collective-permute-done.12.refs_5_.refs_13_.refs_6_ = bf16[272,1024]{1,0:T(8,128)(2,1)} collective-permute-done((bf16[272,1024]{1,0:T(8,128)(2,1)}, bf16[272,1024]{1,0:T(8,128)(2,1)}, u32[]{:S(2)}, u32[]{:S(2)}) %collective-permute-start.12) | collective-permute-done | bytes 557088 | tf_op jit(solution)/shard_map/ppermute | solution.py:874
  99.1 7.3 %collective-permute-done.14.refs_4_ = bf16[256,1024]{1,0:T(8,128)(2,1)} collective-permute-done((bf16[256,1024]{1,0:T(8,128)(2,1)}, bf16[256,1024]{1,0:T(8,128)(2,1)}, u32[]{:S(2)}, u32[]{:S(2)}) %collective-permute-start.14) | collective-permute-done | bytes 524320 | tf_op jit(solution)/shard_map/ppermute | solution.py:874
  108.4 5.5 collective-permute-done.15.refs_4_.refs_12_.refs_5_
  119.8 15.6 %project_qkv.1 = (bf16[1024,1024]{1,0:T(8,128)(2,1)}, bf16[1024,512]{1,0:T(8,128)(2,1)}, bf16[1024,2048]{1,0:T(8,128)(2,1)}) custom-call(bf16[1024,2048]{1,0:T(8,128)(2,1)} %all-gather.5.cloned.1.call-done.x_ref, f32[4,2048]{1,0:T(4,128)} %copy-done.14, f32[1,1536]{1,0:T(1,128)} %copy-done.22, f32[1024,1]{1,0:T(8,128)} %copy-done.4, f32[1024,1]{1,0:T(8,128)} %copy-done.5, ...), custom_call_target="tpu_custom_call" | custom-call | flops 1000000000 | bytes 1 | tf_op jit(solution)/shard_map/project_qkv/pallas_call | solution.py:224
  137.6 17.8 %attend_forward.1 = (bf16[1024,512]{1,0:T(8,128)(2,1)}, f32[4,2,1024]{2,1,0:T(2,128)}) custom-call(bf16[1024,1024]{1,0:T(8,128)(2,1)} %get-tuple-element.523.q_ref.k_ref, bf16[1024,1024]{1,0:T(8,128)(2,1)} %get-tuple-element.523.q_ref.k_ref, bf16[1024,512]{1,0:T(8,128)(2,1)} %get-tuple-element.524.v_ref, s32[1024,1]{1,0:T(8,128)} %copy.53.down_ref, ...), custom_call_target="tpu_custom_call" | custom-call | flops 1000000000 | bytes 1 | tf_op jit(solution)/shard_map/attend_forward/pallas_call | solution.py:78
  162.0 6.6 %from_heads.1 = bf16[1024,2048]{1,0:T(8,128)(2,1)} custom-call(bf16[1024,512]{1,0:T(8,128)(2,1)} %get-tuple-element.538.refs_0_.mixed_ref, bf16[272,1024]{1,0:T(8,128)(2,1)} %fusion.4.refs_0_.refs_8_.refs_1_, bf16[272,1024]{1,0:T(8,128)(2,1)} %collective-permute-done.5.refs_1_.refs_9_.refs_2_, ...), custom_call_target="tpu_custom_call" | custom-call | flops 1000000000 | bytes 1 | tf_op jit(solution)/shard_map/from_heads/pallas_call | solution.py:224
  178.6 10.5 %collective-permute-done.24.refs_5_.refs_8_ = bf16[256,1408]{1,0:T(8,128)(2,1)} collective-permute-done((bf16[256,1408]{1,0:T(8,128)(2,1)}, bf16[256,1408]{1,0:T(8,128)(2,1)}, u32[]{:S(2)}, u32[]{:S(2)}) %collective-permute-start.24) | collective-permute-done | bytes 720928 | tf_op jit(solution)/shard_map/ppermute | solution.py:874
  191.3 21.5 %reduce-scatter.4.cloned.1.call-done.term_ref = bf16[256,2048]{1,0:T(8,128)(2,1)} async-done(((bf16[1024,2048]{1,0:T(8,128)(2,1)}), bf16[256,2048]{1,0:T(8,128)(2,1)}) %reduce-scatter.4.cloned.1.call-update) | async-done | bytes 1048592 | tf_op jit(solution)/shard_map/reduce_scatter | solution.py:1040
  221.6 14.8 %collective-permute-done.28.refs_4_.refs_7_ = bf16[256,1408]{1,0:T(8,128)(2,1)} collective-permute-done((bf16[256,1408]{1,0:T(8,128)(2,1)}, bf16[256,1408]{1,0:T(8,128)(2,1)}, u32[]{:S(2)}, u32[]{:S(2)}) %collective-permute-start.28) | collective-permute-done | bytes 720928 | tf_op jit(solution)/shard_map/ppermute | solution.py:874
  255.6 12.7 %gated_forward.2 = (bf16[1024,1408]{1,0:T(8,128)(2,1)}, bf16[1024,1408]{1,0:T(8,128)(2,1)}, bf16[1024,1408]{1,0:T(8,128)(2,1)}) custom-call(bf16[1024,2048]{1,0:T(8,128)(2,1)} %all-gather.9.cloned.1.call-done.x_ref, bf16[256,1408]{1,0:T(8,128)(2,1)} %refs_3_, bf16[256,1408]{1,0:T(8,128)(2,1)} %copy-done.28, ...), custom_call_target="tpu_custom_call" | custom-call | flops 1000000000 | bytes 1 | tf_op jit(solution)/shard_map/gated_forward/pallas_call | solution.py:224
  272.5 12.7 %gated_forward.3 = (bf16[1024,1408]{1,0:T(8,128)(2,1)}, bf16[1024,1408]{1,0:T(8,128)(2,1)}, bf16[1024,1408]{1,0:T(8,128)(2,1)}) custom-call(bf16[1024,2048]{1,0:T(8,128)(2,1)} %all-gather.9.cloned.1.call-done.x_ref, bf16[256,1408]{1,0:T(8,128)(2,1)} %refs_3_, ...), custom_call_target="tpu_custom_call", output_to_operand_aliasing={{0}: (17, {}), {1}: (18, {}), {2}: (19, {})} | custom-call | flops 1000000000 | bytes 1 | tf_op jit(solution)/shard_map/gated_forward/pallas_call | solution.py:224
  288.4 8.7 %convolution_convert_fusion.2.refs_0_.refs_1_.refs_2_.refs_3_ = bf16[2048,1408]{1,0:T(8,128)(2,1)} fusion(bf16[1024,2048]{1,0:T(8,128)(2,1)S(1)} %copy-done.33, bf16[1024,1408]{1,0:T(8,128)(2,1)S(1)} %copy-done.24), kind=kOutput, calls=%fused_computation.3 | convolution fusion | flops 5908463616 | bytes 12845056 | tf_op jit(solution)/shard_map/dot_general | solution.py:23
  302.1 16.3 %gated_backward.1 = (bf16[1024,1408]{1,0:T(8,128)(2,1)}, bf16[1024,1408]{1,0:T(8,128)(2,1)}) custom-call(bf16[1024,2048]{1,0:T(8,128)(2,1)} %all-gather.7.cloned.1.call-done.refs_0_, bf16[1024,1408]{1,0:T(8,128)(2,1)} %get-tuple-element.613.refs_1_, bf16[1024,1408]{1,0:T(8,128)(2,1)} %get-tuple-element.614.refs_2_, ...), custom_call_target="tpu_custom_call" | custom-call | flops 1000000000 | bytes 1 | tf_op jit(solution)/shard_map/gated_backward/pallas_call | solution.py:224
  323.2 11.0 %convolution_convert_fusion.1.refs_0_.refs_1_.refs_2_.refs_3_ = bf16[2048,1408]{1,0:T(8,128)(2,1)} fusion(bf16[1024,2048]{1,0:T(8,128)(2,1)} %all-gather.9.cloned.1.call-done.x_ref, bf16[1024,1408]{1,0:T(8,128)(2,1)} %get-tuple-element.634.refs_1_), kind=kOutput, calls=%fused_computation.2 | convolution fusion | flops 5908463616 | bytes 12845056 | tf_op jit(solution)/shard_map/dot_general | solution.py:23
  338.6 20.1 %from_gates.1 = (bf16[512,2048]{1,0:T(8,128)(2,1)}, bf16[512,2048]{1,0:T(8,128)(2,1)}) custom-call(s32[1]{0:T(128)} %bitcast.14.refs_0_, bf16[1024,1408]{1,0:T(8,128)(2,1)} %get-tuple-element.634.refs_1_, bf16[1024,1408]{1,0:T(8,128)(2,1)} %get-tuple-element.663.refs_2_, bf16[256,1408]{1,0:T(8,128)(2,1)} %refs_3_, bf16[256,1408]{1,0:T(8,128)(2,1)} %copy-done.28, ...), custom_call_target="tpu_custom_call" | custom-call | flops 1000000000 | bytes 1 | tf_op jit(solution)/shard_map/from_gates/pallas_call | solution.py:224
  376.3 8.5 %convolution_convert_fusion.refs_0_.refs_1_.refs_2_.refs_3_ = bf16[2048,1408]{1,0:T(8,128)(2,1)} fusion(bf16[1024,2048]{1,0:T(8,128)(2,1)S(1)} %copy-done.23, bf16[1024,1408]{1,0:T(8,128)(2,1)S(1)} %copy-done.36), kind=kOutput, calls=%fused_computation.1 | convolution fusion | flops 5908463616 | bytes 12845056 | tf_op jit(solution)/shard_map/dot_general | solution.py:23
  390.7 6.4 %collective-permute-done.53.refs_0_ = bf16[256,1408]{1,0:T(8,128)(2,1)} collective-permute-done((bf16[256,1408]{1,0:T(8,128)(2,1)}, bf16[256,1408]{1,0:T(8,128)(2,1)}, u32[]{:S(2)}, u32[]{:S(2)}) %collective-permute-start.53) | collective-permute-done | bytes 720928 | tf_op jit(solution)/shard_map/ppermute | solution.py:874
  407.5 11.8 %from_hidden.1 = bf16[1024,2048]{1,0:T(8,128)(2,1)} custom-call(bf16[1024,1408]{1,0:T(8,128)(2,1)} %get-tuple-element.690.refs_0_, bf16[128,1408]{1,0:T(8,128)(2,1)} %get-tuple-element.555.refs_3_.refs_1_, bf16[128,1408]{1,0:T(8,128)(2,1)} %get-tuple-element.557.refs_4_.refs_2_, bf16[128,1408]{1,0:T(8,128)(2,1)} %collective-permute-done.31.refs_5_.refs_3_, ...), custom_call_target="tpu_custom_call" | custom-call | flops 1000000000 | bytes 1 | tf_op jit(solution)/shard_map/from_hidden/pallas_call | solution.py:224
  421.4 6.6 %collective-permute-done.57 = bf16[256,1408]{1,0:T(8,128)(2,1)} collective-permute-done((bf16[256,1408]{1,0:T(8,128)(2,1)}, bf16[256,1408]{1,0:T(8,128)(2,1)}, u32[]{:S(2)}, u32[]{:S(2)}) %collective-permute-start.57) | collective-permute-done | bytes 720928 | tf_op jit(solution)/shard_map/ppermute | solution.py:874
  430.7 11.6 %collective-permute-done.59.refs_0_ = bf16[256,1408]{1,0:T(8,128)(2,1)} collective-permute-done((bf16[256,1408]{1,0:T(8,128)(2,1)}, bf16[256,1408]{1,0:T(8,128)(2,1)}, u32[]{:S(2)}, u32[]{:S(2)}) %collective-permute-start.59) | collective-permute-done | bytes 720928 | tf_op jit(solution)/shard_map/ppermute | solution.py:874
  442.2 7.1 %through_out.1.grad_ref = bf16[1024,512]{1,0:T(8,128)(2,1)} custom-call(bf16[1024,2048]{1,0:T(8,128)(2,1)} %all-gather.11.cloned.1.call-done.rows_ref, bf16[272,1024]{1,0:T(8,128)(2,1)} %fusion.4.refs_0_.refs_8_.refs_1_, bf16[272,1024]{1,0:T(8,128)(2,1)} %collective-permute-done.5.refs_1_.refs_9_.refs_2_, ...), custom_call_target="tpu_custom_call" | custom-call | flops 1000000000 | bytes 1 | tf_op jit(solution)/shard_map/through_out/pallas_call | solution.py:224
  449.4 4.4 collective-permute-done.61
  459.3 14.8 %attend_backward.2 = (bf16[1024,512]{1,0:T(8,128)(2,1)}, bf16[1024,512]{1,0:T(8,128)(2,1)}, bf16[1024,512]{1,0:T(8,128)(2,1)}, f32[4,3,128]{2,1,0:T(4,128)}) custom-call(bf16[1024,1024]{1,0:T(8,128)(2,1)} %get-tuple-element.523.q_ref.k_ref, bf16[1024,1024]{1,0:T(8,128)(2,1)} %get-tuple-element.523.q_ref.k_ref, bf16[1024,512]{1,0:T(8,128)(2,1)} %get-tuple-element.524.v_ref, ...), custom_call_target="tpu_custom_call" | custom-call | flops 999999995904 | bytes 1 | tf_op jit(solution)/shard_map/attend_backward/pallas_call | solution.py:175
  479.8 14.8 %attend_backward.3 = (bf16[1024,512]{1,0:T(8,128)(2,1)}, bf16[1024,512]{1,0:T(8,128)(2,1)}, bf16[1024,512]{1,0:T(8,128)(2,1)}, f32[4,3,128]{2,1,0:T(4,128)}) custom-call(bf16[1024,1024]{1,0:T(8,128)(2,1)} %get-tuple-element.523.q_ref.k_ref, ...), custom_call_target="tpu_custom_call", output_to_operand_aliasing={{0}: (10, {}), {1}: (11, {}), {2}: (12, {}), {3}: (13, {})} | custom-call | flops 999999995904 | bytes 1 | tf_op jit(solution)/shard_map/attend_backward/pallas_call | solution.py:175
  495.9 6.1 convolution_convert_fusion.6.refs_0_.refs_2_.refs_4_.refs_1_
  513.2 6.6 %convolution_convert_fusion.4.refs_0_.refs_2_.refs_4_.refs_1_ = bf16[2048,512]{1,0:T(8,128)(2,1)} fusion(bf16[1024,2048]{1,0:T(8,128)(2,1)} %get-tuple-element.736, bf16[1024,512]{1,0:T(8,128)(2,1)} %get-tuple-element.751.v_ref), kind=kOutput, calls=%fused_computation.6 | convolution fusion | flops 2148532224 | bytes 7340032 | tf_op jit(solution)/shard_map/dot_general | solution.py:23
  533.6 13.0 %through_heads.1 = (bf16[1024,2048]{1,0:T(8,128)(2,1)}, f32[2,2048]{1,0:T(2,128)}) custom-call(bf16[1024,512]{1,0:T(8,128)(2,1)} %get-tuple-element.760.q_ref, bf16[1024,512]{1,0:T(8,128)(2,1)} %get-tuple-element.738.k_ref, bf16[1024,512]{1,0:T(8,128)(2,1)} %get-tuple-element.751.v_ref, bf16[1024,2048]{1,0:T(8,128)(2,1)} %all-gather.5.cloned.1.call-done.x_ref, ...), custom_call_target="tpu_custom_call" | custom-call | flops 1000000000 | bytes 1 | tf_op jit(solution)/shard_map/through_heads/pallas_call | solution.py:224
  596.2 4.6 collective-permute-done.83
  (448 shorter events, 264.8 us)
Async XLA Ops:
  7.2 41.8 %all-gather.5.cloned.1.call-start = ((), (), s32[]{:S(2)}) async-start(), calls=%async_computation.3 | async-start | bytes 5242880 | tf_op jit(solution)/shard_map/all_gather | solution.py:1037
  12.0 86.6 %all-gather.7.cloned.1.call-start = ((), (), s32[]{:S(2)}) async-start(), calls=%async_computation.4 | async-start | bytes 5242880 | tf_op jit(solution)/shard_map/all_gather | solution.py:1037
  20.4 25.0 %collective-permute-start.4 = (bf16[272,1024]{1,0:T(8,128)(2,1)}, bf16[272,1024]{1,0:T(8,128)(2,1)}, u32[]{:S(2)}, u32[]{:S(2)}) collective-permute-start(bf16[272,1024]{1,0:T(8,128)(2,1)} %fusion.4.refs_0_.refs_8_.refs_1_), channel_id=1, source_target_pairs={{0,8},{8,16},{16,24},{24,28},{28,20},{20,12},{12,4},{4,0},{1,9},{9... | collective-permute-start | bytes 1671176 | tf_op jit(solution)/shard_map/ppermute | solution.py:874
  22.5 25.1 %collective-permute-start.5 = (bf16[272,1024]{1,0:T(8,128)(2,1)}, bf16[272,1024]{1,0:T(8,128)(2,1)}, u32[]{:S(2)}, u32[]{:S(2)}) collective-permute-start(bf16[272,1024]{1,0:T(8,128)(2,1)} %fusion.4.refs_0_.refs_8_.refs_1_), channel_id=1, source_target_pairs={{8,0},{16,8},{24,16},{28,24},{20,28},{12,20},{4,12},{0,4},{9,1},{1... | collective-permute-start | bytes 1671176 | tf_op jit(solution)/shard_map/ppermute | solution.py:874
  60.8 152.0 %reduce-scatter.4.cloned.1.call-start = ((), (), s32[]{:S(2)}) async-start(), calls=%async_computation.5 | async-start | bytes 5242880 | tf_op jit(solution)/shard_map/reduce_scatter | solution.py:1040
  106.4 29.0 %collective-permute-start.16 = (bf16[256,1408]{1,0:T(8,128)(2,1)S(1)}, bf16[256,1408]{1,0:T(8,128)(2,1)S(1)}, u32[]{:S(2)}, u32[]{:S(2)}) collective-permute-start(bf16[256,1408]{1,0:T(8,128)(2,1)S(1)} %copy-done.25), channel_id=1, source_target_pairs={{0,8},{8,16},{16,24},{24,28},{28,20},{20,12},{12,4},{4,0},{1,9},{9... | collective-permute-start | bytes 2162696 | tf_op jit(solution)/shard_map/ppermute | solution.py:874
  108.4 27.1 %collective-permute-start.17 = (bf16[256,1408]{1,0:T(8,128)(2,1)S(1)}, bf16[256,1408]{1,0:T(8,128)(2,1)S(1)}, u32[]{:S(2)}, u32[]{:S(2)}) collective-permute-start(bf16[256,1408]{1,0:T(8,128)(2,1)S(1)} %copy-done.25), channel_id=1, source_target_pairs={{8,0},{16,8},{24,16},{28,24},{20,28},{12,20},{4,12},{0,4},{9,1},{1... | collective-permute-start | bytes 2162696 | tf_op jit(solution)/shard_map/ppermute | solution.py:874
  113.9 41.5 %collective-permute-start.18 = (bf16[256,1408]{1,0:T(8,128)(2,1)S(1)}, bf16[256,1408]{1,0:T(8,128)(2,1)}, u32[]{:S(2)}, u32[]{:S(2)}) collective-permute-start(bf16[256,1408]{1,0:T(8,128)(2,1)S(1)} %copy-done.26), channel_id=1, source_target_pairs={{0,8},{8,16},{16,24},{24,28},{28,20},{20,12},{12,4},{4,0},{1,9},{9... | collective-permute-start | bytes 2162696 | tf_op jit(solution)/shard_map/ppermute | solution.py:874
  114.4 41.0 %collective-permute-start.19 = (bf16[256,1408]{1,0:T(8,128)(2,1)S(1)}, bf16[256,1408]{1,0:T(8,128)(2,1)}, u32[]{:S(2)}, u32[]{:S(2)}) collective-permute-start(bf16[256,1408]{1,0:T(8,128)(2,1)S(1)} %copy-done.26), channel_id=1, source_target_pairs={{8,0},{16,8},{24,16},{28,24},{20,28},{12,20},{4,12},{0,4},{9,1},{1... | collective-permute-start | bytes 2162696 | tf_op jit(solution)/shard_map/ppermute | solution.py:874
  135.5 33.2 %collective-permute-start.20 = (bf16[256,1408]{1,0:T(8,128)(2,1)S(1)}, bf16[256,1408]{1,0:T(8,128)(2,1)}, u32[]{:S(2)}, u32[]{:S(2)}) collective-permute-start(bf16[256,1408]{1,0:T(8,128)(2,1)S(1)} %collective-permute-done.16.refs_7_.refs_10_), channel_id=1, source_target_pairs={{0,8},{8,16},{16,24},{24,28},{28,20},{20,12},{12,4},{4,0},{1,9},{9... | collective-permute-start | bytes 2162696 | tf_op jit(solution)/shard_map/ppermute | solution.py:874
  136.0 32.7 %collective-permute-start.21 = (bf16[256,1408]{1,0:T(8,128)(2,1)S(1)}, bf16[256,1408]{1,0:T(8,128)(2,1)}, u32[]{:S(2)}, u32[]{:S(2)}) collective-permute-start(bf16[256,1408]{1,0:T(8,128)(2,1)S(1)} %collective-permute-done.17.refs_1_.refs_4_), channel_id=1, source_target_pairs={{8,0},{16,8},{24,16},{28,24},{20,28},{12,20},{4,12},{0,4},{9,1},{1... | collective-permute-start | bytes 2162696 | tf_op jit(solution)/shard_map/ppermute | solution.py:874
  168.7 84.9 %all-gather.9.cloned.1.call-start = ((), (), s32[]{:S(2)}) async-start(), calls=%async_computation.6 | async-start | bytes 5242880 | tf_op jit(solution)/shard_map/all_gather | solution.py:1037
  176.6 42.0 %collective-permute-start.26 = (bf16[256,1408]{1,0:T(8,128)(2,1)}, bf16[256,1408]{1,0:T(8,128)(2,1)}, u32[]{:S(2)}, u32[]{:S(2)}) collective-permute-start(bf16[256,1408]{1,0:T(8,128)(2,1)} %copy-done.29), channel_id=1, source_target_pairs={{0,8},{8,16},{16,24},{24,28},{28,20},{20,12},{12,4},{4,0},{1,9},{9... | collective-permute-start | bytes 2162696 | tf_op jit(solution)/shard_map/ppermute | solution.py:874
  177.8 40.8 %collective-permute-start.27 = (bf16[256,1408]{1,0:T(8,128)(2,1)}, bf16[256,1408]{1,0:T(8,128)(2,1)}, u32[]{:S(2)}, u32[]{:S(2)}) collective-permute-start(bf16[256,1408]{1,0:T(8,128)(2,1)} %copy-done.30), channel_id=1, source_target_pairs={{8,0},{16,8},{24,16},{28,24},{20,28},{12,20},{4,12},{0,4},{9,1},{1... | collective-permute-start | bytes 2162696 | tf_op jit(solution)/shard_map/ppermute | solution.py:874
  218.6 223.7 %all-gather.11.cloned.1.call-start = ((), (), s32[]{:S(2)}) async-start(), calls=%async_computation.7 | async-start | bytes 5242880 | tf_op jit(solution)/shard_map/all_gather | solution.py:1037
  219.6 24.5 %collective-permute-start.30 = (bf16[128,1408]{1,0:T(8,128)(2,1)S(1)}, bf16[128,1408]{1,0:T(8,128)(2,1)}, u32[]{:S(2)}, u32[]{:S(2)}) collective-permute-start(bf16[128,1408]{1,0:T(8,128)(2,1)S(1)} %copy-done.35), channel_id=1, source_target_pairs={{0,8},{8,16},{16,24},{24,28},{28,20},{20,12},{12,4},{4,0},{1,9},{9... | collective-permute-start | bytes 1081352 | tf_op jit(solution)/shard_map/ppermute | solution.py:874
  221.1 24.7 %collective-permute-start.31 = (bf16[128,1408]{1,0:T(8,128)(2,1)S(1)}, bf16[128,1408]{1,0:T(8,128)(2,1)}, u32[]{:S(2)}, u32[]{:S(2)}) collective-permute-start(bf16[128,1408]{1,0:T(8,128)(2,1)S(1)} %copy-done.35), channel_id=1, source_target_pairs={{8,0},{16,8},{24,16},{28,24},{20,28},{12,20},{4,12},{0,4},{9,1},{1... | collective-permute-start | bytes 1081352 | tf_op jit(solution)/shard_map/ppermute | solution.py:874
  321.2 37.5 %collective-permute-start.46 = (bf16[256,1408]{1,0:T(8,128)(2,1)}, bf16[256,1408]{1,0:T(8,128)(2,1)S(1)}, u32[]{:S(2)}, u32[]{:S(2)}) collective-permute-start(bf16[256,1408]{1,0:T(8,128)(2,1)} %get-tuple-element.632), channel_id=1, source_target_pairs={{0,8},{8,16},{16,24},{24,28},{28,20},{20,12},{12,4},{4,0},{1,9},{9... | collective-permute-start | bytes 2162696 | tf_op jit(solution)/shard_map/ppermute | solution.py:874
  322.7 36.1 %collective-permute-start.47 = (bf16[256,1408]{1,0:T(8,128)(2,1)}, bf16[256,1408]{1,0:T(8,128)(2,1)}, u32[]{:S(2)}, u32[]{:S(2)}) collective-permute-start(bf16[256,1408]{1,0:T(8,128)(2,1)} %get-tuple-element.633), channel_id=1, source_target_pairs={{8,0},{16,8},{24,16},{28,24},{20,28},{12,20},{4,12},{0,4},{9,1},{1... | collective-permute-start | bytes 2162696 | tf_op jit(solution)/shard_map/ppermute | solution.py:874
  367.0 30.1 %collective-permute-start.53 = (bf16[256,1408]{1,0:T(8,128)(2,1)}, bf16[256,1408]{1,0:T(8,128)(2,1)}, u32[]{:S(2)}, u32[]{:S(2)}) collective-permute-start(bf16[256,1408]{1,0:T(8,128)(2,1)} %get-tuple-element.670), channel_id=1, source_target_pairs={{0,8},{8,16},{16,24},{24,28},{28,20},{20,12},{12,4},{4,0},{1,9},{9... | collective-permute-start | bytes 2162696 | tf_op jit(solution)/shard_map/ppermute | solution.py:874
  368.5 28.6 %collective-permute-start.54 = (bf16[256,1408]{1,0:T(8,128)(2,1)}, bf16[256,1408]{1,0:T(8,128)(2,1)}, u32[]{:S(2)}, u32[]{:S(2)}) collective-permute-start(bf16[256,1408]{1,0:T(8,128)(2,1)} %get-tuple-element.671), channel_id=1, source_target_pairs={{8,0},{16,8},{24,16},{28,24},{20,28},{12,20},{4,12},{0,4},{9,1},{1... | collective-permute-start | bytes 2162696 | tf_op jit(solution)/shard_map/ppermute | solution.py:874
  373.7 23.9 %collective-permute-start.55 = (bf16[256,2048]{1,0:T(8,128)(2,1)}, bf16[256,2048]{1,0:T(8,128)(2,1)S(1)}, u32[]{:S(2)}, u32[]{:S(2)}) collective-permute-start(bf16[256,2048]{1,0:T(8,128)(2,1)} %get-tuple-element.672), channel_id=1, source_target_pairs={{0,2},{1,3},{2,0},{3,1},{4,6},{5,7},{6,4},{7,5},{8,10},{9,11},{10,... | collective-permute-start | bytes 3145736 | tf_op jit(solution)/shard_map/ppermute | solution.py:993
  387.0 32.3 %collective-permute-start.56 = (bf16[256,1408]{1,0:T(8,128)(2,1)}, bf16[256,1408]{1,0:T(8,128)(2,1)}, u32[]{:S(2)}, u32[]{:S(2)}) collective-permute-start(bf16[256,1408]{1,0:T(8,128)(2,1)} %hand_on.25), channel_id=1, source_target_pairs={{0,8},{8,16},{16,24},{24,28},{28,20},{20,12},{12,4},{4,0},{1,9},{9... | collective-permute-start | bytes 2162696 | tf_op jit(solution)/shard_map/ppermute | solution.py:874
  407.4 118.3 %reduce-scatter.6.cloned.1.call-start = ((), (), s32[]{:S(2)}) async-start(), calls=%async_computation.8 | async-start | bytes 5242880 | tf_op jit(solution)/shard_map/reduce_scatter | solution.py:1040
  419.3 22.9 %collective-permute-start.59 = (bf16[256,1408]{1,0:T(8,128)(2,1)}, bf16[256,1408]{1,0:T(8,128)(2,1)}, u32[]{:S(2)}, u32[]{:S(2)}) collective-permute-start(bf16[256,1408]{1,0:T(8,128)(2,1)} %get-tuple-element.699), channel_id=1, source_target_pairs={{0,8},{8,16},{16,24},{24,28},{28,20},{20,12},{12,4},{4,0},{1,9},{9... | collective-permute-start | bytes 2162696 | tf_op jit(solution)/shard_map/ppermute | solution.py:874
  430.1 23.6 %collective-permute-start.61 = (bf16[256,1408]{1,0:T(8,128)(2,1)}, bf16[256,1408]{1,0:T(8,128)(2,1)S(1)}, u32[]{:S(2)}, u32[]{:S(2)}) collective-permute-start(bf16[256,1408]{1,0:T(8,128)(2,1)} %hand_on.28), channel_id=1, source_target_pairs={{8,0},{16,8},{24,16},{28,24},{20,28},{12,20},{4,12},{0,4},{9,1},{1... | collective-permute-start | bytes 2162696 | tf_op jit(solution)/shard_map/ppermute | solution.py:874
  458.8 145.3 %reduce-scatter.8.cloned.1.call-start = ((), (), s32[]{:S(2)}) async-start(), calls=%async_computation.9 | async-start | bytes 5242880 | tf_op jit(solution)/shard_map/reduce_scatter | solution.py:1040
  512.0 34.6 %collective-permute-start.68 = (bf16[256,1408]{1,0:T(8,128)(2,1)}, bf16[256,1408]{1,0:T(8,128)(2,1)}, u32[]{:S(2)}, u32[]{:S(2)}) collective-permute-start(bf16[256,1408]{1,0:T(8,128)(2,1)} %hand_on.33), channel_id=1, source_target_pairs={{0,8},{8,16},{16,24},{24,28},{28,20},{20,12},{12,4},{4,0},{1,9},{9... | collective-permute-start | bytes 2162696 | tf_op jit(solution)/shard_map/ppermute | solution.py:874
  525.7 23.9 %collective-permute-start.69 = (bf16[256,1024]{1,0:T(8,128)(2,1)}, bf16[256,1024]{1,0:T(8,128)(2,1)S(1)}, u32[]{:S(2)}, u32[]{:S(2)}) collective-permute-start(bf16[256,1024]{1,0:T(8,128)(2,1)} %get-tuple-element.758), channel_id=1, source_target_pairs={{0,8},{8,16},{16,24},{24,28},{28,20},{20,12},{12,4},{4,0},{1,9},{9... | collective-permute-start | bytes 1572872 | tf_op jit(solution)/shard_map/ppermute | solution.py:874
  526.7 22.9 %collective-permute-start.70 = (bf16[256,1024]{1,0:T(8,128)(2,1)}, bf16[256,1024]{1,0:T(8,128)(2,1)S(1)}, u32[]{:S(2)}, u32[]{:S(2)}) collective-permute-start(bf16[256,1024]{1,0:T(8,128)(2,1)} %get-tuple-element.759), channel_id=1, source_target_pairs={{8,0},{16,8},{24,16},{28,24},{20,28},{12,20},{4,12},{0,4},{9,1},{1... | collective-permute-start | bytes 1572872 | tf_op jit(solution)/shard_map/ppermute | solution.py:874
  531.6 29.8 %collective-permute-start.71 = (bf16[256,1024]{1,0:T(8,128)(2,1)}, bf16[256,1024]{1,0:T(8,128)(2,1)}, u32[]{:S(2)}, u32[]{:S(2)}) collective-permute-start(bf16[256,1024]{1,0:T(8,128)(2,1)} %get-tuple-element.773), channel_id=1, source_target_pairs={{0,8},{8,16},{16,24},{24,28},{28,20},{20,12},{12,4},{4,0},{1,9},{9... | collective-permute-start | bytes 1572872 | tf_op jit(solution)/shard_map/ppermute | solution.py:874
  532.6 28.8 %collective-permute-start.72 = (bf16[256,1024]{1,0:T(8,128)(2,1)}, bf16[256,1024]{1,0:T(8,128)(2,1)}, u32[]{:S(2)}, u32[]{:S(2)}) collective-permute-start(bf16[256,1024]{1,0:T(8,128)(2,1)} %get-tuple-element.774), channel_id=1, source_target_pairs={{8,0},{16,8},{24,16},{28,24},{20,28},{12,20},{4,12},{0,4},{9,1},{1... | collective-permute-start | bytes 1572872 | tf_op jit(solution)/shard_map/ppermute | solution.py:874
  (133 other events, 1433.2 us)
Sparse Core Ops, SparseCore 0:
  12.1 36.8 all-gather.4
  60.9 34.7 all-gather.6
  168.8 43.9 reduce-scatter.3
  218.7 33.5 all-gather.8
  407.5 33.5 all-gather.10
  458.9 42.4 reduce-scatter.5
  546.8 41.6 reduce-scatter.7

commit v4 on v3

--- a/solution.py
+++ b/solution.py
@@ -36,37 +36,38 @@
 
 def forward_body(block, count, q_ref, k_ref, v_ref, down_ref, across_ref, mixed_ref, lse_ref):
     lane = lax.broadcasted_iota(jnp.int32, (block, PAIR), 1)
-    earlier = lax.broadcasted_iota(jnp.int32, (block, block), 0) <= lax.broadcasted_iota(
-        jnp.int32, (block, block), 1
+    earlier = lax.broadcasted_iota(jnp.int32, (block, block), 1) <= lax.broadcasted_iota(
+        jnp.int32, (block, block), 0
     )
     spans = [pl.ds(i * block, block) for i in range(count)]
     for i in range(count):
         queries = q_ref[spans[i], :] * jnp.asarray(HD**-0.5, BF16)
-        segment = across_ref[:, spans[i]]
-        kept = [down_ref[spans[j], :] == segment for j in range(i + 1)]
+        segment = down_ref[spans[i], :]
+        kept = [across_ref[:, spans[j]] == segment for j in range(i + 1)]
         kept[i] = kept[i] & earlier
         sums = []
         for half in range(2):
             mine = lane < HD if half == 0 else lane >= HD
             chosen = jnp.where(mine, queries, jnp.zeros_like(queries))
             scores = [
-                jnp.where(kept[j], product(k_ref[spans[j], :], chosen, 1, 1), NEGATIVE)
+                jnp.where(kept[j], product(chosen, k_ref[spans[j], :], 1, 1), NEGATIVE)
                 for j in range(i + 1)
             ]
-            top = scores[0].max(0, keepdims=True)
+            tops = scores[0]
             for part in scores[1:]:
-                top = jnp.maximum(top, part.max(0, keepdims=True))
-            raised = [jnp.exp(part - top) for part in scores]
-            total = raised[0].sum(0, keepdims=True)
-            for part in raised[1:]:
-                total = total + part.sum(0, keepdims=True)
-            inverse = 1.0 / total
+                tops = jnp.maximum(tops, part)
+            top = tops.max(1, keepdims=True)
             out = None
             for j in range(i + 1):
-                term = product((raised[j] * inverse).astype(BF16), v_ref[spans[j], :], 0, 0)
+                values = v_ref[spans[j], :]
+                beside = jnp.where(mine, values, jnp.ones_like(values))
+                term = product(jnp.exp(scores[j] - top).astype(BF16), beside, 1, 0)
                 out = term if out is None else out + term
-            sums.append(out)
-            lse_ref[0, half : half + 1, spans[i]] = top + jnp.log(total)
+            other = slice(HD, HD + 1) if half == 0 else slice(0, 1)
+            total = out[:, other]
+            sums.append(out * (1.0 / total))
+            lse = jnp.broadcast_to(top + jnp.log(total), (block, PAIR))
+            lse_ref[0, half : half + 1, spans[i]] = lse.T[0:1, :]
         mixed_ref[spans[i], :] = jnp.where(lane < HD, sums[0], sums[1]).astype(BF16)
 
 
@@ -115,6 +116,7 @@
         jnp.int32, (block, block), 1
     )
     spans = [pl.ds(i * block, block) for i in range(count)]
+    turned = [k_ref[span, :].T for span in spans]
     for i in range(count):
         queries = q_ref[spans[i], :] * jnp.asarray(HD**-0.5, BF16)
         upstream = grad_ref[spans[i], :]
@@ -139,7 +141,7 @@
                 score_grad = (weights * (weight_grad - centre)).astype(BF16)
                 v_term = product(weights.astype(BF16), chosen_grad, 1, 0)
                 k_term = product(score_grad, chosen, 1, 0)
-                term = product(score_grad, keys, 0, 0)
+                term = product(turned[j], score_grad, 1, 0)
                 q_sum = term if q_sum is None else q_sum + term
                 if i == j and half == 0:
                     v_total[spans[j], :] = v_term
@@ -147,8 +149,8 @@
                 else:
                     v_total[spans[j], :] += v_term
                     k_total[spans[j], :] += k_term
-            sums.append(q_sum)
-        q_total[spans[i], :] = jnp.where(lane < HD, sums[0], sums[1])
+            sums.append(q_sum[half * HD : (half + 1) * HD, :])
+        q_total[spans[i], :] = jnp.concatenate(sums, axis=0).T
     opening = opening_lanes(block * count)
     cos_values = cos_ref[...]
     sin_values = -sin_ref[...]
@@ -302,6 +304,10 @@
     return pick_columns(back, values)
 
 
+def chunks(wide):
+    return [(at, min(256, wide - at)) for at in range(0, wide, 256)]
+
+
 def reorder_body(count, width, order_ref, in_ref, out_ref):
     for j in range(count):
         source = pl.ds(pl.multiple_of(order_ref[j] * width, width), width)
@@ -404,16 +410,19 @@
     values = (x_ref[...].astype(F32) - mean_ref[...]) * inverse_ref[...]
     normed = (values * norm_ref[0:1, :] + norm_ref[1:2, :]).astype(BF16)
     normed_ref[...] = normed
-    wait_at(step, 0, copies_a)
-    both = product(normed, weight_a[...], 1, 0) + bias_ref[:, :width]
+    wait_at(step, 0, copies_a + copies_v)
     opening = opening_lanes(normed.shape[0])
     cos_values = cos_ref[...]
     sin_values = sin_ref[...]
-    for at in range(0, width, PAIR):
-        part = turn(both[:, at : at + PAIR], cos_values, sin_values, opening)
-        qk_ref[:, at : at + PAIR] = part.astype(BF16)
-    wait_at(step, 0, copies_v)
-    v_ref[...] = (product(normed, weight_v[...], 1, 0) + bias_ref[:, width:]).astype(BF16)
+    for at, wide in chunks(width):
+        both = product(normed, weight_a[:, at : at + wide], 1, 0) + bias_ref[:, at : at + wide]
+        for pair in range(0, wide, PAIR):
+            part = turn(both[:, pair : pair + PAIR], cos_values, sin_values, opening)
+            qk_ref[:, at + pair : at + pair + PAIR] = part.astype(BF16)
+    for at, wide in chunks(width // 2):
+        values = product(normed, weight_v[:, at : at + wide], 1, 0)
+        bias = bias_ref[:, width + at : width + at + wide]
+        v_ref[:, at : at + wide] = (values + bias).astype(BF16)
 
 
 def project_qkv(inputs, mean, inverse, norm_rows, bias_row, cos_table, sin_table, blocks_a, blocks_b):
@@ -500,19 +509,19 @@
     blocks = refs[:count]
     gate_grad_ref, up_grad_ref, weight, semaphores = refs[-4:]
     step = pl.program_id(0)
-    early, late = halves(copies_into(blocks, weight, semaphores, 0))
-    start_all(step, early + late)
-    gate = gate_ref[...].astype(F32)
-    sigmoid = jax.nn.sigmoid(gate)
-    silu = gate * sigmoid
-    slope = sigmoid + silu * (1.0 - sigmoid)
-    half = weight.shape[0] // 2
-    wait_at(step, 0, early)
-    hidden_grad = product(grad_ref[:, :half], weight[:half, :], 1, 0)
-    wait_at(step, 0, late)
-    hidden_grad = hidden_grad + product(grad_ref[:, half:], weight[half:, :], 1, 0)
-    up_grad_ref[...] = (hidden_grad * silu).astype(BF16)
-    gate_grad_ref[...] = (hidden_grad * up_ref[...].astype(F32) * slope).astype(BF16)
+    copies = copies_into(blocks, weight, semaphores, 0)
+    start_all(step, copies)
+    wait_at(step, 0, copies)
+    rows = grad_ref[...]
+    for at, wide in chunks(weight.shape[1]):
+        span = slice(at, at + wide)
+        hidden_grad = product(rows, weight[:, span], 1, 0)
+        gate = gate_ref[:, span].astype(F32)
+        sigmoid = jax.nn.sigmoid(gate)
+        silu = gate * sigmoid
+        up_grad_ref[:, span] = (hidden_grad * silu).astype(BF16)
+        slope = sigmoid + silu * (1.0 - sigmoid)
+        gate_grad_ref[:, span] = (hidden_grad * up_ref[:, span].astype(F32) * slope).astype(BF16)
 
 
 def gated_backward(grads, gate, up, blocks):
@@ -695,6 +704,37 @@
     )
 
 
+def over_tokens_body(count, *refs):
+    out_ref = refs[-1]
+    first = 0
+    for i in range(count):
+        left, right = refs[2 * i], refs[2 * i + 1]
+        wide = right.shape[1]
+        out_ref[:, first : first + wide] = product(left[...], right[...], 0, 0).astype(BF16)
+        first += wide
+
+
+def over_tokens(groups, flops=10**9):
+    length, depth = groups[0][0].shape
+    wide = sum(right.shape[1] for _, right in groups)
+    block = depth // STRIPES
+    return kernel_call(
+        functools.partial(over_tokens_body, len(groups)),
+        "over_tokens",
+        [values for group in groups for values in group],
+        [
+            spec
+            for _, right in groups
+            for spec in (pl.BlockSpec((length, block), lambda i: (0, i)), whole(right.shape))
+        ],
+        pl.BlockSpec((block, wide), lambda i: (i, 0)),
+        shaped((depth, wide)),
+        grid=(STRIPES,),
+        flops=flops,
+        vmem=60,
+    )
+
+
 def added(refs):
     total = refs[0][...].astype(F32)
     for ref in refs[1:]:
@@ -1112,7 +1152,7 @@
         x_all, mean_one, inverse_one, norm_rows, bias_row, cos_table, sin_table, blocks_a, blocks_b
     )
     qk, values = advance([ring_gate], qk, values, busy=True)
-    mixed, lse = attend_forward(qk, values, segment_down, segment_across, shards)
+    mixed, lse = attend_forward(qk, values, segment_down, segment_across, 2)
     mixed, lse = advance([ring_up], mixed, lse, busy=True)
     arriving = scatter(outward([(mixed, blocks_b, heads_wide)], depth, "from_heads")[0])
     advance([ring_gate])
@@ -1183,28 +1223,27 @@
             segment_across,
             cos_table,
             sin_table,
-            shards,
+            2,
             half,
             grads,
         )
-        grads = advance([sum_up], *grads, busy=half == 0)
+        grads = advance([sum_up], *grads, busy=True)
     q_grad, k_grad, v_grad, bias_sums = grads
-    q_sum = product(normed, q_grad, 0, 0).astype(BF16)
-    k_sum = product(normed, k_grad, 0, 0).astype(BF16)
-    sum_qk = Summing(route, lambda: [q_sum, k_sum], width, 1, 0, 1)
-    q_sum, k_sum, v_grad, branch = advance([sum_qk], q_sum, k_sum, v_grad, branch)
-    out_sum = product(branch, mixed, 0, 0).astype(BF16)
-    v_sum = product(normed, v_grad, 0, 0).astype(BF16)
-    sum_vo = Summing(route, lambda: [v_sum, out_sum], width, 1, 0, 0)
-    out_sum, v_sum, q_grad, arriving_result = advance(
-        [sum_qk, sum_vo], out_sum, v_sum, q_grad, arriving_result, busy=True
+    qk_sum = over_tokens([(normed, q_grad), (normed, k_grad)])
+    sum_qk = Summing(route, lambda: [qk_sum], width, 1, 0, 1)
+    qk_sum, v_grad, branch = advance([sum_qk], qk_sum, v_grad, branch, busy=True)
+    vo_sum = over_tokens([(normed, v_grad), (branch, mixed)])
+    sum_vo = Summing(route, lambda: [vo_sum], width, 1, 0, 0)
+    vo_sum = advance([sum_up], vo_sum)
+    vo_sum, q_grad, arriving_result = advance(
+        [sum_qk, sum_vo], vo_sum, q_grad, arriving_result, busy=True
     )
     heads_terms, one_sums = through_heads(
         [q_grad, k_grad, v_grad], x_all, mean_one, inverse_one, blocks_a, blocks_b
     )
     arriving = scatter(heads_terms)
     one_sums, middle, arriving_result, down_sum = advance(
-        [sum_up, sum_vo], one_sums, middle, arriving_result, down_sum, long=True
+        [sum_vo], one_sums, middle, arriving_result, down_sum, long=True
     )
     norm_grads = jnp.concatenate([one_sums, two_sums], axis=0)
     bias_sums = bias_sums.transpose(1, 0, 2).reshape(3, local_heads, count, HD // count)
@@ -1244,16 +1283,18 @@
     input_grad = input_back(order, arriving, own_bf16, norm_rows, middle_grad)
     input_grad, norm_sums = advance([sum_vo], input_grad, norm_sums)
 
+    q_k = sum_qk.total(qk_sum, 0)
+    v_o = sum_vo.total(vo_sum, 0)
     return (
         result,
         input_grad,
         norm_sums[0],
         norm_sums[1],
-        sum_qk.total(q_sum, 0),
-        sum_qk.total(k_sum, heads_wide),
-        sum_vo.total(v_sum, 0),
+        q_k[:, :heads_wide],
+        q_k[:, heads_wide:],
+        v_o[:, :heads_wide],
         bias_grad,
-        sum_vo.total(out_sum, heads_wide).T,
+        v_o[:, heads_wide:].T,
         norm_sums[2],
         norm_sums[3],
         grad_gate,

time: 632 us -> 617 us (0.976)
  matrix products: 48.4 us -> 28.3 us
    dot_general x7 -> x3, matrix products: 48.4 us -> 28.3 us  [product(): lax.dot_general(left, right, (((left_dim,), (right_dim,)), ((), ())), pre...]
    pallas_call x78 -> x79, Pallas kernels: 188 us -> 202 us  [kernel_call(): pl.pallas_call(body, grid_spec=pltpu.PrefetchScalarGridSpec(num_scalar_pr...]
    ppermute x77, waiting for transfers between devices: 150 us -> 157 us  [send(): return lax.ppermute(values, 'dp', self.pairs[direction])]
    pallas_call x2, Pallas kernels: 29.6 us -> 23.2 us  [attend_backward(): pl.pallas_call(functools.partial(backward_body, length // count, count, l...]
    unnamed x147 -> x133, local copies, waits for them, and re-layouts: 25.7 us -> 23.9 us
  transfers between devices with their start and end apart: 93 -> 93, of which waited for: 38 -> 40; matrix products, arithmetic and copies ran while one was open for 12% -> 9% of each run, Pallas kernels for 37% -> 39%
where the time goes in v4:
time: 617 us; the launch traced here: 607 us
  Pallas kernels  241 us (39%)
  waiting for transfers between devices  182 us (29%)
  starting transfers between devices  89.3 us (14%)
  local copies, waits for them, and re-layouts  34.1 us (6%)
  matrix products  28.3 us (5%)
  other arithmetic  16.9 us (3%)
  between operations  15.6 us (3%)
    pallas_call x79, Pallas kernels, kernel_call(): pl.pallas_call(body, grid_spec=pltpu.PrefetchScalarGridSpec(num_scalar_pr...  202 us
    ppermute x77, waiting for transfers between devices, send(): return lax.ppermute(values, 'dp', self.pairs[direction])  157 us
    ppermute x77, starting transfers between devices, send(): return lax.ppermute(values, 'dp', self.pairs[direction])  79.8 us
    dot_general x3, matrix products, product(): lax.dot_general(left, right, (((left_dim,), (right_dim,)), ((), ())), pre...  28.3 us
    unnamed x133, local copies, waits for them, and re-layouts  23.9 us
    pallas_call x2, Pallas kernels, attend_backward(): pl.pallas_call(functools.partial(backward_body, length // count, count, l...  23.2 us
    reduce_scatter x3, waiting for transfers between devices, scatter(): return lax.psum_scatter(values, 'tensor', scatter_dimension=0, tiled=True)  17.8 us
    pallas_call x1, Pallas kernels, attend_forward(): pl.pallas_call(functools.partial(forward_body, length // count, count), g...  15.1 us
  transfers between devices with their start and end apart: 93, of which 40 were waited for; matrix products, arithmetic and copies ran while one was open for 9% of the time, Pallas kernels for 39%

profile of v4, /device:TPU:0, one launch (start us, length us, event | category | flops | bytes accessed | tf_op | source)
XLA Modules:
  0.0 606.9 jit_solution(10110786832485650307)
XLA Ops:
  25.4 8.1 %collective-permute-done.2.refs_7_ = bf16[256,1024]{1,0:T(8,128)(2,1)} collective-permute-done((bf16[256,1024]{1,0:T(8,128)(2,1)}, bf16[256,1024]{1,0:T(8,128)(2,1)}, u32[]{:S(2)}, u32[]{:S(2)}) %collective-permute-start.2) | collective-permute-done | bytes 524320 | tf_op jit(solution)/shard_map/ppermute | solution.py:914
  37.6 7.8 %collective-permute-done.4.refs_7_.refs_15_.refs_8_ = bf16[272,1024]{1,0:T(8,128)(2,1)} collective-permute-done((bf16[272,1024]{1,0:T(8,128)(2,1)}, bf16[272,1024]{1,0:T(8,128)(2,1)}, u32[]{:S(2)}, u32[]{:S(2)}) %collective-permute-start.4) | collective-permute-done | bytes 557088 | tf_op jit(solution)/shard_map/ppermute | solution.py:914
  64.4 8.1 %collective-permute-done.8.refs_6_.refs_14_.refs_7_ = bf16[272,1024]{1,0:T(8,128)(2,1)} collective-permute-done((bf16[272,1024]{1,0:T(8,128)(2,1)}, bf16[272,1024]{1,0:T(8,128)(2,1)}, u32[]{:S(2)}, u32[]{:S(2)}) %collective-permute-start.8) | collective-permute-done | bytes 557088 | tf_op jit(solution)/shard_map/ppermute | solution.py:914
  74.1 7.4 %collective-permute-done.10.refs_5_ = bf16[256,1024]{1,0:T(8,128)(2,1)} collective-permute-done((bf16[256,1024]{1,0:T(8,128)(2,1)S(1)}, bf16[256,1024]{1,0:T(8,128)(2,1)}, u32[]{:S(2)}, u32[]{:S(2)}) %collective-permute-start.10) | collective-permute-done | bytes 524320 | tf_op jit(solution)/shard_map/ppermute | solution.py:914
  86.2 12.3 %collective-permute-done.12.refs_5_.refs_13_.refs_6_ = bf16[272,1024]{1,0:T(8,128)(2,1)} collective-permute-done((bf16[272,1024]{1,0:T(8,128)(2,1)}, bf16[272,1024]{1,0:T(8,128)(2,1)}, u32[]{:S(2)}, u32[]{:S(2)}) %collective-permute-start.12) | collective-permute-done | bytes 557088 | tf_op jit(solution)/shard_map/ppermute | solution.py:914
  99.1 7.4 %collective-permute-done.14.refs_4_ = bf16[256,1024]{1,0:T(8,128)(2,1)} collective-permute-done((bf16[256,1024]{1,0:T(8,128)(2,1)}, bf16[256,1024]{1,0:T(8,128)(2,1)}, u32[]{:S(2)}, u32[]{:S(2)}) %collective-permute-start.14) | collective-permute-done | bytes 524320 | tf_op jit(solution)/shard_map/ppermute | solution.py:914
  108.5 5.3 collective-permute-done.15.refs_4_.refs_12_.refs_5_
  119.7 14.5 %project_qkv.1 = (bf16[1024,1024]{1,0:T(8,128)(2,1)}, bf16[1024,512]{1,0:T(8,128)(2,1)}, bf16[1024,2048]{1,0:T(8,128)(2,1)}) custom-call(bf16[1024,2048]{1,0:T(8,128)(2,1)} %all-gather.5.cloned.1.call-done.x_ref, f32[4,2048]{1,0:T(4,128)} %copy-done.14, f32[1,1536]{1,0:T(1,128)} %copy-done.22, f32[1024,1]{1,0:T(8,128)} %copy-done.4, f32[1024,1]{1,0:T(8,128)} %copy-done.5, ...), custom_call_target="tpu_custom_call" | custom-call | flops 1000000000 | bytes 1 | tf_op jit(solution)/shard_map/project_qkv/pallas_call | solution.py:226
  136.3 15.1 %attend_forward.1 = (bf16[1024,512]{1,0:T(8,128)(2,1)}, f32[4,2,1024]{2,1,0:T(2,128)}) custom-call(bf16[1024,1024]{1,0:T(8,128)(2,1)} %get-tuple-element.515.q_ref.k_ref, bf16[1024,1024]{1,0:T(8,128)(2,1)} %get-tuple-element.515.q_ref.k_ref, bf16[1024,512]{1,0:T(8,128)(2,1)} %get-tuple-element.516.v_ref, s32[1024,1]{1,0:T(8,128)} %copy.53.down_ref, ...), custom_call_target="tpu_custom_call" | custom-call | flops 1000000000 | bytes 1 | tf_op jit(solution)/shard_map/attend_forward/pallas_call | solution.py:79
  157.9 6.7 %from_heads.1 = bf16[1024,2048]{1,0:T(8,128)(2,1)} custom-call(bf16[1024,512]{1,0:T(8,128)(2,1)} %get-tuple-element.530.refs_0_.mixed_ref.refs_3_, bf16[272,1024]{1,0:T(8,128)(2,1)} %fusion.4.refs_0_.refs_8_.refs_1_, bf16[272,1024]{1,0:T(8,128)(2,1)} %collective-permute-done.5.refs_1_.refs_9_.refs_2_, ...), custom_call_target="tpu_custom_call" | custom-call | flops 1000000000 | bytes 1 | tf_op jit(solution)/shard_map/from_heads/pallas_call | solution.py:226
  166.8 5.1 collective-permute-done.22.refs_14_.refs_17_
  178.5 9.0 %collective-permute-done.24.refs_5_.refs_8_ = bf16[256,1408]{1,0:T(8,128)(2,1)} collective-permute-done((bf16[256,1408]{1,0:T(8,128)(2,1)}, bf16[256,1408]{1,0:T(8,128)(2,1)}, u32[]{:S(2)}, u32[]{:S(2)}) %collective-permute-start.24) | collective-permute-done | bytes 720928 | tf_op jit(solution)/shard_map/ppermute | solution.py:914
  191.1 17.8 %reduce-scatter.4.cloned.1.call-done.term_ref = bf16[256,2048]{1,0:T(8,128)(2,1)} async-done(((bf16[1024,2048]{1,0:T(8,128)(2,1)}), bf16[256,2048]{1,0:T(8,128)(2,1)}) %reduce-scatter.4.cloned.1.call-update) | async-done | bytes 1048592 | tf_op jit(solution)/shard_map/reduce_scatter | solution.py:1080
  217.7 14.8 %collective-permute-done.28.refs_4_.refs_7_ = bf16[256,1408]{1,0:T(8,128)(2,1)} collective-permute-done((bf16[256,1408]{1,0:T(8,128)(2,1)}, bf16[256,1408]{1,0:T(8,128)(2,1)}, u32[]{:S(2)}, u32[]{:S(2)}) %collective-permute-start.28) | collective-permute-done | bytes 720928 | tf_op jit(solution)/shard_map/ppermute | solution.py:914
  251.6 12.7 %gated_forward.2 = (bf16[1024,1408]{1,0:T(8,128)(2,1)}, bf16[1024,1408]{1,0:T(8,128)(2,1)}, bf16[1024,1408]{1,0:T(8,128)(2,1)}) custom-call(bf16[1024,2048]{1,0:T(8,128)(2,1)} %all-gather.9.cloned.1.call-done.x_ref, bf16[256,1408]{1,0:T(8,128)(2,1)} %refs_3_, bf16[256,1408]{1,0:T(8,128)(2,1)} %copy-done.28, ...), custom_call_target="tpu_custom_call" | custom-call | flops 1000000000 | bytes 1 | tf_op jit(solution)/shard_map/gated_forward/pallas_call | solution.py:226
  268.6 12.7 %gated_forward.3 = (bf16[1024,1408]{1,0:T(8,128)(2,1)}, bf16[1024,1408]{1,0:T(8,128)(2,1)}, bf16[1024,1408]{1,0:T(8,128)(2,1)}) custom-call(bf16[1024,2048]{1,0:T(8,128)(2,1)} %all-gather.9.cloned.1.call-done.x_ref, bf16[256,1408]{1,0:T(8,128)(2,1)} %refs_3_, ...), custom_call_target="tpu_custom_call", output_to_operand_aliasing={{0}: (17, {}), {1}: (18, {}), {2}: (19, {})} | custom-call | flops 1000000000 | bytes 1 | tf_op jit(solution)/shard_map/gated_forward/pallas_call | solution.py:226
  284.5 8.7 %convolution_convert_fusion.2.refs_0_.refs_1_.refs_2_.refs_3_ = bf16[2048,1408]{1,0:T(8,128)(2,1)} fusion(bf16[1024,2048]{1,0:T(8,128)(2,1)S(1)} %copy-done.32, bf16[1024,1408]{1,0:T(8,128)(2,1)S(1)} %copy-done.24), kind=kOutput, calls=%fused_computation.3 | convolution fusion | flops 5908463616 | bytes 12845056 | tf_op jit(solution)/shard_map/dot_general | solution.py:23
  298.3 13.7 %gated_backward.1 = (bf16[1024,1408]{1,0:T(8,128)(2,1)}, bf16[1024,1408]{1,0:T(8,128)(2,1)}) custom-call(bf16[1024,2048]{1,0:T(8,128)(2,1)} %all-gather.7.cloned.1.call-done.refs_0_, bf16[1024,1408]{1,0:T(8,128)(2,1)} %get-tuple-element.605.refs_1_, bf16[1024,1408]{1,0:T(8,128)(2,1)} %get-tuple-element.606.refs_2_, ...), custom_call_target="tpu_custom_call" | custom-call | flops 1000000000 | bytes 1 | tf_op jit(solution)/shard_map/gated_backward/pallas_call | solution.py:226
  317.9 11.1 %convolution_convert_fusion.1.refs_0_.refs_1_.refs_2_.refs_3_ = bf16[2048,1408]{1,0:T(8,128)(2,1)} fusion(bf16[1024,2048]{1,0:T(8,128)(2,1)} %all-gather.9.cloned.1.call-done.x_ref, bf16[1024,1408]{1,0:T(8,128)(2,1)} %get-tuple-element.626.refs_1_), kind=kOutput, calls=%fused_computation.2 | convolution fusion | flops 5908463616 | bytes 12845056 | tf_op jit(solution)/shard_map/dot_general | solution.py:23
  333.2 20.1 %from_gates.1 = (bf16[512,2048]{1,0:T(8,128)(2,1)}, bf16[512,2048]{1,0:T(8,128)(2,1)}) custom-call(s32[1]{0:T(128)} %bitcast.14.refs_0_, bf16[1024,1408]{1,0:T(8,128)(2,1)} %get-tuple-element.626.refs_1_, bf16[1024,1408]{1,0:T(8,128)(2,1)} %get-tuple-element.655.refs_2_, bf16[256,1408]{1,0:T(8,128)(2,1)} %refs_3_, bf16[256,1408]{1,0:T(8,128)(2,1)} %copy-done.28, ...), custom_call_target="tpu_custom_call" | custom-call | flops 1000000000 | bytes 1 | tf_op jit(solution)/shard_map/from_gates/pallas_call | solution.py:226
  371.1 8.5 %convolution_convert_fusion.refs_0_.refs_1_.refs_2_.refs_3_ = bf16[2048,1408]{1,0:T(8,128)(2,1)} fusion(bf16[1024,2048]{1,0:T(8,128)(2,1)S(1)} %copy-done.23, bf16[1024,1408]{1,0:T(8,128)(2,1)S(1)} %copy-done.35), kind=kOutput, calls=%fused_computation.1 | convolution fusion | flops 5908463616 | bytes 12845056 | tf_op jit(solution)/shard_map/dot_general | solution.py:23
  385.6 6.2 %collective-permute-done.53.refs_0_ = bf16[256,1408]{1,0:T(8,128)(2,1)} collective-permute-done((bf16[256,1408]{1,0:T(8,128)(2,1)}, bf16[256,1408]{1,0:T(8,128)(2,1)}, u32[]{:S(2)}, u32[]{:S(2)}) %collective-permute-start.53) | collective-permute-done | bytes 720928 | tf_op jit(solution)/shard_map/ppermute | solution.py:914
  402.3 11.8 %from_hidden.1 = bf16[1024,2048]{1,0:T(8,128)(2,1)} custom-call(bf16[1024,1408]{1,0:T(8,128)(2,1)} %get-tuple-element.682.refs_0_, bf16[128,1408]{1,0:T(8,128)(2,1)} %get-tuple-element.547.refs_3_.refs_1_, bf16[128,1408]{1,0:T(8,128)(2,1)} %get-tuple-element.549.refs_4_.refs_2_, bf16[128,1408]{1,0:T(8,128)(2,1)} %collective-permute-done.31.refs_5_.refs_3_, ...), custom_call_target="tpu_custom_call" | custom-call | flops 1000000000 | bytes 1 | tf_op jit(solution)/shard_map/from_hidden/pallas_call | solution.py:226
  416.3 6.4 %collective-permute-done.57 = bf16[256,1408]{1,0:T(8,128)(2,1)} collective-permute-done((bf16[256,1408]{1,0:T(8,128)(2,1)}, bf16[256,1408]{1,0:T(8,128)(2,1)}, u32[]{:S(2)}, u32[]{:S(2)}) %collective-permute-start.57) | collective-permute-done | bytes 720928 | tf_op jit(solution)/shard_map/ppermute | solution.py:914
  425.3 11.6 %collective-permute-done.59.refs_0_ = bf16[256,1408]{1,0:T(8,128)(2,1)} collective-permute-done((bf16[256,1408]{1,0:T(8,128)(2,1)}, bf16[256,1408]{1,0:T(8,128)(2,1)}, u32[]{:S(2)}, u32[]{:S(2)}) %collective-permute-start.59) | collective-permute-done | bytes 720928 | tf_op jit(solution)/shard_map/ppermute | solution.py:914
  436.9 7.1 %through_out.1.grad_ref = bf16[1024,512]{1,0:T(8,128)(2,1)} custom-call(bf16[1024,2048]{1,0:T(8,128)(2,1)} %all-gather.11.cloned.1.call-done.rows_ref.refs_2_, bf16[272,1024]{1,0:T(8,128)(2,1)} %fusion.4.refs_0_.refs_8_.refs_1_, bf16[272,1024]{1,0:T(8,128)(2,1)} %collective-permute-done.5.refs_1_.refs_9_.refs_2_, ...), custom_call_target="tpu_custom_call" | custom-call | flops 1000000000 | bytes 1 | tf_op jit(solution)/shard_map/through_out/pallas_call | solution.py:226
  453.9 11.6 %attend_backward.2 = (bf16[1024,512]{1,0:T(8,128)(2,1)}, bf16[1024,512]{1,0:T(8,128)(2,1)}, bf16[1024,512]{1,0:T(8,128)(2,1)}, f32[4,3,128]{2,1,0:T(4,128)}) custom-call(bf16[1024,1024]{1,0:T(8,128)(2,1)} %get-tuple-element.515.q_ref.k_ref, bf16[1024,1024]{1,0:T(8,128)(2,1)} %get-tuple-element.515.q_ref.k_ref, bf16[1024,512]{1,0:T(8,128)(2,1)} %get-tuple-element.516.v_ref, ...), custom_call_target="tpu_custom_call" | custom-call | flops 999999995904 | bytes 1 | tf_op jit(solution)/shard_map/attend_backward/pallas_call | solution.py:177
  474.7 11.6 %attend_backward.3 = (bf16[1024,512]{1,0:T(8,128)(2,1)}, bf16[1024,512]{1,0:T(8,128)(2,1)}, bf16[1024,512]{1,0:T(8,128)(2,1)}, f32[4,3,128]{2,1,0:T(4,128)}) custom-call(bf16[1024,1024]{1,0:T(8,128)(2,1)} %get-tuple-element.515.q_ref.k_ref, ...), custom_call_target="tpu_custom_call", output_to_operand_aliasing={{0}: (10, {}), {1}: (11, {}), {2}: (12, {}), {3}: (13, {})} | custom-call | flops 999999995904 | bytes 1 | tf_op jit(solution)/shard_map/attend_backward/pallas_call | solution.py:177
  491.1 9.1 %over_tokens.2.refs_0_.refs_1_.refs_2_.refs_3_ = bf16[2048,1024]{1,0:T(8,128)(2,1)} custom-call(bf16[1024,2048]{1,0:T(8,128)(2,1)} %get-tuple-element.723.refs_0_.refs_2_, bf16[1024,512]{1,0:T(8,128)(2,1)} %get-tuple-element.746.refs_1_.q_ref, bf16[1024,2048]{1,0:T(8,128)(2,1)} %get-tuple-element.723.refs_0_.refs_2_, ...), custom_call_target="tpu_custom_call" | custom-call | flops 1000000000 | bytes 1 | tf_op jit(solution)/shard_map/over_tokens/pallas_call | solution.py:226
  504.3 9.1 %over_tokens.3.refs_0_.refs_1_.refs_2_.refs_3_ = bf16[2048,1024]{1,0:T(8,128)(2,1)} custom-call(bf16[1024,2048]{1,0:T(8,128)(2,1)} %get-tuple-element.723.refs_0_.refs_2_, bf16[1024,512]{1,0:T(8,128)(2,1)} %get-tuple-element.732.refs_1_.v_ref, bf16[1024,2048]{1,0:T(8,128)(2,1)} %all-gather.11.cloned.1.call-done.rows_ref.refs_2_, ...), custom_call_target="tpu_custom_call" | custom-call | flops 1000000000 | bytes 1 | tf_op jit(solution)/shard_map/over_tokens/pallas_call | solution.py:226
  524.4 13.0 %through_heads.1 = (bf16[1024,2048]{1,0:T(8,128)(2,1)}, f32[2,2048]{1,0:T(2,128)}) custom-call(bf16[1024,512]{1,0:T(8,128)(2,1)} %get-tuple-element.746.refs_1_.q_ref, bf16[1024,512]{1,0:T(8,128)(2,1)} %get-tuple-element.725.refs_3_.k_ref, bf16[1024,512]{1,0:T(8,128)(2,1)} %get-tuple-element.732.refs_1_.v_ref, ...), custom_call_target="tpu_custom_call" | custom-call | flops 1000000000 | bytes 1 | tf_op jit(solution)/shard_map/through_heads/pallas_call | solution.py:226
  580.6 6.2 %collective-permute-done.83 = bf16[256,1024]{1,0:T(8,128)(2,1)S(1)} collective-permute-done((bf16[256,1024]{1,0:T(8,128)(2,1)}, bf16[256,1024]{1,0:T(8,128)(2,1)S(1)}, u32[]{:S(2)}, u32[]{:S(2)}) %collective-permute-start.83) | collective-permute-done | bytes 524320 | tf_op jit(solution)/shard_map/ppermute | solution.py:914
  (433 shorter events, 260.8 us)
Async XLA Ops:
  7.2 41.8 %all-gather.5.cloned.1.call-start = ((), (), s32[]{:S(2)}) async-start(), calls=%async_computation.3 | async-start | bytes 5242880 | tf_op jit(solution)/shard_map/all_gather | solution.py:1077
  12.0 86.6 %all-gather.7.cloned.1.call-start = ((), (), s32[]{:S(2)}) async-start(), calls=%async_computation.4 | async-start | bytes 5242880 | tf_op jit(solution)/shard_map/all_gather | solution.py:1077
  20.4 25.0 %collective-permute-start.4 = (bf16[272,1024]{1,0:T(8,128)(2,1)}, bf16[272,1024]{1,0:T(8,128)(2,1)}, u32[]{:S(2)}, u32[]{:S(2)}) collective-permute-start(bf16[272,1024]{1,0:T(8,128)(2,1)} %fusion.4.refs_0_.refs_8_.refs_1_), channel_id=1, source_target_pairs={{0,8},{8,16},{16,24},{24,28},{28,20},{20,12},{12,4},{4,0},{1,9},{9... | collective-permute-start | bytes 1671176 | tf_op jit(solution)/shard_map/ppermute | solution.py:914
  22.4 25.1 %collective-permute-start.5 = (bf16[272,1024]{1,0:T(8,128)(2,1)}, bf16[272,1024]{1,0:T(8,128)(2,1)}, u32[]{:S(2)}, u32[]{:S(2)}) collective-permute-start(bf16[272,1024]{1,0:T(8,128)(2,1)} %fusion.4.refs_0_.refs_8_.refs_1_), channel_id=1, source_target_pairs={{8,0},{16,8},{24,16},{28,24},{20,28},{12,20},{4,12},{0,4},{9,1},{1... | collective-permute-start | bytes 1671176 | tf_op jit(solution)/shard_map/ppermute | solution.py:914
  58.7 22.9 %collective-permute-start.10 = (bf16[256,1024]{1,0:T(8,128)(2,1)S(1)}, bf16[256,1024]{1,0:T(8,128)(2,1)}, u32[]{:S(2)}, u32[]{:S(2)}) collective-permute-start(bf16[256,1024]{1,0:T(8,128)(2,1)S(1)} %collective-permute-done.6.refs_6_), channel_id=1, source_target_pairs={{0,8},{8,16},{16,24},{24,28},{28,20},{20,12},{12,4},{4,0},{1,9},{9... | collective-permute-start | bytes 1572872 | tf_op jit(solution)/shard_map/ppermute | solution.py:914
  60.7 148.2 %reduce-scatter.4.cloned.1.call-start = ((), (), s32[]{:S(2)}) async-start(), calls=%async_computation.5 | async-start | bytes 5242880 | tf_op jit(solution)/shard_map/reduce_scatter | solution.py:1080
  106.5 27.7 %collective-permute-start.16 = (bf16[256,1408]{1,0:T(8,128)(2,1)S(1)}, bf16[256,1408]{1,0:T(8,128)(2,1)S(1)}, u32[]{:S(2)}, u32[]{:S(2)}) collective-permute-start(bf16[256,1408]{1,0:T(8,128)(2,1)S(1)} %copy-done.25), channel_id=1, source_target_pairs={{0,8},{8,16},{16,24},{24,28},{28,20},{20,12},{12,4},{4,0},{1,9},{9... | collective-permute-start | bytes 2162696 | tf_op jit(solution)/shard_map/ppermute | solution.py:914
  108.4 25.8 %collective-permute-start.17 = (bf16[256,1408]{1,0:T(8,128)(2,1)S(1)}, bf16[256,1408]{1,0:T(8,128)(2,1)S(1)}, u32[]{:S(2)}, u32[]{:S(2)}) collective-permute-start(bf16[256,1408]{1,0:T(8,128)(2,1)S(1)} %copy-done.25), channel_id=1, source_target_pairs={{8,0},{16,8},{24,16},{28,24},{20,28},{12,20},{4,12},{0,4},{9,1},{1... | collective-permute-start | bytes 2162696 | tf_op jit(solution)/shard_map/ppermute | solution.py:914
  113.8 37.6 %collective-permute-start.18 = (bf16[256,1408]{1,0:T(8,128)(2,1)S(1)}, bf16[256,1408]{1,0:T(8,128)(2,1)}, u32[]{:S(2)}, u32[]{:S(2)}) collective-permute-start(bf16[256,1408]{1,0:T(8,128)(2,1)S(1)} %copy-done.26), channel_id=1, source_target_pairs={{0,8},{8,16},{16,24},{24,28},{28,20},{20,12},{12,4},{4,0},{1,9},{9... | collective-permute-start | bytes 2162696 | tf_op jit(solution)/shard_map/ppermute | solution.py:914
  114.3 37.1 %collective-permute-start.19 = (bf16[256,1408]{1,0:T(8,128)(2,1)S(1)}, bf16[256,1408]{1,0:T(8,128)(2,1)}, u32[]{:S(2)}, u32[]{:S(2)}) collective-permute-start(bf16[256,1408]{1,0:T(8,128)(2,1)S(1)} %copy-done.26), channel_id=1, source_target_pairs={{8,0},{16,8},{24,16},{28,24},{20,28},{12,20},{4,12},{0,4},{9,1},{1... | collective-permute-start | bytes 2162696 | tf_op jit(solution)/shard_map/ppermute | solution.py:914
  134.2 30.5 %collective-permute-start.20 = (bf16[256,1408]{1,0:T(8,128)(2,1)S(1)}, bf16[256,1408]{1,0:T(8,128)(2,1)}, u32[]{:S(2)}, u32[]{:S(2)}) collective-permute-start(bf16[256,1408]{1,0:T(8,128)(2,1)S(1)} %collective-permute-done.16.refs_7_.refs_10_), channel_id=1, source_target_pairs={{0,8},{8,16},{16,24},{24,28},{28,20},{20,12},{12,4},{4,0},{1,9},{9... | collective-permute-start | bytes 2162696 | tf_op jit(solution)/shard_map/ppermute | solution.py:914
  134.7 30.0 %collective-permute-start.21 = (bf16[256,1408]{1,0:T(8,128)(2,1)S(1)}, bf16[256,1408]{1,0:T(8,128)(2,1)}, u32[]{:S(2)}, u32[]{:S(2)}) collective-permute-start(bf16[256,1408]{1,0:T(8,128)(2,1)S(1)} %collective-permute-done.17.refs_1_.refs_4_), channel_id=1, source_target_pairs={{8,0},{16,8},{24,16},{28,24},{20,28},{12,20},{4,12},{0,4},{9,1},{1... | collective-permute-start | bytes 2162696 | tf_op jit(solution)/shard_map/ppermute | solution.py:914
  151.9 23.6 %collective-permute-start.23 = (bf16[256,1408]{1,0:T(8,128)(2,1)}, bf16[256,1408]{1,0:T(8,128)(2,1)S(1)}, u32[]{:S(2)}, u32[]{:S(2)}) collective-permute-start(bf16[256,1408]{1,0:T(8,128)(2,1)} %collective-permute-done.19.refs_9_.refs_12_), channel_id=1, source_target_pairs={{8,0},{16,8},{24,16},{28,24},{20,28},{12,20},{4,12},{0,4},{9,1},{1... | collective-permute-start | bytes 2162696 | tf_op jit(solution)/shard_map/ppermute | solution.py:914
  164.6 85.0 %all-gather.9.cloned.1.call-start = ((), (), s32[]{:S(2)}) async-start(), calls=%async_computation.6 | async-start | bytes 5242880 | tf_op jit(solution)/shard_map/all_gather | solution.py:1077
  165.2 25.9 %collective-permute-start.25 = (bf16[256,1408]{1,0:T(8,128)(2,1)}, bf16[256,1408]{1,0:T(8,128)(2,1)}, u32[]{:S(2)}, u32[]{:S(2)}) collective-permute-start(bf16[256,1408]{1,0:T(8,128)(2,1)} %collective-permute-done.21.refs_2_.refs_5_), channel_id=1, source_target_pairs={{8,0},{16,8},{24,16},{28,24},{20,28},{12,20},{4,12},{0,4},{9,1},{1... | collective-permute-start | bytes 2162696 | tf_op jit(solution)/shard_map/ppermute | solution.py:914
  176.4 38.3 %collective-permute-start.26 = (bf16[256,1408]{1,0:T(8,128)(2,1)}, bf16[256,1408]{1,0:T(8,128)(2,1)}, u32[]{:S(2)}, u32[]{:S(2)}) collective-permute-start(bf16[256,1408]{1,0:T(8,128)(2,1)} %copy-done.29), channel_id=1, source_target_pairs={{0,8},{8,16},{16,24},{24,28},{28,20},{20,12},{12,4},{4,0},{1,9},{9... | collective-permute-start | bytes 2162696 | tf_op jit(solution)/shard_map/ppermute | solution.py:914
  176.9 37.8 %collective-permute-start.27 = (bf16[256,1408]{1,0:T(8,128)(2,1)}, bf16[256,1408]{1,0:T(8,128)(2,1)}, u32[]{:S(2)}, u32[]{:S(2)}) collective-permute-start(bf16[256,1408]{1,0:T(8,128)(2,1)} %copy-done.30), channel_id=1, source_target_pairs={{8,0},{16,8},{24,16},{28,24},{20,28},{12,20},{4,12},{0,4},{9,1},{1... | collective-permute-start | bytes 2162696 | tf_op jit(solution)/shard_map/ppermute | solution.py:914
  214.6 222.3 %all-gather.11.cloned.1.call-start = ((), (), s32[]{:S(2)}) async-start(), calls=%async_computation.7 | async-start | bytes 5242880 | tf_op jit(solution)/shard_map/all_gather | solution.py:1077
  215.7 24.5 %collective-permute-start.30 = (bf16[128,1408]{1,0:T(8,128)(2,1)S(1)}, bf16[128,1408]{1,0:T(8,128)(2,1)}, u32[]{:S(2)}, u32[]{:S(2)}) collective-permute-start(bf16[128,1408]{1,0:T(8,128)(2,1)S(1)} %copy-done.34), channel_id=1, source_target_pairs={{0,8},{8,16},{16,24},{24,28},{28,20},{20,12},{12,4},{4,0},{1,9},{9... | collective-permute-start | bytes 1081352 | tf_op jit(solution)/shard_map/ppermute | solution.py:914
  217.1 24.7 %collective-permute-start.31 = (bf16[128,1408]{1,0:T(8,128)(2,1)S(1)}, bf16[128,1408]{1,0:T(8,128)(2,1)}, u32[]{:S(2)}, u32[]{:S(2)}) collective-permute-start(bf16[128,1408]{1,0:T(8,128)(2,1)S(1)} %copy-done.34), channel_id=1, source_target_pairs={{8,0},{16,8},{24,16},{28,24},{20,28},{12,20},{4,12},{0,4},{9,1},{1... | collective-permute-start | bytes 1081352 | tf_op jit(solution)/shard_map/ppermute | solution.py:914
  315.8 37.5 %collective-permute-start.46 = (bf16[256,1408]{1,0:T(8,128)(2,1)}, bf16[256,1408]{1,0:T(8,128)(2,1)S(1)}, u32[]{:S(2)}, u32[]{:S(2)}) collective-permute-start(bf16[256,1408]{1,0:T(8,128)(2,1)} %get-tuple-element.624), channel_id=1, source_target_pairs={{0,8},{8,16},{16,24},{24,28},{28,20},{20,12},{12,4},{4,0},{1,9},{9... | collective-permute-start | bytes 2162696 | tf_op jit(solution)/shard_map/ppermute | solution.py:914
  317.3 36.1 %collective-permute-start.47 = (bf16[256,1408]{1,0:T(8,128)(2,1)}, bf16[256,1408]{1,0:T(8,128)(2,1)}, u32[]{:S(2)}, u32[]{:S(2)}) collective-permute-start(bf16[256,1408]{1,0:T(8,128)(2,1)} %get-tuple-element.625), channel_id=1, source_target_pairs={{8,0},{16,8},{24,16},{28,24},{20,28},{12,20},{4,12},{0,4},{9,1},{1... | collective-permute-start | bytes 2162696 | tf_op jit(solution)/shard_map/ppermute | solution.py:914
  361.8 29.9 %collective-permute-start.53 = (bf16[256,1408]{1,0:T(8,128)(2,1)}, bf16[256,1408]{1,0:T(8,128)(2,1)}, u32[]{:S(2)}, u32[]{:S(2)}) collective-permute-start(bf16[256,1408]{1,0:T(8,128)(2,1)} %get-tuple-element.662), channel_id=1, source_target_pairs={{0,8},{8,16},{16,24},{24,28},{28,20},{20,12},{12,4},{4,0},{1,9},{9... | collective-permute-start | bytes 2162696 | tf_op jit(solution)/shard_map/ppermute | solution.py:914
  363.3 28.6 %collective-permute-start.54 = (bf16[256,1408]{1,0:T(8,128)(2,1)}, bf16[256,1408]{1,0:T(8,128)(2,1)}, u32[]{:S(2)}, u32[]{:S(2)}) collective-permute-start(bf16[256,1408]{1,0:T(8,128)(2,1)} %get-tuple-element.663), channel_id=1, source_target_pairs={{8,0},{16,8},{24,16},{28,24},{20,28},{12,20},{4,12},{0,4},{9,1},{1... | collective-permute-start | bytes 2162696 | tf_op jit(solution)/shard_map/ppermute | solution.py:914
  368.6 23.9 %collective-permute-start.55 = (bf16[256,2048]{1,0:T(8,128)(2,1)}, bf16[256,2048]{1,0:T(8,128)(2,1)S(1)}, u32[]{:S(2)}, u32[]{:S(2)}) collective-permute-start(bf16[256,2048]{1,0:T(8,128)(2,1)} %get-tuple-element.664), channel_id=1, source_target_pairs={{0,2},{1,3},{2,0},{3,1},{4,6},{5,7},{6,4},{7,5},{8,10},{9,11},{10,... | collective-permute-start | bytes 3145736 | tf_op jit(solution)/shard_map/ppermute | solution.py:1033
  381.8 32.4 %collective-permute-start.56 = (bf16[256,1408]{1,0:T(8,128)(2,1)}, bf16[256,1408]{1,0:T(8,128)(2,1)}, u32[]{:S(2)}, u32[]{:S(2)}) collective-permute-start(bf16[256,1408]{1,0:T(8,128)(2,1)} %hand_on.25), channel_id=1, source_target_pairs={{0,8},{8,16},{16,24},{24,28},{28,20},{20,12},{12,4},{4,0},{1,9},{9... | collective-permute-start | bytes 2162696 | tf_op jit(solution)/shard_map/ppermute | solution.py:914
  402.3 114.1 %reduce-scatter.6.cloned.1.call-start = ((), (), s32[]{:S(2)}) async-start(), calls=%async_computation.8 | async-start | bytes 5242880 | tf_op jit(solution)/shard_map/reduce_scatter | solution.py:1080
  424.8 23.8 %collective-permute-start.61 = (bf16[256,1408]{1,0:T(8,128)(2,1)}, bf16[256,1408]{1,0:T(8,128)(2,1)S(1)}, u32[]{:S(2)}, u32[]{:S(2)}) collective-permute-start(bf16[256,1408]{1,0:T(8,128)(2,1)} %hand_on.28), channel_id=1, source_target_pairs={{8,0},{16,8},{24,16},{28,24},{20,28},{12,20},{4,12},{0,4},{9,1},{1... | collective-permute-start | bytes 2162696 | tf_op jit(solution)/shard_map/ppermute | solution.py:914
  453.7 135.6 %reduce-scatter.8.cloned.1.call-start = ((), (), s32[]{:S(2)}) async-start(), calls=%async_computation.9 | async-start | bytes 5242880 | tf_op jit(solution)/shard_map/reduce_scatter | solution.py:1080
  490.5 22.9 %collective-permute-start.66 = (bf16[256,1408]{1,0:T(8,128)(2,1)}, bf16[256,1408]{1,0:T(8,128)(2,1)}, u32[]{:S(2)}, u32[]{:S(2)}) collective-permute-start(bf16[256,1408]{1,0:T(8,128)(2,1)} %hand_on.32), channel_id=1, source_target_pairs={{0,8},{8,16},{16,24},{24,28},{28,20},{20,12},{12,4},{4,0},{1,9},{9... | collective-permute-start | bytes 2162696 | tf_op jit(solution)/shard_map/ppermute | solution.py:914
  522.2 24.1 %collective-permute-start.71 = (bf16[256,1024]{1,0:T(8,128)(2,1)}, bf16[256,1024]{1,0:T(8,128)(2,1)}, u32[]{:S(2)}, u32[]{:S(2)}) collective-permute-start(bf16[256,1024]{1,0:T(8,128)(2,1)} %get-tuple-element.758), channel_id=1, source_target_pairs={{0,8},{8,16},{16,24},{24,28},{28,20},{20,12},{12,4},{4,0},{1,9},{9... | collective-permute-start | bytes 1572872 | tf_op jit(solution)/shard_map/ppermute | solution.py:914
  523.1 23.1 %collective-permute-start.72 = (bf16[256,1024]{1,0:T(8,128)(2,1)}, bf16[256,1024]{1,0:T(8,128)(2,1)}, u32[]{:S(2)}, u32[]{:S(2)}) collective-permute-start(bf16[256,1024]{1,0:T(8,128)(2,1)} %get-tuple-element.759), channel_id=1, source_target_pairs={{8,0},{16,8},{24,16},{28,24},{20,28},{12,20},{4,12},{0,4},{9,1},{1... | collective-permute-start | bytes 1572872 | tf_op jit(solution)/shard_map/ppermute | solution.py:914
  (126 other events, 1374.4 us)
Sparse Core Ops, SparseCore 0:
  12.1 36.8 all-gather.4
  60.8 34.7 all-gather.6
  164.7 44.0 reduce-scatter.3
  214.8 33.5 all-gather.8
  402.4 33.5 all-gather.10
  453.8 42.4 reduce-scatter.5
  537.6 41.3 reduce-scatter.7

commit v5 on v4

--- a/solution.py
+++ b/solution.py
@@ -325,6 +325,7 @@
         [whole(values.shape)],
         whole(values.shape),
         shaped(values.shape),
+        vmem=60,
         grid=(1,),
         scalars=[order],
     )
@@ -784,6 +785,7 @@
         [whole(shape)] * 2 + [whole(norm_rows.shape)],
         [whole(shape), whole(column), whole(column), whole(shape)],
         [shaped(shape, F32), shaped(column, F32), shaped(column, F32), shaped(shape)],
+        vmem=60,
         grid=(1,),
     )
 
@@ -819,6 +821,7 @@
         [whole(shape)] * 3 + [whole(column)] * 2 + [whole(norm_rows.shape), whole(shape)],
         [whole(shape), whole(shape), whole((2, shape[1]))],
         [shaped(shape, F32), shaped(shape), shaped((2, shape[1]), F32)],
+        vmem=60,
         grid=(1,),
     )
 
@@ -1096,18 +1099,15 @@
 
     packed = jnp.stack([norm_one_gain, norm_one_bias, norm_two_gain, norm_two_bias])
     packed_core = across_core(packed)
+    packed_chip = across_chip(packed)
+    packed_far = lax.ppermute(packed, "tensor", [(i, i ^ 3) for i in range(4)])
     own_bf16 = reorder(order, activations)
     x_all = gather(own_bf16)
-    packed = jnp.concatenate([packed, packed_core], axis=0)
-    packed, w_down, w_value, w_out, cotangent = advance(
-        [], packed, w_down, w_value, w_out, cotangent
-    )
-    packed_chip = across_chip(packed)
     weight_vo = jnp.concatenate([w_value, w_out.T], axis=1)
-    packed_chip, weight_vo, cotangent, w_down = advance(
-        [], packed_chip, weight_vo, cotangent, w_down
-    )
-    packed = jnp.concatenate([packed, packed_chip], axis=0).reshape(shards, 4, norm_part)
+    packed, packed_core, packed_chip, packed_far, weight_vo, cotangent, w_down = advance(
+        [], packed, packed_core, packed_chip, packed_far, weight_vo, cotangent, w_down
+    )
+    packed = jnp.stack([packed, packed_core, packed_chip, packed_far])
     packed = relative(packed).transpose(1, 0, 2).reshape(4, width)
     wide = 2 * heads_wide
     packed = jnp.concatenate(
@@ -1124,10 +1124,11 @@
     down_rows = w_down.T
     ring_down[0].flying = [down_rows[:part]]
     ring_down[1].flying = [down_rows[part:]]
-    x_all, own_grad = advance([ring_vo], x_all, own_grad)
+    own_grad = advance([ring_vo], own_grad)
+    x_all, own_grad = advance([ring_qk], x_all, own_grad)
     grad_all = gather(own_grad)
     mean_one, inverse_one = row_stats(x_all)
-    mean_one, inverse_one, segments = advance([ring_qk], mean_one, inverse_one, segments)
+    mean_one, inverse_one, segments = advance([ring_vo], mean_one, inverse_one, segments)
     segment_down, segment_across = segments[:, None], segments[None, :]
     begins = jnp.sum((segment_across < segment_down).astype(F32), axis=1, keepdims=True)
     places = jnp.arange(length, dtype=jnp.int32)[:, None].astype(F32)
@@ -1139,19 +1140,18 @@
         lanes < ROT, jnp.where(lanes < ROT // 2, -1.0, 1.0) * jnp.sin(angles), 0.0
     )
     cos_table, sin_table, segment_down, segment_across = advance(
-        [ring_vo], cos_table, sin_table, segment_down, segment_across
-    )
-    advance([ring_qk], long=True)
-    grad_all = advance([ring_vo], grad_all)
+        [ring_qk], cos_table, sin_table, segment_down, segment_across
+    )
+    advance([ring_vo])
     advance([ring_qk, ring_gate])
-    advance([ring_vo, ring_up], busy=True)
+    advance([ring_vo, ring_up], long=True)
     blocks_a = ring_qk.all()
     blocks_b = ring_vo.all()
     norm_rows, bias_row = decode(order, blocks_b, depth, 3 * heads_wide)
     qk, values, normed = project_qkv(
         x_all, mean_one, inverse_one, norm_rows, bias_row, cos_table, sin_table, blocks_a, blocks_b
     )
-    qk, values = advance([ring_gate], qk, values, busy=True)
+    qk, values, grad_all = advance([ring_gate], qk, values, grad_all, busy=True)
     mixed, lse = attend_forward(qk, values, segment_down, segment_across, 2)
     mixed, lse = advance([ring_up], mixed, lse, busy=True)
     arriving = scatter(outward([(mixed, blocks_b, heads_wide)], depth, "from_heads")[0])
@@ -1210,7 +1210,7 @@
     branch, result_terms = advance([sum_up], branch, result_terms, busy=True)
     arriving_result = scatter(result_terms)
     mixed_grad = through_out(branch, blocks_b)
-    mixed_grad, branch = advance([sum_gate], mixed_grad, branch, busy=True)
+    mixed_grad, branch = advance([], mixed_grad, branch, busy=True)
     grads = None
     for half in range(2):
         grads = attend_backward(
@@ -1227,6 +1227,8 @@
             half,
             grads,
         )
+        if half == 0:
+            grads = advance([sum_gate], *grads)
         grads = advance([sum_up], *grads, busy=True)
     q_grad, k_grad, v_grad, bias_sums = grads
     qk_sum = over_tokens([(normed, q_grad), (normed, k_grad)])

time: 617 us -> 609 us (0.987)
  local copies, waits for them, and re-layouts: 34.1 us -> 26.2 us
    pallas_call x79 -> x80, Pallas kernels: 202 us -> 207 us  [kernel_call(): pl.pallas_call(body, grid_spec=pltpu.PrefetchScalarGridSpec(num_scalar_pr...]
    unnamed x133 -> x170, local copies, waits for them, and re-layouts: 23.9 us -> 19.2 us
  transfers between devices with their start and end apart: 93 -> 94, of which waited for: 40 -> 37; matrix products, arithmetic and copies ran while one was open for 9% -> 8% of each run, Pallas kernels for 39% -> 40%
where the time goes in v5:
time: 609 us; the launch traced here: 600 us
  Pallas kernels  246 us (40%)
  waiting for transfers between devices  178 us (29%)
  starting transfers between devices  89.2 us (15%)
  matrix products  28 us (5%)
  local copies, waits for them, and re-layouts  26.2 us (4%)
  other arithmetic  16.8 us (3%)
  between operations  15.9 us (3%)
    pallas_call x80, Pallas kernels, kernel_call(): pl.pallas_call(body, grid_spec=pltpu.PrefetchScalarGridSpec(num_scalar_pr...  207 us
    ppermute x77, waiting for transfers between devices, send(): return lax.ppermute(values, 'dp', self.pairs[direction])  154 us
    ppermute x77, starting transfers between devices, send(): return lax.ppermute(values, 'dp', self.pairs[direction])  80.3 us
    dot_general x3, matrix products, product(): lax.dot_general(left, right, (((left_dim,), (right_dim,)), ((), ())), pre...  28 us
    pallas_call x2, Pallas kernels, attend_backward(): pl.pallas_call(functools.partial(backward_body, length // count, count, l...  23.3 us
    unnamed x170, local copies, waits for them, and re-layouts  19.2 us
    pallas_call x1, Pallas kernels, attend_forward(): pl.pallas_call(functools.partial(forward_body, length // count, count), g...  15.1 us
    reduce_scatter x3, waiting for transfers between devices, scatter(): return lax.psum_scatter(values, 'tensor', scatter_dimension=0, tiled=True)  14.5 us
  transfers between devices with their start and end apart: 94, of which 37 were waited for; matrix products, arithmetic and copies ran while one was open for 8% of the time, Pallas kernels for 40%

profile of v5, /device:TPU:0, one launch (start us, length us, event | category | flops | bytes accessed | tf_op | source)
XLA Modules:
  0.0 599.5 jit_solution(5542479837648562385)
XLA Ops:
  24.4 7.9 %collective-permute-done.3.refs_7_ = bf16[256,1024]{1,0:T(8,128)(2,1)} collective-permute-done((bf16[256,1024]{1,0:T(8,128)(2,1)}, bf16[256,1024]{1,0:T(8,128)(2,1)}, u32[]{:S(2)}, u32[]{:S(2)}) %collective-permute-start.3) | collective-permute-done | bytes 524320 | tf_op jit(solution)/shard_map/ppermute | solution.py:917
  36.2 8.1 %collective-permute-done.5.refs_7_.refs_15_.refs_8_ = bf16[272,1024]{1,0:T(8,128)(2,1)} collective-permute-done((bf16[272,1024]{1,0:T(8,128)(2,1)}, bf16[272,1024]{1,0:T(8,128)(2,1)}, u32[]{:S(2)}, u32[]{:S(2)}) %collective-permute-start.5) | collective-permute-done | bytes 557088 | tf_op jit(solution)/shard_map/ppermute | solution.py:917
  48.1 7.3 %collective-permute-done.7.refs_6_ = bf16[256,1024]{1,0:T(8,128)(2,1)S(1)} collective-permute-done((bf16[256,1024]{1,0:T(8,128)(2,1)}, bf16[256,1024]{1,0:T(8,128)(2,1)S(1)}, u32[]{:S(2)}, u32[]{:S(2)}) %collective-permute-start.7) | collective-permute-done | bytes 524320 | tf_op jit(solution)/shard_map/ppermute | solution.py:917
  76.0 7.1 %collective-permute-done.11.refs_5_ = bf16[256,1024]{1,0:T(8,128)(2,1)S(1)} collective-permute-done((bf16[256,1024]{1,0:T(8,128)(2,1)S(1)}, bf16[256,1024]{1,0:T(8,128)(2,1)S(1)}, u32[]{:S(2)}, u32[]{:S(2)}) %collective-permute-start.11) | collective-permute-done | bytes 524320 | tf_op jit(solution)/shard_map/ppermute | solution.py:917
  86.3 8.8 %collective-permute-done.13.refs_5_.refs_13_.refs_6_ = bf16[272,1024]{1,0:T(8,128)(2,1)S(1)} collective-permute-done((bf16[272,1024]{1,0:T(8,128)(2,1)S(1)}, bf16[272,1024]{1,0:T(8,128)(2,1)S(1)}, u32[]{:S(2)}, u32[]{:S(2)}) %collective-permute-start.13) | collective-permute-done | bytes 557088 | tf_op jit(solution)/shard_map/ppermute | solution.py:917
  97.3 7.2 %collective-permute-done.15.refs_4_ = bf16[256,1024]{1,0:T(8,128)(2,1)} collective-permute-done((bf16[256,1024]{1,0:T(8,128)(2,1)S(1)}, bf16[256,1024]{1,0:T(8,128)(2,1)}, u32[]{:S(2)}, u32[]{:S(2)}) %collective-permute-start.15) | collective-permute-done | bytes 524320 | tf_op jit(solution)/shard_map/ppermute | solution.py:917
  114.1 14.6 %project_qkv.1 = (bf16[1024,1024]{1,0:T(8,128)(2,1)}, bf16[1024,512]{1,0:T(8,128)(2,1)}, bf16[1024,2048]{1,0:T(8,128)(2,1)}) custom-call(bf16[1024,2048]{1,0:T(8,128)(2,1)} %all-gather.5.cloned.1.call-done.x_ref, f32[4,2048]{1,0:T(4,128)} %copy-done.18, f32[1,1536]{1,0:T(1,128)} %copy-done.22, f32[1024,1]{1,0:T(8,128)} %copy-done.12, f32[1024,1]{1,0:T(8,128)} %copy-done.13, ...), custom_call_target="tpu_custom_call" | custom-call | flops 1000000000 | bytes 1 | tf_op jit(solution)/shard_map/project_qkv/pallas_call | solution.py:226
  134.3 15.1 %attend_forward.1 = (bf16[1024,512]{1,0:T(8,128)(2,1)}, f32[4,2,1024]{2,1,0:T(2,128)}) custom-call(bf16[1024,1024]{1,0:T(8,128)(2,1)} %get-tuple-element.515.q_ref.k_ref, bf16[1024,1024]{1,0:T(8,128)(2,1)} %get-tuple-element.515.q_ref.k_ref, bf16[1024,512]{1,0:T(8,128)(2,1)} %get-tuple-element.516.v_ref, s32[1024,1]{1,0:T(8,128)} %copy.53.down_ref, ...), custom_call_target="tpu_custom_call" | custom-call | flops 1000000000 | bytes 1 | tf_op jit(solution)/shard_map/attend_forward/pallas_call | solution.py:79
  152.9 6.7 %from_heads.1 = bf16[1024,2048]{1,0:T(8,128)(2,1)} custom-call(bf16[1024,512]{1,0:T(8,128)(2,1)} %get-tuple-element.530.refs_0_.mixed_ref.refs_3_, bf16[272,1024]{1,0:T(8,128)(2,1)} %fusion.4.refs_0_.refs_8_.refs_1_, bf16[272,1024]{1,0:T(8,128)(2,1)} %collective-permute-done.6.refs_1_.refs_9_.refs_2_, bf16[272,1024]{1,0:T(8,128)(2,1)} %copy-done.3, ...), custom_call_target="tpu_custom_call" | custom-call | flops 1000000000 | bytes 1 | tf_op jit(solution)/shard_map/from_heads/pallas_call | solution.py:226
  159.7 7.8 %collective-permute-done.23.refs_14_.refs_17_ = bf16[256,1408]{1,0:T(8,128)(2,1)S(1)} collective-permute-done((bf16[256,1408]{1,0:T(8,128)(2,1)}, bf16[256,1408]{1,0:T(8,128)(2,1)S(1)}, u32[]{:S(2)}, u32[]{:S(2)}) %collective-permute-start.23) | collective-permute-done | bytes 720928 | tf_op jit(solution)/shard_map/ppermute | solution.py:917
  173.0 15.3 %collective-permute-done.25.refs_5_.refs_8_ = bf16[256,1408]{1,0:T(8,128)(2,1)} collective-permute-done((bf16[256,1408]{1,0:T(8,128)(2,1)}, bf16[256,1408]{1,0:T(8,128)(2,1)}, u32[]{:S(2)}, u32[]{:S(2)}) %collective-permute-start.25) | collective-permute-done | bytes 720928 | tf_op jit(solution)/shard_map/ppermute | solution.py:917
  189.9 14.5 %reduce-scatter.4.cloned.1.call-done.term_ref = bf16[256,2048]{1,0:T(8,128)(2,1)} async-done(((bf16[1024,2048]{1,0:T(8,128)(2,1)}), bf16[256,2048]{1,0:T(8,128)(2,1)}) %reduce-scatter.4.cloned.1.call-update) | async-done | bytes 1048592 | tf_op jit(solution)/shard_map/reduce_scatter | solution.py:1083
  212.6 14.8 %collective-permute-done.29.refs_4_.refs_7_ = bf16[256,1408]{1,0:T(8,128)(2,1)} collective-permute-done((bf16[256,1408]{1,0:T(8,128)(2,1)}, bf16[256,1408]{1,0:T(8,128)(2,1)}, u32[]{:S(2)}, u32[]{:S(2)}) %collective-permute-start.29) | collective-permute-done | bytes 720928 | tf_op jit(solution)/shard_map/ppermute | solution.py:917
  246.4 12.7 %gated_forward.2 = (bf16[1024,1408]{1,0:T(8,128)(2,1)}, bf16[1024,1408]{1,0:T(8,128)(2,1)}, bf16[1024,1408]{1,0:T(8,128)(2,1)}) custom-call(bf16[1024,2048]{1,0:T(8,128)(2,1)} %all-gather.9.cloned.1.call-done.x_ref, bf16[256,1408]{1,0:T(8,128)(2,1)} %refs_3_, bf16[256,1408]{1,0:T(8,128)(2,1)} %collective-permute-done.18.refs_1_.refs_4_, ...), custom_call_target="tpu_custom_call" | custom-call | flops 1000000000 | bytes 1 | tf_op jit(solution)/shard_map/gated_forward/pallas_call | solution.py:226
  263.4 12.7 %gated_forward.3 = (bf16[1024,1408]{1,0:T(8,128)(2,1)}, bf16[1024,1408]{1,0:T(8,128)(2,1)}, bf16[1024,1408]{1,0:T(8,128)(2,1)}) custom-call(bf16[1024,2048]{1,0:T(8,128)(2,1)} %all-gather.9.cloned.1.call-done.x_ref, bf16[256,1408]{1,0:T(8,128)(2,1)} %refs_3_, ...), custom_call_target="tpu_custom_call", output_to_operand_aliasing={{0}: (17, {}), {1}: (18, {}), {2}: (19, {})} | custom-call | flops 1000000000 | bytes 1 | tf_op jit(solution)/shard_map/gated_forward/pallas_call | solution.py:226
  279.8 8.6 %convolution_convert_fusion.2.refs_0_.refs_1_.refs_2_.refs_3_ = bf16[2048,1408]{1,0:T(8,128)(2,1)} fusion(bf16[1024,2048]{1,0:T(8,128)(2,1)S(1)} %copy-done.28, bf16[1024,1408]{1,0:T(8,128)(2,1)S(1)} %copy-done.24), kind=kOutput, calls=%fused_computation.3 | convolution fusion | flops 5908463616 | bytes 12845056 | tf_op jit(solution)/shard_map/dot_general | solution.py:23
  292.9 13.7 %gated_backward.1 = (bf16[1024,1408]{1,0:T(8,128)(2,1)}, bf16[1024,1408]{1,0:T(8,128)(2,1)}) custom-call(bf16[1024,2048]{1,0:T(8,128)(2,1)} %all-gather.7.cloned.1.call-done.refs_0_, bf16[1024,1408]{1,0:T(8,128)(2,1)} %get-tuple-element.605.refs_1_, bf16[1024,1408]{1,0:T(8,128)(2,1)} %get-tuple-element.606.refs_2_, ...), custom_call_target="tpu_custom_call" | custom-call | flops 1000000000 | bytes 1 | tf_op jit(solution)/shard_map/gated_backward/pallas_call | solution.py:226
  313.5 10.8 %convolution_convert_fusion.1.refs_0_.refs_1_.refs_2_.refs_3_ = bf16[2048,1408]{1,0:T(8,128)(2,1)} fusion(bf16[1024,2048]{1,0:T(8,128)(2,1)} %all-gather.9.cloned.1.call-done.x_ref, bf16[1024,1408]{1,0:T(8,128)(2,1)S(1)} %copy-done.32), kind=kOutput, calls=%fused_computation.2 | convolution fusion | flops 5908463616 | bytes 12845056 | tf_op jit(solution)/shard_map/dot_general | solution.py:23
  328.8 20.1 %from_gates.1 = (bf16[512,2048]{1,0:T(8,128)(2,1)}, bf16[512,2048]{1,0:T(8,128)(2,1)}) custom-call(s32[1]{0:T(128)} %bitcast.13.refs_0_, bf16[1024,1408]{1,0:T(8,128)(2,1)} %get-tuple-element.626.refs_1_, bf16[1024,1408]{1,0:T(8,128)(2,1)} %get-tuple-element.655.refs_2_, bf16[256,1408]{1,0:T(8,128)(2,1)} %refs_3_, ...), custom_call_target="tpu_custom_call" | custom-call | flops 1000000000 | bytes 1 | tf_op jit(solution)/shard_map/from_gates/pallas_call | solution.py:226
  364.3 8.6 %convolution_convert_fusion.refs_0_.refs_1_.refs_2_.refs_3_ = bf16[2048,1408]{1,0:T(8,128)(2,1)} fusion(bf16[1024,2048]{1,0:T(8,128)(2,1)S(1)} %copy-done.23, bf16[1024,1408]{1,0:T(8,128)(2,1)S(1)} %copy-done.31), kind=kOutput, calls=%fused_computation.1 | convolution fusion | flops 5908463616 | bytes 12845056 | tf_op jit(solution)/shard_map/dot_general | solution.py:23
  379.7 7.7 %collective-permute-done.54.refs_0_ = bf16[256,1408]{1,0:T(8,128)(2,1)} collective-permute-done((bf16[256,1408]{1,0:T(8,128)(2,1)}, bf16[256,1408]{1,0:T(8,128)(2,1)}, u32[]{:S(2)}, u32[]{:S(2)}) %collective-permute-start.54) | collective-permute-done | bytes 720928 | tf_op jit(solution)/shard_map/ppermute | solution.py:917
  388.3 6.0 second_norm_back.1
  399.1 12.1 %from_hidden.1 = bf16[1024,2048]{1,0:T(8,128)(2,1)} custom-call(bf16[1024,1408]{1,0:T(8,128)(2,1)} %get-tuple-element.682.refs_0_, bf16[128,1408]{1,0:T(8,128)(2,1)} %get-tuple-element.547.refs_3_.refs_1_, bf16[128,1408]{1,0:T(8,128)(2,1)} %get-tuple-element.549.refs_4_.refs_2_, bf16[128,1408]{1,0:T(8,128)(2,1)} %copy-done.38, bf16[128,1408]{1,0:T(8,128)(2,1)} %copy-done.40, ...), custom_call_target="tpu_custom_call" | custom-call | flops 1000000000 | bytes 1 | tf_op jit(solution)/shard_map/from_hidden/pallas_call | solution.py:226
  421.7 10.7 %collective-permute-done.60.refs_0_ = bf16[256,1408]{1,0:T(8,128)(2,1)S(1)} collective-permute-done((bf16[256,1408]{1,0:T(8,128)(2,1)}, bf16[256,1408]{1,0:T(8,128)(2,1)S(1)}, u32[]{:S(2)}, u32[]{:S(2)}) %collective-permute-start.60) | collective-permute-done | bytes 720928 | tf_op jit(solution)/shard_map/ppermute | solution.py:917
  432.6 7.5 %through_out.1.grad_ref = bf16[1024,512]{1,0:T(8,128)(2,1)} custom-call(bf16[1024,2048]{1,0:T(8,128)(2,1)} %all-gather.11.cloned.1.call-done.rows_ref.refs_2_, bf16[272,1024]{1,0:T(8,128)(2,1)} %fusion.4.refs_0_.refs_8_.refs_1_, bf16[272,1024]{1,0:T(8,128)(2,1)} %collective-permute-done.6.refs_1_.refs_9_.refs_2_, bf16[272,1024]{1,0:T(8,128)(2,1)} %copy-done.3, ...), custom_call_target="tpu_custom_call" | custom-call | flops 1000000000 | bytes 1 | tf_op jit(solution)/shard_map/through_out/pallas_call | solution.py:226
  445.1 11.6 %attend_backward.2 = (bf16[1024,512]{1,0:T(8,128)(2,1)}, bf16[1024,512]{1,0:T(8,128)(2,1)}, bf16[1024,512]{1,0:T(8,128)(2,1)}, f32[4,3,128]{2,1,0:T(4,128)}) custom-call(bf16[1024,1024]{1,0:T(8,128)(2,1)} %get-tuple-element.515.q_ref.k_ref, bf16[1024,1024]{1,0:T(8,128)(2,1)} %get-tuple-element.515.q_ref.k_ref, bf16[1024,512]{1,0:T(8,128)(2,1)} %get-tuple-element.516.v_ref, ...), custom_call_target="tpu_custom_call" | custom-call | flops 999999995904 | bytes 1 | tf_op jit(solution)/shard_map/attend_backward/pallas_call | solution.py:177
  466.4 11.7 %attend_backward.3 = (bf16[1024,512]{1,0:T(8,128)(2,1)}, bf16[1024,512]{1,0:T(8,128)(2,1)}, bf16[1024,512]{1,0:T(8,128)(2,1)}, f32[4,3,128]{2,1,0:T(4,128)}) custom-call(bf16[1024,1024]{1,0:T(8,128)(2,1)} %get-tuple-element.515.q_ref.k_ref, ...), custom_call_target="tpu_custom_call", output_to_operand_aliasing={{0}: (10, {}), {1}: (11, {}), {2}: (12, {}), {3}: (13, {})} | custom-call | flops 999999995904 | bytes 1 | tf_op jit(solution)/shard_map/attend_backward/pallas_call | solution.py:177
  485.3 9.2 %over_tokens.2.refs_0_.refs_1_.refs_2_.refs_3_ = bf16[2048,1024]{1,0:T(8,128)(2,1)} custom-call(bf16[1024,2048]{1,0:T(8,128)(2,1)} %get-tuple-element.733.refs_0_.refs_2_, bf16[1024,512]{1,0:T(8,128)(2,1)} %get-tuple-element.756.refs_1_.q_ref, bf16[1024,2048]{1,0:T(8,128)(2,1)} %get-tuple-element.733.refs_0_.refs_2_, ...), custom_call_target="tpu_custom_call" | custom-call | flops 1000000000 | bytes 1 | tf_op jit(solution)/shard_map/over_tokens/pallas_call | solution.py:226
  498.6 9.2 %over_tokens.3.refs_0_.refs_1_.refs_2_.refs_3_ = bf16[2048,1024]{1,0:T(8,128)(2,1)} custom-call(bf16[1024,2048]{1,0:T(8,128)(2,1)} %get-tuple-element.733.refs_0_.refs_2_, bf16[1024,512]{1,0:T(8,128)(2,1)} %get-tuple-element.742.refs_1_.v_ref, bf16[1024,2048]{1,0:T(8,128)(2,1)} %all-gather.11.cloned.1.call-done.rows_ref.refs_2_, ...), custom_call_target="tpu_custom_call" | custom-call | flops 1000000000 | bytes 1 | tf_op jit(solution)/shard_map/over_tokens/pallas_call | solution.py:226
  518.4 13.0 %through_heads.1 = (bf16[1024,2048]{1,0:T(8,128)(2,1)}, f32[2,2048]{1,0:T(2,128)}) custom-call(bf16[1024,512]{1,0:T(8,128)(2,1)} %get-tuple-element.756.refs_1_.q_ref, bf16[1024,512]{1,0:T(8,128)(2,1)} %get-tuple-element.735.refs_3_.k_ref, bf16[1024,512]{1,0:T(8,128)(2,1)} %get-tuple-element.742.refs_1_.v_ref, ...), custom_call_target="tpu_custom_call" | custom-call | flops 1000000000 | bytes 1 | tf_op jit(solution)/shard_map/through_heads/pallas_call | solution.py:226
  547.4 5.8 collective-permute-done.77
  574.2 6.4 %collective-permute-done.84 = bf16[256,1024]{1,0:T(8,128)(2,1)S(1)} collective-permute-done((bf16[256,1024]{1,0:T(8,128)(2,1)}, bf16[256,1024]{1,0:T(8,128)(2,1)S(1)}, u32[]{:S(2)}, u32[]{:S(2)}) %collective-permute-start.84) | collective-permute-done | bytes 524320 | tf_op jit(solution)/shard_map/ppermute | solution.py:917
  (468 shorter events, 250.5 us)
Async XLA Ops:
  7.2 50.0 %all-gather.5.cloned.1.call-start = ((), (), s32[]{:S(2)}) async-start(), calls=%async_computation.3 | async-start | bytes 5242880 | tf_op jit(solution)/shard_map/all_gather | solution.py:1080
  14.9 117.3 %all-gather.7.cloned.1.call-start = ((), (), s32[]{:S(2)}) async-start(), calls=%async_computation.4 | async-start | bytes 5242880 | tf_op jit(solution)/shard_map/all_gather | solution.py:1080
  19.3 25.0 %collective-permute-start.5 = (bf16[272,1024]{1,0:T(8,128)(2,1)}, bf16[272,1024]{1,0:T(8,128)(2,1)}, u32[]{:S(2)}, u32[]{:S(2)}) collective-permute-start(bf16[272,1024]{1,0:T(8,128)(2,1)} %fusion.4.refs_0_.refs_8_.refs_1_), channel_id=1, source_target_pairs={{0,8},{8,16},{16,24},{24,28},{28,20},{20,12},{12,4},{4,0},{1,9},{9... | collective-permute-start | bytes 1671176 | tf_op jit(solution)/shard_map/ppermute | solution.py:917
  21.1 25.0 %collective-permute-start.6 = (bf16[272,1024]{1,0:T(8,128)(2,1)}, bf16[272,1024]{1,0:T(8,128)(2,1)}, u32[]{:S(2)}, u32[]{:S(2)}) collective-permute-start(bf16[272,1024]{1,0:T(8,128)(2,1)} %fusion.4.refs_0_.refs_8_.refs_1_), channel_id=1, source_target_pairs={{8,0},{16,8},{24,16},{28,24},{20,28},{12,20},{4,12},{0,4},{9,1},{1... | collective-permute-start | bytes 1671176 | tf_op jit(solution)/shard_map/ppermute | solution.py:917
  70.8 24.2 %collective-permute-start.13 = (bf16[272,1024]{1,0:T(8,128)(2,1)S(1)}, bf16[272,1024]{1,0:T(8,128)(2,1)S(1)}, u32[]{:S(2)}, u32[]{:S(2)}) collective-permute-start(bf16[272,1024]{1,0:T(8,128)(2,1)S(1)} %collective-permute-done.9.refs_6_.refs_14_.refs_7_), channel_id=1, source_target_pairs={{0,8},{8,16},{16,24},{24,28},{28,20},{20,12},{12,4},{4,0},{1,9},{9... | collective-permute-start | bytes 1671176 | tf_op jit(solution)/shard_map/ppermute | solution.py:917
  72.5 23.4 %collective-permute-start.14 = (bf16[272,1024]{1,0:T(8,128)(2,1)S(1)}, bf16[272,1024]{1,0:T(8,128)(2,1)S(1)}, u32[]{:S(2)}, u32[]{:S(2)}) collective-permute-start(bf16[272,1024]{1,0:T(8,128)(2,1)S(1)} %collective-permute-done.10.refs_2_.refs_10_.refs_3_), channel_id=1, source_target_pairs={{8,0},{16,8},{24,16},{28,24},{20,28},{12,20},{4,12},{0,4},{9,1},{1... | collective-permute-start | bytes 1671176 | tf_op jit(solution)/shard_map/ppermute | solution.py:917
  96.3 108.1 %reduce-scatter.4.cloned.1.call-start = ((), (), s32[]{:S(2)}) async-start(), calls=%async_computation.5 | async-start | bytes 5242880 | tf_op jit(solution)/shard_map/reduce_scatter | solution.py:1083
  104.6 24.2 %collective-permute-start.17 = (bf16[256,1408]{1,0:T(8,128)(2,1)}, bf16[256,1408]{1,0:T(8,128)(2,1)}, u32[]{:S(2)}, u32[]{:S(2)}) collective-permute-start(bf16[256,1408]{1,0:T(8,128)(2,1)} %refs_3_), channel_id=1, source_target_pairs={{0,8},{8,16},{16,24},{24,28},{28,20},{20,12},{12,4},{4,0},{1,9},{9... | collective-permute-start | bytes 2162696 | tf_op jit(solution)/shard_map/ppermute | solution.py:917
  106.2 22.6 %collective-permute-start.18 = (bf16[256,1408]{1,0:T(8,128)(2,1)}, bf16[256,1408]{1,0:T(8,128)(2,1)}, u32[]{:S(2)}, u32[]{:S(2)}) collective-permute-start(bf16[256,1408]{1,0:T(8,128)(2,1)} %refs_3_), channel_id=1, source_target_pairs={{8,0},{16,8},{24,16},{28,24},{20,28},{12,20},{4,12},{0,4},{9,1},{1... | collective-permute-start | bytes 2162696 | tf_op jit(solution)/shard_map/ppermute | solution.py:917
  107.9 41.4 %collective-permute-start.19 = (bf16[256,1408]{1,0:T(8,128)(2,1)}, bf16[256,1408]{1,0:T(8,128)(2,1)}, u32[]{:S(2)}, u32[]{:S(2)}) collective-permute-start(bf16[256,1408]{1,0:T(8,128)(2,1)} %refs_11_), channel_id=1, source_target_pairs={{0,8},{8,16},{16,24},{24,28},{28,20},{20,12},{12,4},{4,0},{1,9},{9... | collective-permute-start | bytes 2162696 | tf_op jit(solution)/shard_map/ppermute | solution.py:917
  109.5 39.9 %collective-permute-start.20 = (bf16[256,1408]{1,0:T(8,128)(2,1)}, bf16[256,1408]{1,0:T(8,128)(2,1)}, u32[]{:S(2)}, u32[]{:S(2)}) collective-permute-start(bf16[256,1408]{1,0:T(8,128)(2,1)} %refs_11_), channel_id=1, source_target_pairs={{8,0},{16,8},{24,16},{28,24},{20,28},{12,20},{4,12},{0,4},{9,1},{1... | collective-permute-start | bytes 2162696 | tf_op jit(solution)/shard_map/ppermute | solution.py:917
  132.3 27.4 %collective-permute-start.21 = (bf16[256,1408]{1,0:T(8,128)(2,1)}, bf16[256,1408]{1,0:T(8,128)(2,1)}, u32[]{:S(2)}, u32[]{:S(2)}) collective-permute-start(bf16[256,1408]{1,0:T(8,128)(2,1)} %collective-permute-done.17.refs_7_.refs_10_), channel_id=1, source_target_pairs={{0,8},{8,16},{16,24},{24,28},{28,20},{20,12},{12,4},{4,0},{1,9},{9... | collective-permute-start | bytes 2162696 | tf_op jit(solution)/shard_map/ppermute | solution.py:917
  133.8 26.0 %collective-permute-start.22 = (bf16[256,1408]{1,0:T(8,128)(2,1)}, bf16[256,1408]{1,0:T(8,128)(2,1)}, u32[]{:S(2)}, u32[]{:S(2)}) collective-permute-start(bf16[256,1408]{1,0:T(8,128)(2,1)} %collective-permute-done.18.refs_1_.refs_4_), channel_id=1, source_target_pairs={{8,0},{16,8},{24,16},{28,24},{20,28},{12,20},{4,12},{0,4},{9,1},{1... | collective-permute-start | bytes 2162696 | tf_op jit(solution)/shard_map/ppermute | solution.py:917
  159.7 84.8 %all-gather.9.cloned.1.call-start = ((), (), s32[]{:S(2)}) async-start(), calls=%async_computation.6 | async-start | bytes 5242880 | tf_op jit(solution)/shard_map/all_gather | solution.py:1080
  170.9 38.7 %collective-permute-start.27 = (bf16[256,1408]{1,0:T(8,128)(2,1)}, bf16[256,1408]{1,0:T(8,128)(2,1)}, u32[]{:S(2)}, u32[]{:S(2)}) collective-permute-start(bf16[256,1408]{1,0:T(8,128)(2,1)} %copy-done.25), channel_id=1, source_target_pairs={{0,8},{8,16},{16,24},{24,28},{28,20},{20,12},{12,4},{4,0},{1,9},{9... | collective-permute-start | bytes 2162696 | tf_op jit(solution)/shard_map/ppermute | solution.py:917
  172.5 37.1 %collective-permute-start.28 = (bf16[256,1408]{1,0:T(8,128)(2,1)}, bf16[256,1408]{1,0:T(8,128)(2,1)}, u32[]{:S(2)}, u32[]{:S(2)}) collective-permute-start(bf16[256,1408]{1,0:T(8,128)(2,1)} %copy-done.26), channel_id=1, source_target_pairs={{8,0},{16,8},{24,16},{28,24},{20,28},{12,20},{4,12},{0,4},{9,1},{1... | collective-permute-start | bytes 2162696 | tf_op jit(solution)/shard_map/ppermute | solution.py:917
  209.5 223.0 %all-gather.11.cloned.1.call-start = ((), (), s32[]{:S(2)}) async-start(), calls=%async_computation.7 | async-start | bytes 5242880 | tf_op jit(solution)/shard_map/all_gather | solution.py:1080
  210.6 24.4 %collective-permute-start.31 = (bf16[128,1408]{1,0:T(8,128)(2,1)S(1)}, bf16[128,1408]{1,0:T(8,128)(2,1)S(1)}, u32[]{:S(2)}, u32[]{:S(2)}) collective-permute-start(bf16[128,1408]{1,0:T(8,128)(2,1)S(1)} %copy-done.30), channel_id=1, source_target_pairs={{0,8},{8,16},{16,24},{24,28},{28,20},{20,12},{12,4},{4,0},{1,9},{9... | collective-permute-start | bytes 1081352 | tf_op jit(solution)/shard_map/ppermute | solution.py:917
  212.1 24.6 %collective-permute-start.32 = (bf16[128,1408]{1,0:T(8,128)(2,1)S(1)}, bf16[128,1408]{1,0:T(8,128)(2,1)S(1)}, u32[]{:S(2)}, u32[]{:S(2)}) collective-permute-start(bf16[128,1408]{1,0:T(8,128)(2,1)S(1)} %copy-done.30), channel_id=1, source_target_pairs={{8,0},{16,8},{24,16},{28,24},{20,28},{12,20},{4,12},{0,4},{9,1},{1... | collective-permute-start | bytes 1081352 | tf_op jit(solution)/shard_map/ppermute | solution.py:917
  236.7 22.5 %collective-permute-start.35 = (bf16[128,1408]{1,0:T(8,128)(2,1)S(1)}, bf16[128,1408]{1,0:T(8,128)(2,1)S(1)}, u32[]{:S(2)}, u32[]{:S(2)}) collective-permute-start(bf16[128,1408]{1,0:T(8,128)(2,1)S(1)} %collective-permute-done.31.refs_17_.refs_15_), channel_id=1, source_target_pairs={{0,8},{8,16},{16,24},{24,28},{28,20},{20,12},{12,4},{4,0},{1,9},{9... | collective-permute-start | bytes 1081352 | tf_op jit(solution)/shard_map/ppermute | solution.py:917
  311.5 37.4 %collective-permute-start.47 = (bf16[256,1408]{1,0:T(8,128)(2,1)}, bf16[256,1408]{1,0:T(8,128)(2,1)S(1)}, u32[]{:S(2)}, u32[]{:S(2)}) collective-permute-start(bf16[256,1408]{1,0:T(8,128)(2,1)} %get-tuple-element.624), channel_id=1, source_target_pairs={{0,8},{8,16},{16,24},{24,28},{28,20},{20,12},{12,4},{4,0},{1,9},{9... | collective-permute-start | bytes 2162696 | tf_op jit(solution)/shard_map/ppermute | solution.py:917
  313.0 36.0 %collective-permute-start.48 = (bf16[256,1408]{1,0:T(8,128)(2,1)}, bf16[256,1408]{1,0:T(8,128)(2,1)}, u32[]{:S(2)}, u32[]{:S(2)}) collective-permute-start(bf16[256,1408]{1,0:T(8,128)(2,1)} %get-tuple-element.625), channel_id=1, source_target_pairs={{8,0},{16,8},{24,16},{28,24},{20,28},{12,20},{4,12},{0,4},{9,1},{1... | collective-permute-start | bytes 2162696 | tf_op jit(solution)/shard_map/ppermute | solution.py:917
  357.4 30.0 %collective-permute-start.54 = (bf16[256,1408]{1,0:T(8,128)(2,1)}, bf16[256,1408]{1,0:T(8,128)(2,1)}, u32[]{:S(2)}, u32[]{:S(2)}) collective-permute-start(bf16[256,1408]{1,0:T(8,128)(2,1)} %get-tuple-element.662), channel_id=1, source_target_pairs={{0,8},{8,16},{16,24},{24,28},{28,20},{20,12},{12,4},{4,0},{1,9},{9... | collective-permute-start | bytes 2162696 | tf_op jit(solution)/shard_map/ppermute | solution.py:917
  358.9 28.5 %collective-permute-start.55 = (bf16[256,1408]{1,0:T(8,128)(2,1)}, bf16[256,1408]{1,0:T(8,128)(2,1)}, u32[]{:S(2)}, u32[]{:S(2)}) collective-permute-start(bf16[256,1408]{1,0:T(8,128)(2,1)} %get-tuple-element.663), channel_id=1, source_target_pairs={{8,0},{16,8},{24,16},{28,24},{20,28},{12,20},{4,12},{0,4},{9,1},{1... | collective-permute-start | bytes 2162696 | tf_op jit(solution)/shard_map/ppermute | solution.py:917
  361.6 25.7 %collective-permute-start.56 = (bf16[256,2048]{1,0:T(8,128)(2,1)S(1)}, bf16[256,2048]{1,0:T(8,128)(2,1)S(1)}, u32[]{:S(2)}, u32[]{:S(2)}) collective-permute-start(bf16[256,2048]{1,0:T(8,128)(2,1)S(1)} %get-tuple-element.664), channel_id=1, source_target_pairs={{0,2},{1,3},{2,0},{3,1},{4,6},{5,7},{6,4},{7,5},{8,10},{9,11},{10,... | collective-permute-start | bytes 3145736 | tf_op jit(solution)/shard_map/ppermute | solution.py:1036
  375.9 35.4 %collective-permute-start.57 = (bf16[256,1408]{1,0:T(8,128)(2,1)}, bf16[256,1408]{1,0:T(8,128)(2,1)}, u32[]{:S(2)}, u32[]{:S(2)}) collective-permute-start(bf16[256,1408]{1,0:T(8,128)(2,1)} %hand_on.25), channel_id=1, source_target_pairs={{0,8},{8,16},{16,24},{24,28},{28,20},{20,12},{12,4},{4,0},{1,9},{9... | collective-permute-start | bytes 2162696 | tf_op jit(solution)/shard_map/ppermute | solution.py:917
  394.3 115.9 %reduce-scatter.6.cloned.1.call-start = ((), (), s32[]{:S(2)}) async-start(), calls=%async_computation.8 | async-start | bytes 5242880 | tf_op jit(solution)/shard_map/reduce_scatter | solution.py:1083
  421.2 35.5 %collective-permute-start.62 = (bf16[256,1408]{1,0:T(8,128)(2,1)}, bf16[256,1408]{1,0:T(8,128)(2,1)}, u32[]{:S(2)}, u32[]{:S(2)}) collective-permute-start(bf16[256,1408]{1,0:T(8,128)(2,1)} %hand_on.28), channel_id=1, source_target_pairs={{8,0},{16,8},{24,16},{28,24},{20,28},{12,20},{4,12},{0,4},{9,1},{1... | collective-permute-start | bytes 2162696 | tf_op jit(solution)/shard_map/ppermute | solution.py:917
  456.7 126.3 %reduce-scatter.8.cloned.1.call-start = ((), (), s32[]{:S(2)}) async-start(), calls=%async_computation.9 | async-start | bytes 5242880 | tf_op jit(solution)/shard_map/reduce_scatter | solution.py:1083
  483.7 24.1 %collective-permute-start.67 = (bf16[256,1408]{1,0:T(8,128)(2,1)}, bf16[256,1408]{1,0:T(8,128)(2,1)S(1)}, u32[]{:S(2)}, u32[]{:S(2)}) collective-permute-start(bf16[256,1408]{1,0:T(8,128)(2,1)} %hand_on.32), channel_id=1, source_target_pairs={{0,8},{8,16},{16,24},{24,28},{28,20},{20,12},{12,4},{4,0},{1,9},{9... | collective-permute-start | bytes 2162696 | tf_op jit(solution)/shard_map/ppermute | solution.py:917
  516.1 24.9 %collective-permute-start.72 = (bf16[256,1024]{1,0:T(8,128)(2,1)}, bf16[256,1024]{1,0:T(8,128)(2,1)}, u32[]{:S(2)}, u32[]{:S(2)}) collective-permute-start(bf16[256,1024]{1,0:T(8,128)(2,1)} %get-tuple-element.768), channel_id=1, source_target_pairs={{0,8},{8,16},{16,24},{24,28},{28,20},{20,12},{12,4},{4,0},{1,9},{9... | collective-permute-start | bytes 1572872 | tf_op jit(solution)/shard_map/ppermute | solution.py:917
  517.9 23.1 %collective-permute-start.73 = (bf16[256,1024]{1,0:T(8,128)(2,1)}, bf16[256,1024]{1,0:T(8,128)(2,1)}, u32[]{:S(2)}, u32[]{:S(2)}) collective-permute-start(bf16[256,1024]{1,0:T(8,128)(2,1)} %get-tuple-element.769), channel_id=1, source_target_pairs={{8,0},{16,8},{24,16},{28,24},{20,28},{12,20},{4,12},{0,4},{9,1},{1... | collective-permute-start | bytes 1572872 | tf_op jit(solution)/shard_map/ppermute | solution.py:917
  (145 other events, 1601.0 us)
Sparse Core Ops, SparseCore 0:
  15.1 35.9 all-gather.4
  96.4 35.8 all-gather.6
  159.8 44.5 reduce-scatter.3
  209.7 33.5 all-gather.8
  394.5 33.5 all-gather.10
  456.8 43.6 reduce-scatter.5
  531.5 42.6 reduce-scatter.7
